TPU v7x, 32 devices: a whole 2x2x4 slice. The times are simulated.
32 devices in a mesh: dp: 8 (over z, x), head: 4 (over y, core).
Axes of the slice: x: 2, y: 2, z: 4, core: 2. Of those that a mesh axis runs over, the one named last changes fastest.
Arguments:
- tokens: bfloat16 [4096, 768], P(('dp', 'head')), may hold values from -6 to 6
- segments: int32 [8, 512], P('dp'), may hold values from 0 to 3, never falling along the last dimension, each value on 1 to 256 neighbouring positions
- routes: int32 [4096, 1], P(('dp', 'head')), may hold values from 0 to 1; in each aligned block of 128 rows (0 to 127, 128 to 255, ...) at most 96 rows name the same one
- norm_gain: bfloat16 [2, 2, 2, 768], P(None, None, None, 'dp'), may hold values from 0.25 to 1.75
- norm_bias: bfloat16 [2, 2, 2, 768], P(None, None, None, 'dp'), may hold values from -3 to 3
- w_qkv: bfloat16 [2, 768, 2304], P(None, 'dp'), may hold values from -0.21875 to 0.21875
- w_out: bfloat16 [2, 768, 768], P(None, 'dp'), may hold values from -0.625 to 0.625
- w_up: bfloat16 [2, 2, 768, 3072], P(None, None, 'dp'), may hold values from -0.21875 to 0.21875
- w_down: bfloat16 [2, 2, 3072, 768], P(None, None, 'dp'), may hold values from -0.15625 to 0.15625
- cotangent: bfloat16 [4096, 768], P(('dp', 'head')), may hold values from -6 to 6
Outputs:
- output: float32 [4096, 768], P(('dp', 'head'))
- grad_input: float32 [4096, 768], P(('dp', 'head'))
- grad_norm_gain: float32 [2, 2, 2, 768], P(None, None, None, 'dp')
- grad_norm_bias: float32 [2, 2, 2, 768], P(None, None, None, 'dp')
- grad_qkv: float32 [2, 768, 2304], P(None, 'dp')
- grad_out: float32 [2, 768, 768], P(None, 'dp')
- grad_up: float32 [2, 2, 768, 3072], P(None, None, 'dp')
- grad_down: float32 [2, 2, 3072, 768], P(None, None, 'dp')
Inputs may be any that keep to these rules, and one draw needn't show every extreme that they name: `segments`: along each row the ids never fall, every id appears, and each document covers at most half of 512 positions; one covers exactly that many. `routes`: in the rows of one device no expert is named by more than 96 rows.
All inputs are finite; a program needn't handle non-finite values.
Results may differ from a plain program's by a relative error of at most 0.015.
Values may be sent and summed in bfloat16 or wider, within the bound.
No kernel may reach another device: no remote copies, remote signals or barrier semaphores. Data moves between devices by JAX's collectives and lax.ppermute only.
A program may use at most 256 MiB of HBM per device.

v0:
```python
import math

import jax
import jax.numpy as jnp
from jax import lax
from jax.sharding import PartitionSpec as P

H = 12
HD = 64
MOST = 96


precise = lax.Precision.HIGHEST
far_below = -1e30


def norm_parts(values, gain_rows, bias_rows):
    row_mean = jnp.mean(values, axis=-1, keepdims=True)
    centred = values - row_mean
    inv_std = lax.rsqrt(jnp.mean(centred * centred, axis=-1, keepdims=True) + 1e-05)
    unit_rows = centred * inv_std
    return (unit_rows * gain_rows + bias_rows, unit_rows, inv_std)


def norm_back(gradient, unit_rows, inv_std, gain_rows):
    scaled = gradient * gain_rows
    return inv_std * (
        scaled
        - jnp.mean(scaled, axis=-1, keepdims=True)
        - unit_rows * jnp.mean(scaled * unit_rows, axis=-1, keepdims=True)
    )


def by_expert(selector, values):
    return jnp.einsum("te,td->ed", selector, values, precision=precise)


def gelu_slope(values):
    return (
        0.5 * (1.0 + lax.erf(values * 0.7071067811865476))
        + values * jnp.exp(-0.5 * values * values) * 0.3989422804014327
    )


def plan_routes(routes, most_rows):
    expert = routes[:, 0]
    token_total = expert.shape[0]
    sorted_pos = jnp.argsort(expert, stable=True)
    rank_pos = jnp.argsort(sorted_pos, stable=True)
    first_count = jnp.sum((expert == 0).astype(jnp.int32))
    starts = jnp.stack([jnp.int32(0), first_count])
    expert_load = jnp.stack([first_count, jnp.int32(token_total) - first_count])
    slot_ids = jnp.arange(most_rows, dtype=jnp.int32)
    slot_token = sorted_pos[jnp.minimum(starts[:, None] + slot_ids[None, :], token_total - 1)]
    slot_live = (slot_ids[None, :] < expert_load[:, None]).astype(jnp.bfloat16)[..., None]
    token_slot = expert * most_rows + rank_pos - jnp.where(expert == 1, first_count, 0)
    selector = jnp.stack([expert == 0, expert == 1], axis=1).astype(jnp.float32)
    return (slot_token, slot_live, token_slot, selector)


def score_rows(queries, keys_rows, seg_rows):
    score_scale = queries.shape[-1] ** (-0.5)
    scores = (
        jnp.einsum("bqhd,bkhd->bhqk", queries, keys_rows, preferred_element_type=jnp.float32)
        * score_scale
    )
    same_doc = seg_rows[:, None, :, None] == seg_rows[:, None, None, :]
    return jnp.where(same_doc, scores, far_below)


def attend_rows(packed):
    qkv_rows, seg_rows = packed
    masked = score_rows(qkv_rows[:, :, 0], qkv_rows[:, :, 1], seg_rows)
    row_top = jnp.max(masked, axis=-1, keepdims=True)
    exponent = jnp.exp(masked - row_top)
    row_total = jnp.sum(exponent, axis=-1, keepdims=True)
    attn_prob = (exponent / row_total).astype(jnp.bfloat16)
    attn_out = jnp.einsum(
        "bhqk,bkhd->bqhd", attn_prob, qkv_rows[:, :, 2], preferred_element_type=jnp.float32
    )
    return (attn_out.astype(jnp.bfloat16), (row_top + jnp.log(row_total))[..., 0])


def attend_back(packed):
    qkv_rows, seg_rows, log_total, grad_rows = packed
    queries = qkv_rows[:, :, 0]
    keys_rows = qkv_rows[:, :, 1]
    values_rows = qkv_rows[:, :, 2]
    score_scale = queries.shape[-1] ** (-0.5)
    masked = score_rows(queries, keys_rows, seg_rows)
    attn_prob = jnp.exp(masked - log_total[..., None])
    grad_prob = jnp.einsum(
        "bqhd,bkhd->bhqk", grad_rows, values_rows, preferred_element_type=jnp.float32
    )
    grad_values = jnp.einsum(
        "bhqk,bqhd->bkhd",
        attn_prob.astype(jnp.bfloat16),
        grad_rows,
        preferred_element_type=jnp.float32,
    )
    inner_sum = jnp.sum(attn_prob * grad_prob, axis=-1, keepdims=True)
    grad_score = (attn_prob * (grad_prob - inner_sum)).astype(jnp.bfloat16)
    grad_queries = (
        jnp.einsum("bhqk,bkhd->bqhd", grad_score, keys_rows, preferred_element_type=jnp.float32)
        * score_scale
    )
    grad_keys = (
        jnp.einsum("bhqk,bqhd->bkhd", grad_score, queries, preferred_element_type=jnp.float32)
        * score_scale
    )
    return jnp.stack([grad_queries, grad_keys, grad_values], axis=2).astype(jnp.bfloat16)


def body(tokens, segments, routes, norm_gain, norm_bias, w_qkv, w_out, w_up, w_down, cotangent):
    head_count = lax.axis_size("head")
    tok_count = tokens.shape[0]
    width = tokens.shape[1]
    row_count = segments.shape[0]
    row_len = segments.shape[1]
    local_heads = H // head_count
    step_rows = math.gcd(row_count, max(1, 512 // row_len))
    block_count = row_count // step_rows
    layer_count = norm_gain.shape[0]
    slot_token, slot_live, token_slot, selector = plan_routes(routes, MOST)
    second_route = routes == 1
    seg_blocks = segments.reshape(block_count, step_rows, row_len)
    stream = tokens.astype(jnp.float32)
    fetched = []
    saved = []
    for layer in range(layer_count):
        layer_w = (
            lax.all_gather(norm_gain[layer], "dp", axis=2, tiled=True),
            lax.all_gather(norm_bias[layer], "dp", axis=2, tiled=True),
            lax.all_gather(w_qkv[layer], "dp", axis=0, tiled=True),
            lax.all_gather(w_out[layer], "dp", axis=0, tiled=True),
            lax.all_gather(w_up[layer], "dp", axis=1, tiled=True),
            lax.all_gather(w_down[layer], "dp", axis=1, tiled=True),
        )
        fetched.append(layer_w)
        layer_gain, layer_bias, qkv_weight, out_weight, up_weight, down_weight = layer_w
        gain_first = jnp.where(second_route, layer_gain[0, 1], layer_gain[0, 0]).astype(jnp.float32)
        bias_first = jnp.where(second_route, layer_bias[0, 1], layer_bias[0, 0]).astype(jnp.float32)
        normed, unit_first, inv_first = norm_parts(stream, gain_first, bias_first)
        first_b = normed.astype(jnp.bfloat16)
        qkv_local = jnp.dot(first_b, qkv_weight, preferred_element_type=jnp.float32).astype(
            jnp.bfloat16
        )
        qkv_local = qkv_local.reshape(tok_count, 3, head_count, local_heads * HD)
        head_view = lax.all_to_all(qkv_local, "head", split_axis=2, concat_axis=0, tiled=True)
        head_view = head_view.reshape(block_count, step_rows, row_len, 3, local_heads, HD)
        attn_heads, log_total = lax.map(attend_rows, (head_view, seg_blocks))
        attn_tok = lax.all_to_all(
            attn_heads.reshape(head_count * tok_count, 1, local_heads * HD),
            "head",
            split_axis=0,
            concat_axis=1,
            tiled=True,
        ).reshape(tok_count, width)
        middle = stream + jnp.dot(attn_tok, out_weight, preferred_element_type=jnp.float32)
        gain_second = jnp.where(second_route, layer_gain[1, 1], layer_gain[1, 0]).astype(
            jnp.float32
        )
        bias_second = jnp.where(second_route, layer_bias[1, 1], layer_bias[1, 0]).astype(
            jnp.float32
        )
        normed_two, unit_second, inv_second = norm_parts(middle, gain_second, bias_second)
        second_b = normed_two.astype(jnp.bfloat16)
        buffer = jnp.take(second_b, slot_token, axis=0) * slot_live
        up_proj = jnp.einsum("esd,edf->esf", buffer, up_weight, preferred_element_type=jnp.float32)
        active = jax.nn.gelu(up_proj, approximate=False).astype(jnp.bfloat16)
        down_proj = jnp.einsum(
            "esf,efd->esd", active, down_weight, preferred_element_type=jnp.float32
        )
        branch = jnp.take(down_proj.reshape(2 * MOST, width), token_slot, axis=0)
        saved.append(
            (
                unit_first,
                inv_first,
                first_b,
                head_view,
                log_total,
                attn_tok,
                unit_second,
                inv_second,
                buffer,
                up_proj,
                active,
            )
        )
        stream = middle + branch
    gradient = cotangent.astype(jnp.float32)
    summed_all = [None] * layer_count
    for layer in reversed(range(layer_count)):
        layer_w = (
            lax.all_gather(norm_gain[layer], "dp", axis=2, tiled=True),
            lax.all_gather(norm_bias[layer], "dp", axis=2, tiled=True),
            lax.all_gather(w_qkv[layer], "dp", axis=0, tiled=True),
            lax.all_gather(w_out[layer], "dp", axis=0, tiled=True),
            lax.all_gather(w_up[layer], "dp", axis=1, tiled=True),
            lax.all_gather(w_down[layer], "dp", axis=1, tiled=True),
        )
        layer_gain, layer_bias, qkv_weight, out_weight, up_weight, down_weight = layer_w
        (
            unit_first,
            inv_first,
            first_b,
            head_view,
            log_total,
            attn_tok,
            unit_second,
            inv_second,
            buffer,
            up_proj,
            active,
        ) = saved[layer]
        gain_first = jnp.where(second_route, layer_gain[0, 1], layer_gain[0, 0]).astype(jnp.float32)
        gain_second = jnp.where(second_route, layer_gain[1, 1], layer_gain[1, 0]).astype(
            jnp.float32
        )
        grad_b = gradient.astype(jnp.bfloat16)
        grad_buffer = jnp.take(grad_b, slot_token, axis=0) * slot_live
        grad_down = jnp.einsum(
            "esf,esd->efd", active, grad_buffer, preferred_element_type=jnp.float32
        )
        grad_active = jnp.einsum(
            "esd,efd->esf", grad_buffer, down_weight, preferred_element_type=jnp.float32
        )
        grad_upper = (grad_active * gelu_slope(up_proj)).astype(jnp.bfloat16)
        grad_up = jnp.einsum("esd,esf->edf", buffer, grad_upper, preferred_element_type=jnp.float32)
        grad_slots = jnp.einsum(
            "esf,edf->esd", grad_upper, up_weight, preferred_element_type=jnp.float32
        )
        grad_second = jnp.take(grad_slots.reshape(2 * MOST, width), token_slot, axis=0)
        grad_middle = gradient + norm_back(grad_second, unit_second, inv_second, gain_second)
        gain_two = by_expert(selector, grad_second * unit_second)
        bias_two = by_expert(selector, grad_second)
        middle_b = grad_middle.astype(jnp.bfloat16)
        grad_outw = jnp.einsum("td,te->de", attn_tok, middle_b, preferred_element_type=jnp.float32)
        grad_attn = jnp.dot(middle_b, out_weight.T, preferred_element_type=jnp.float32).astype(
            jnp.bfloat16
        )
        grad_heads = lax.all_to_all(
            grad_attn.reshape(tok_count, head_count, local_heads * HD),
            "head",
            split_axis=1,
            concat_axis=0,
            tiled=True,
        )
        grad_heads = grad_heads.reshape(block_count, step_rows, row_len, local_heads, HD)
        grad_qkv_heads = lax.map(attend_back, (head_view, seg_blocks, log_total, grad_heads))
        grad_qkv_tok = lax.all_to_all(
            grad_qkv_heads.reshape(head_count * tok_count, 3, 1, local_heads * HD),
            "head",
            split_axis=0,
            concat_axis=2,
            tiled=True,
        ).reshape(tok_count, 3 * width)
        grad_qkvw = jnp.einsum(
            "td,tf->df", first_b, grad_qkv_tok, preferred_element_type=jnp.float32
        )
        grad_first = jnp.dot(grad_qkv_tok, qkv_weight.T, preferred_element_type=jnp.float32)
        gradient = grad_middle + norm_back(grad_first, unit_first, inv_first, gain_first)
        gain_one = by_expert(selector, grad_first * unit_first)
        bias_one = by_expert(selector, grad_first)
        gain_terms = jnp.stack([gain_one, gain_two])
        bias_terms = jnp.stack([bias_one, bias_two])
        shards = (
            lax.psum_scatter(gain_terms, "dp", scatter_dimension=2, tiled=True),
            lax.psum_scatter(bias_terms, "dp", scatter_dimension=2, tiled=True),
            lax.psum_scatter(grad_qkvw, "dp", scatter_dimension=0, tiled=True),
            lax.psum_scatter(grad_outw, "dp", scatter_dimension=0, tiled=True),
            lax.psum_scatter(grad_up, "dp", scatter_dimension=1, tiled=True),
            lax.psum_scatter(grad_down, "dp", scatter_dimension=1, tiled=True),
        )
        pieces = (
            lax.psum_scatter(
                shards[0].astype(jnp.bfloat16), "head", scatter_dimension=2, tiled=True
            ).astype(jnp.float32),
            lax.psum_scatter(
                shards[1].astype(jnp.bfloat16), "head", scatter_dimension=2, tiled=True
            ).astype(jnp.float32),
            lax.psum_scatter(
                shards[2].astype(jnp.bfloat16), "head", scatter_dimension=0, tiled=True
            ).astype(jnp.float32),
            lax.psum_scatter(
                shards[3].astype(jnp.bfloat16), "head", scatter_dimension=0, tiled=True
            ).astype(jnp.float32),
            lax.psum_scatter(
                shards[4].astype(jnp.bfloat16), "head", scatter_dimension=1, tiled=True
            ).astype(jnp.float32),
            lax.psum_scatter(
                shards[5].astype(jnp.bfloat16), "head", scatter_dimension=1, tiled=True
            ).astype(jnp.float32),
        )
        summed = (
            lax.all_gather(pieces[0].astype(jnp.bfloat16), "head", axis=2, tiled=True).astype(
                jnp.float32
            ),
            lax.all_gather(pieces[1].astype(jnp.bfloat16), "head", axis=2, tiled=True).astype(
                jnp.float32
            ),
            lax.all_gather(pieces[2].astype(jnp.bfloat16), "head", axis=0, tiled=True).astype(
                jnp.float32
            ),
            lax.all_gather(pieces[3].astype(jnp.bfloat16), "head", axis=0, tiled=True).astype(
                jnp.float32
            ),
            lax.all_gather(pieces[4].astype(jnp.bfloat16), "head", axis=1, tiled=True).astype(
                jnp.float32
            ),
            lax.all_gather(pieces[5].astype(jnp.bfloat16), "head", axis=1, tiled=True).astype(
                jnp.float32
            ),
        )
        summed_all[layer] = summed
    stacked = [
        jnp.stack([summed_all[layer][member] for layer in range(layer_count)])
        for member in range(6)
    ]
    return (
        stream,
        gradient,
        stacked[0],
        stacked[1],
        stacked[2],
        stacked[3],
        stacked[4],
        stacked[5],
    )


def solution(mesh):
    placed = (
        P(("dp", "head"), None),
        P("dp", None),
        P(("dp", "head"), None),
        P(None, None, None, "dp"),
        P(None, None, None, "dp"),
        P(None, "dp", None),
        P(None, "dp", None),
        P(None, None, "dp", None),
        P(None, None, "dp", None),
        P(("dp", "head"), None),
    )
    return jax.shard_map(
        body,
        mesh=mesh,
        in_specs=placed,
        out_specs=(
            P(("dp", "head"), None),
            P(("dp", "head"), None),
            P(None, None, None, "dp"),
            P(None, None, None, "dp"),
            P(None, "dp", None),
            P(None, "dp", None),
            P(None, None, "dp", None),
            P(None, None, "dp", None),
        ),
        check_vma=False,
    )
```

profile of v0, /device:TPU:0, one launch (start us, length us, event | category | flops | bytes accessed | tf_op | source)
XLA Modules:
  0.0 3018.6 jit_solution(4061575511070476291)
XLA Ops:
  27.3 34.0 %all-gather = bf16[1,2,2,768]{2,1,0,3:T(2,128)(2,1)S(1)} all-gather(bf16[1,2,2,96]{2,1,0,3:T(2,128)(2,1)S(1)} %copy.236), channel_id=2, replica_groups=mesh['dp'=8,'head'=4] {'dp'}, dimensions={3}, use_global_device_ids=true | all-gather | bytes 6912 | tf_op jit(solution)/shard_map/all_gather | solution.py:132
  61.3 32.0 %all-gather.1 = bf16[1,2,2,768]{2,1,0,3:T(2,128)(2,1)S(1)} all-gather(bf16[1,2,2,96]{2,1,0,3:T(2,128)(2,1)S(1)} %copy.237), channel_id=3, replica_groups=mesh['dp'=8,'head'=4] {'dp'}, dimensions={3}, use_global_device_ids=true | all-gather | bytes 6912 | tf_op jit(solution)/shard_map/all_gather | solution.py:133
  93.3 32.0 %all-gather.6 = bf16[1,2,2,768]{2,1,0,3:T(2,128)(2,1)S(1)} all-gather(bf16[1,2,2,96]{2,1,0,3:T(2,128)(2,1)S(1)} %copy.238), channel_id=8, replica_groups=mesh['dp'=8,'head'=4] {'dp'}, dimensions={3}, use_global_device_ids=true | all-gather | bytes 6912 | tf_op jit(solution)/shard_map/all_gather | solution.py:132
  127.3 9.1 slice_reduce_fusion.11
  136.4 9.7 slice_reduce_fusion.9
  146.1 9.7 slice_reduce_fusion.3
  164.1 32.3 %all-gather.7 = bf16[1,2,2,768]{2,1,0,3:T(2,128)(2,1)S(1)} all-gather(bf16[1,2,2,96]{2,1,0,3:T(2,128)(2,1)S(1)} %copy.239), channel_id=9, replica_groups=mesh['dp'=8,'head'=4] {'dp'}, dimensions={3}, use_global_device_ids=true | all-gather | bytes 6912 | tf_op jit(solution)/shard_map/all_gather | solution.py:133
  196.4 9.5 slice_reduce_fusion.1
  215.1 5.2 all-to-all-done.1
  224.4 50.0 %all-gather.37.cloned.1.call-done = bf16[1,2,768,3072]{3,2,1,0:T(8,128)(2,1)} async-done(((bf16[1,2,96,3072]{3,2,1,0:T(8,128)(2,1)}), bf16[1,2,768,3072]{3,2,1,0:T(8,128)(2,1)}) %all-gather.37.cloned.1.call-update) | async-done | bytes 9437200 | tf_op jit(solution)/shard_map/all_gather | solution.py:136
  274.4 7.4 fusion.98
  281.8 131.5 %all-gather.39.cloned.1.call-done = bf16[1,2,3072,768]{3,2,1,0:T(8,128)(2,1)} async-done(((bf16[1,2,384,768]{3,2,1,0:T(8,128)(2,1)}), bf16[1,2,3072,768]{3,2,1,0:T(8,128)(2,1)}) %all-gather.39.cloned.1.call-update) | async-done | bytes 9437200 | tf_op jit(solution)/shard_map/all_gather | solution.py:137
  413.4 9.4 fusion.10
  424.1 54.7 %all-gather.41.cloned.1.call-done = bf16[1,768,2304]{2,1,0:T(8,128)(2,1)} async-done(((bf16[1,96,2304]{2,1,0:T(8,128)(2,1)}), bf16[1,768,2304]{2,1,0:T(8,128)(2,1)}) %all-gather.41.cloned.1.call-update) | async-done | bytes 3538960 | tf_op jit(solution)/shard_map/all_gather | solution.py:134
  481.9 12.1 all_to_all.120
  525.7 133.8 %all-gather.45.cloned.1.call-done = bf16[1,2,768,3072]{3,2,1,0:T(8,128)(2,1)} async-done(((bf16[1,2,96,3072]{3,2,1,0:T(8,128)(2,1)}), bf16[1,2,768,3072]{3,2,1,0:T(8,128)(2,1)}) %all-gather.45.cloned.1.call-update) | async-done | bytes 9437200 | tf_op jit(solution)/shard_map/all_gather | solution.py:136
  659.5 6.2 fusion.99
  667.3 11.6 fusion.132
  678.9 119.6 %all-gather.47.cloned.1.call-done = bf16[1,2,3072,768]{3,2,1,0:T(8,128)(2,1)} async-done(((bf16[1,2,384,768]{3,2,1,0:T(8,128)(2,1)}), bf16[1,2,3072,768]{3,2,1,0:T(8,128)(2,1)}) %all-gather.47.cloned.1.call-update) | async-done | bytes 9437200 | tf_op jit(solution)/shard_map/all_gather | solution.py:137
  798.5 10.0 fusion.2
  811.5 7.5 fusion.22
  819.0 8.0 fusion.4
  839.2 5.2 all-to-all-done.4
  858.3 17.2 all_to_all.121
  883.4 12.8 fusion.133
  897.6 8.0 fusion.131
  905.6 7.5 fusion.25
  913.2 8.2 fusion.130
  924.7 6.9 fusion.12
  935.4 4.2 fusion.192
  948.9 4.6 all-to-all-done.6
  976.3 17.2 all_to_all.122
  1000.6 113.3 %reduce-scatter.61.cloned.1.call-done = f32[2,384,768]{2,1,0:T(8,128)} async-done(((f32[2,3072,768]{2,1,0:T(8,128)}), f32[2,384,768]{2,1,0:T(8,128)}) %reduce-scatter.61.cloned.1.call-update) | async-done | bytes 2359312 | tf_op jit(solution)/shard_map/reduce_scatter | solution.py:273
  1116.8 313.2 %reduce-scatter.57.cloned.1.call-done = f32[2,384,768]{2,1,0:T(8,128)} async-done(((f32[2,3072,768]{2,1,0:T(8,128)}), f32[2,384,768]{2,1,0:T(8,128)}) %reduce-scatter.57.cloned.1.call-update) | async-done | bytes 2359312 | tf_op jit(solution)/shard_map/reduce_scatter | solution.py:273
  1433.0 313.3 %reduce-scatter.55.cloned.1.call-done = f32[2,96,3072]{2,1,0:T(8,128)} async-done(((f32[2,768,3072]{2,1,0:T(8,128)}), f32[2,96,3072]{2,1,0:T(8,128)}) %reduce-scatter.55.cloned.1.call-update) | async-done | bytes 2359312 | tf_op jit(solution)/shard_map/reduce_scatter | solution.py:272
  1764.2 298.2 %reduce-scatter.53.cloned.1.call-done = f32[2,96,3072]{2,1,0:T(8,128)} async-done(((f32[2,768,3072]{2,1,0:T(8,128)}), f32[2,96,3072]{2,1,0:T(8,128)}) %reduce-scatter.53.cloned.1.call-update) | async-done | bytes 2359312 | tf_op jit(solution)/shard_map/reduce_scatter | solution.py:272
  2066.8 67.8 %reduce-scatter.49.cloned.1.call-done = f32[96,768]{1,0:T(8,128)} async-done(((f32[768,768]{1,0:T(8,128)}), f32[96,768]{1,0:T(8,128)}) %reduce-scatter.49.cloned.1.call-update) | async-done | bytes 294928 | tf_op jit(solution)/shard_map/reduce_scatter | solution.py:271
  2136.4 69.7 %reduce-scatter.45.cloned.1.call-done = f32[96,768]{1,0:T(8,128)} async-done(((f32[768,768]{1,0:T(8,128)}), f32[96,768]{1,0:T(8,128)}) %reduce-scatter.45.cloned.1.call-update) | async-done | bytes 294928 | tf_op jit(solution)/shard_map/reduce_scatter | solution.py:271
  2207.8 129.9 %reduce-scatter.41.cloned.1.call-done = f32[96,2304]{1,0:T(8,128)} async-done(((f32[768,2304]{1,0:T(8,128)}), f32[96,2304]{1,0:T(8,128)}) %reduce-scatter.41.cloned.1.call-update) | async-done | bytes 884752 | tf_op jit(solution)/shard_map/reduce_scatter | solution.py:270
  2339.7 130.0 %reduce-scatter.37.cloned.1.call-done = f32[96,2304]{1,0:T(8,128)} async-done(((f32[768,2304]{1,0:T(8,128)}), f32[96,2304]{1,0:T(8,128)}) %reduce-scatter.37.cloned.1.call-update) | async-done | bytes 884752 | tf_op jit(solution)/shard_map/reduce_scatter | solution.py:270
  2471.8 25.2 reduce-scatter.63.cloned.1.call-done
  2497.1 28.3 reduce-scatter.59.cloned.1.call-done
  2525.4 28.8 reduce-scatter.75.cloned.1.call-done
  2557.7 61.3 %reduce-scatter.71.cloned.1.call-done = f32[96,4]{1,0:T(8,128)} async-done(((f32[768,4]{1,0:T(8,128)}), f32[96,4]{1,0:T(8,128)}) %reduce-scatter.71.cloned.1.call-update) | async-done | bytes 1552
  2620.1 63.7 %reduce-scatter.67.cloned.1.call-done = f32[96,4]{1,0:T(8,128)} async-done(((f32[768,4]{1,0:T(8,128)}), f32[96,4]{1,0:T(8,128)}) %reduce-scatter.67.cloned.1.call-update) | async-done | bytes 1552
  2685.7 62.1 %reduce-scatter.69.cloned.1.call-done = f32[96,4]{1,0:T(8,128)} async-done(((f32[768,4]{1,0:T(8,128)}), f32[96,4]{1,0:T(8,128)}) %reduce-scatter.69.cloned.1.call-update) | async-done | bytes 1552
  2748.8 63.0 %reduce-scatter.65.cloned.1.call-done = f32[96,4]{1,0:T(8,128)} async-done(((f32[768,4]{1,0:T(8,128)}), f32[96,4]{1,0:T(8,128)}) %reduce-scatter.65.cloned.1.call-update) | async-done | bytes 1552
  2812.8 5.7 all-reduce.4
  2818.4 21.4 reduce-scatter.73.cloned.1.call-done
  2842.0 5.2 all_gather.96
  2847.5 5.2 all_gather.97
  2853.0 5.2 all_gather.94
  2858.5 5.2 all_gather.95
  2865.0 5.7 all_gather.101
  2870.7 13.2 reduce-scatter.47.cloned.1.call-done
  2883.9 5.7 all_gather.100
  2890.4 17.6 reduce-scatter.43.cloned.1.call-done
  2908.0 6.5 all_gather.99
  2914.5 17.1 reduce-scatter.39.cloned.1.call-done
  2931.6 6.5 all_gather.98
  2939.4 11.2 all-gather.31.cloned.1.call-done
  2950.7 18.9 all-gather.29.cloned.1.call-done
  2973.7 14.9 all-gather.27.cloned.1.call-done
  2988.6 19.1 all-gather.25.cloned.1.call-done
  (507 shorter events, 221.3 us)
Async XLA Ops:
  7.2 148.6 %all-gather.33.cloned.1.call-start = ((), (), s32[]{:S(2)}) async-start(), calls=%async_computation.46 | async-start | bytes 3981312 | tf_op jit(solution)/shard_map/all_gather | solution.py:134
  9.5 211.6 %all-gather.35.cloned.1.call-start = ((), (), s32[]{:S(2)}) async-start(), calls=%async_computation.47 | async-start | bytes 1327104 | tf_op jit(solution)/shard_map/all_gather | solution.py:135
  10.3 264.1 %all-gather.37.cloned.1.call-start = ((), (), s32[]{:S(2)}) async-start(), calls=%async_computation.48 | async-start | bytes 10616832 | tf_op jit(solution)/shard_map/all_gather | solution.py:136
  12.0 401.4 %all-gather.39.cloned.1.call-start = ((), (), s32[]{:S(2)}) async-start(), calls=%async_computation.49 | async-start | bytes 10616832 | tf_op jit(solution)/shard_map/all_gather | solution.py:137
  15.2 463.6 %all-gather.41.cloned.1.call-start = ((), (), s32[]{:S(2)}) async-start(), calls=%async_computation.50 | async-start | bytes 3981312 | tf_op jit(solution)/shard_map/all_gather | solution.py:134
  15.8 504.6 %all-gather.43.cloned.1.call-start = ((), (), s32[]{:S(2)}) async-start(), calls=%async_computation.51 | async-start | bytes 1327104 | tf_op jit(solution)/shard_map/all_gather | solution.py:135
  16.4 643.1 %all-gather.45.cloned.1.call-start = ((), (), s32[]{:S(2)}) async-start(), calls=%async_computation.52 | async-start | bytes 10616832 | tf_op jit(solution)/shard_map/all_gather | solution.py:136
  16.5 109.5 %copy-start.8 = (bf16[128,768]{1,0:T(8,128)(2,1)S(1)}, bf16[128,768]{1,0:T(8,128)(2,1)}, u32[]{:S(2)}) copy-start(bf16[128,768]{1,0:T(8,128)(2,1)} %param.14) | copy-start | bytes 589828
  17.2 109.9 %copy-start.95 = (s32[1,512]{1,0:T(1,128)S(1)}, s32[1,512]{1,0:T(1,128)}, u32[]{:S(2)}) copy-start(s32[1,512]{1,0:T(1,128)} %param.15) | copy-start | bytes 6148
  17.2 781.4 %all-gather.47.cloned.1.call-start = ((), (), s32[]{:S(2)}) async-start(), calls=%async_computation.53 | async-start | bytes 10616832 | tf_op jit(solution)/shard_map/all_gather | solution.py:137
  126.1 29.7 copy-start.69
  126.3 29.5 copy-start.75
  127.0 147.4 %copy-start.88 = (pred[2,96]{1,0:T(4,128)(4,1)}, pred[2,96]{1,0:T(4,128)(4,1)S(1)}, u32[]{:S(2)}) copy-start(pred[2,96]{1,0:T(4,128)(4,1)S(1)} %get-tuple-element.167) | copy-start | bytes 580
  127.0 147.4 %copy-start.91 = (bf16[2,96]{1,0:T(2,128)(2,1)}, bf16[2,96]{1,0:T(2,128)(2,1)S(1)}, u32[]{:S(2)}) copy-start(bf16[2,96]{1,0:T(2,128)(2,1)S(1)} %get-tuple-element.168) | copy-start | bytes 1156
  136.3 22.2 copy-start.38
  136.4 22.2 copy-start.40
  136.4 86.8 %copy-start.56 = (bf16[768]{0:T(1024)(128)(2,1)}, bf16[768]{0:T(1024)(128)(2,1)S(1)}, u32[]{:S(2)}) copy-start(bf16[768]{0:T(1024)(128)(2,1)S(1)} %get-tuple-element.116) | copy-start | bytes 4612
  136.4 86.8 %copy-start.58 = (bf16[768]{0:T(1024)(128)(2,1)}, bf16[768]{0:T(1024)(128)(2,1)S(1)}, u32[]{:S(2)}) copy-start(bf16[768]{0:T(1024)(128)(2,1)S(1)} %get-tuple-element.117) | copy-start | bytes 4612
  155.8 323.0 %copy-start.42 = (bf16[768]{0:T(1024)(128)(2,1)}, bf16[768]{0:T(1024)(128)(2,1)S(1)}, u32[]{:S(2)}) copy-start(bf16[768]{0:T(1024)(128)(2,1)S(1)} %get-tuple-element.111) | copy-start | bytes 4612
  159.8 46.2 %all-to-all-start = ((bf16[128,3,4,192]{0,3,1,2:T(8,128)(2,1)}), bf16[128,3,4,192]{0,3,1,2:T(8,128)(2,1)S(1)}, u32[]{:S(2)}, u32[]{:S(2)}) async-start(bf16[128,3,4,192]{0,3,1,2:T(8,128)(2,1)} %copy.163), calls=%async_computation | async-start | bytes 1179648 | tf_op jit(solution)/shard_map/all_to_all | solution.py:149
  163.9 259.7 %copy-start.52 = (pred[128]{0:T(512)(128)(4,1)}, pred[128]{0:T(512)(128)(4,1)S(1)}, u32[]{:S(2)}) copy-start(pred[128]{0:T(512)(128)(4,1)S(1)} %get-tuple-element.132) | copy-start | bytes 388
  205.9 272.9 %copy-start.48 = (bf16[768]{0:T(1024)(128)(2,1)}, bf16[768]{0:T(1024)(128)(2,1)S(1)}, u32[]{:S(2)}) copy-start(bf16[768]{0:T(1024)(128)(2,1)S(1)} %get-tuple-element.114) | copy-start | bytes 4612
  205.9 272.9 %copy-start.50 = (bf16[768]{0:T(1024)(128)(2,1)}, bf16[768]{0:T(1024)(128)(2,1)S(1)}, u32[]{:S(2)}) copy-start(bf16[768]{0:T(1024)(128)(2,1)S(1)} %get-tuple-element.115) | copy-start | bytes 4612
  211.4 8.9 all-to-all-start.1
  215.0 207.8 %copy-start.94 = (s32[1024]{0:T(1024)}, s32[1024]{0:T(1024)S(1)}, u32[]{:S(2)}) copy-start(s32[1024]{0:T(1024)S(1)} %pad_clamp_fusion) | copy-start | bytes 12292
  222.9 200.7 %copy-start.5 = (f32[128,768]{1,0:T(8,128)}, f32[128,768]{1,0:T(8,128)S(1)}, u32[]{:S(2)}) copy-start(f32[128,768]{1,0:T(8,128)S(1)} %get-tuple-element.154) | copy-start | bytes 1179652
  222.9 58.9 %copy-start.82 = (f32[128]{0:T(128)}, f32[128]{0:T(128)S(1)}, u32[]{:S(2)}) copy-start(f32[128]{0:T(128)S(1)} %broadcast_multiply_fusion.10) | copy-start | bytes 1540
  223.2 58.7 %copy-start.96 = (f32[128]{0:T(128)}, f32[128]{0:T(128)S(1)}, u32[]{:S(2)}) copy-start(f32[128]{0:T(128)S(1)} %add_rsqrt_fusion.2) | copy-start | bytes 1540
  224.4 57.4 %copy-start.33 = (bf16[192,768]{1,0:T(8,128)(2,1)}, bf16[192,768]{1,0:T(8,128)(2,1)S(1)}, u32[]{:S(2)}) copy-start(bf16[192,768]{1,0:T(8,128)(2,1)S(1)} %gather_fusion.1) | copy-start | bytes 884740
  281.8 140.9 %copy-start.109 = (u8[96,3072]{1,0:T(8,128)(4,1)}, u8[96,3072]{1,0:T(8,128)(4,1)S(1)}, u32[]{:S(2)}) copy-start(u8[96,3072]{1,0:T(8,128)(4,1)S(1)} %get-tuple-element.98) | copy-start | bytes 884740
  281.8 140.9 %copy-start.111 = (u8[96,3072]{1,0:T(8,128)(4,1)}, u8[96,3072]{1,0:T(8,128)(4,1)S(1)}, u32[]{:S(2)}) copy-start(u8[96,3072]{1,0:T(8,128)(4,1)S(1)} %get-tuple-element.99) | copy-start | bytes 884740
  423.8 57.7 %copy-start.3 = (f32[128,768]{1,0:T(8,128)}, f32[128,768]{1,0:T(8,128)S(1)}, u32[]{:S(2)}) copy-start(f32[128,768]{1,0:T(8,128)S(1)} %get-tuple-element.131) | copy-start | bytes 1179652
  423.9 57.7 %copy-start.71 = (f32[128]{0:T(128)}, f32[128]{0:T(128)S(1)}, u32[]{:S(2)}) copy-start(f32[128]{0:T(128)S(1)} %broadcast_multiply_fusion.9) | copy-start | bytes 1540
  424.1 57.8 %copy-start.77 = (f32[128]{0:T(128)}, f32[128]{0:T(128)S(1)}, u32[]{:S(2)}) copy-start(f32[128]{0:T(128)S(1)} %add_rsqrt_fusion.1) | copy-start | bytes 1540
  505.1 8.7 all-to-all-start.3
  508.4 605.5 %reduce-scatter.61.cloned.1.call-start = ((), (), s32[]{:S(2)}) async-start(), calls=%async_computation.43 | async-start | bytes 21233664 | tf_op jit(solution)/shard_map/reduce_scatter | solution.py:273
  835.7 8.7 all-to-all-start.4
  839.1 590.9 %reduce-scatter.57.cloned.1.call-start = ((), (), s32[]{:S(2)}) async-start(), calls=%async_computation.40 | async-start | bytes 21233664 | tf_op jit(solution)/shard_map/reduce_scatter | solution.py:273
  896.3 850.0 %reduce-scatter.55.cloned.1.call-start = ((), (), s32[]{:S(2)}) async-start(), calls=%async_computation.38 | async-start | bytes 21233664 | tf_op jit(solution)/shard_map/reduce_scatter | solution.py:272
  905.6 1156.9 %reduce-scatter.53.cloned.1.call-start = ((), (), s32[]{:S(2)}) async-start(), calls=%async_computation.36 | async-start | bytes 21233664 | tf_op jit(solution)/shard_map/reduce_scatter | solution.py:272
  921.5 1213.2 %reduce-scatter.49.cloned.1.call-start = ((), (), s32[]{:S(2)}) async-start(), calls=%async_computation.34 | async-start | bytes 2654208 | tf_op jit(solution)/shard_map/reduce_scatter | solution.py:271
  924.3 1281.8 %reduce-scatter.45.cloned.1.call-start = ((), (), s32[]{:S(2)}) async-start(), calls=%async_computation.32 | async-start | bytes 2654208 | tf_op jit(solution)/shard_map/reduce_scatter | solution.py:271
  935.3 1402.4 %reduce-scatter.41.cloned.1.call-start = ((), (), s32[]{:S(2)}) async-start(), calls=%async_computation.30 | async-start | bytes 7962624 | tf_op jit(solution)/shard_map/reduce_scatter | solution.py:270
  944.2 9.4 all-to-all-start.6
  948.2 1521.6 %reduce-scatter.37.cloned.1.call-start = ((), (), s32[]{:S(2)}) async-start(), calls=%async_computation.28 | async-start | bytes 7962624 | tf_op jit(solution)/shard_map/reduce_scatter | solution.py:270
  976.2 20.1 copy-start.9
  1000.6 1496.4 %reduce-scatter.63.cloned.1.call-start = ((), (), s32[]{:S(2)}) async-start(), calls=%async_computation.44 | async-start | bytes 1474560 | tf_op jit(solution)/shard_map/reduce_scatter | solution.py:291
  1116.8 1408.6 %reduce-scatter.59.cloned.1.call-start = ((), (), s32[]{:S(2)}) async-start(), calls=%async_computation.41 | async-start | bytes 1474560 | tf_op jit(solution)/shard_map/reduce_scatter | solution.py:291
  1432.9 1121.3 %reduce-scatter.75.cloned.1.call-start = ((), (), s32[]{:S(2)}) async-start(), calls=%async_computation.59 | async-start | bytes 1474560
  1750.7 868.4 %reduce-scatter.71.cloned.1.call-start = ((), (), s32[]{:S(2)}) async-start(), calls=%async_computation.57 | async-start | bytes 442368
  1754.7 929.1 %reduce-scatter.67.cloned.1.call-start = ((), (), s32[]{:S(2)}) async-start(), calls=%async_computation.55 | async-start | bytes 442368
  1756.4 991.4 %reduce-scatter.69.cloned.1.call-start = ((), (), s32[]{:S(2)}) async-start(), calls=%async_computation.56 | async-start | bytes 442368
  1762.4 1049.4 %reduce-scatter.65.cloned.1.call-start = ((), (), s32[]{:S(2)}) async-start(), calls=%async_computation.54 | async-start | bytes 442368
  1764.1 1075.7 %reduce-scatter.73.cloned.1.call-start = ((), (), s32[]{:S(2)}) async-start(), calls=%async_computation.58 | async-start | bytes 1474560
  2066.8 798.3 %reduce-scatter.51.cloned.1.call-start = ((), (), s32[]{:S(2)}) async-start(), calls=%async_computation.35 | async-start | bytes 184320 | tf_op jit(solution)/shard_map/reduce_scatter | solution.py:285
  2136.3 747.6 %reduce-scatter.47.cloned.1.call-start = ((), (), s32[]{:S(2)}) async-start(), calls=%async_computation.33 | async-start | bytes 184320 | tf_op jit(solution)/shard_map/reduce_scatter | solution.py:285
  2207.7 700.3 %reduce-scatter.43.cloned.1.call-start = ((), (), s32[]{:S(2)}) async-start(), calls=%async_computation.31 | async-start | bytes 552960 | tf_op jit(solution)/shard_map/reduce_scatter | solution.py:282
  2339.6 216.9 %copy-start.107 = (u32[32]{0:T(128)S(1)}, u32[32]{0:T(128)}, u32[]{:S(2)}) copy-start(u32[32]{0:T(128)} %constant.201) | copy-start | bytes 388
  2339.6 345.1 %copy-start.20 = (f32[128,768]{1,0:T(8,128)S(1)}, f32[128,768]{1,0:T(8,128)}, u32[]{:S(2)}) copy-start(f32[128,768]{1,0:T(8,128)} %copy-done.19) | copy-start | bytes 1179652
  2339.7 591.9 %reduce-scatter.39.cloned.1.call-start = ((), (), s32[]{:S(2)}) async-start(), calls=%async_computation.29 | async-start | bytes 552960 | tf_op jit(solution)/shard_map/reduce_scatter | solution.py:282
  2471.8 478.9 %all-gather.31.cloned.1.call-start = ((), (), s32[]{:S(2)}) async-start(), calls=%async_computation.45 | async-start | bytes 1474560 | tf_op jit(solution)/shard_map/all_gather | solution.py:311
  2497.0 472.6 %all-gather.29.cloned.1.call-start = ((), (), s32[]{:S(2)}) async-start(), calls=%async_computation.42 | async-start | bytes 1474560 | tf_op jit(solution)/shard_map/all_gather | solution.py:311
  2525.4 463.3 %all-gather.27.cloned.1.call-start = ((), (), s32[]{:S(2)}) async-start(), calls=%async_computation.39 | async-start | bytes 1474560 | tf_op jit(solution)/shard_map/all_gather | solution.py:308
  2556.2 451.5 %all-gather.25.cloned.1.call-start = ((), (), s32[]{:S(2)}) async-start(), calls=%async_computation.37 | async-start | bytes 1474560 | tf_op jit(solution)/shard_map/all_gather | solution.py:308
  (88 other events, 466.2 us)
Sparse Core Ops, SparseCore 0:
  10.8 76.9 all-gather.32
  90.5 41.5 all-gather.34
  134.9 139.4 all-gather.36
  276.5 136.8 all-gather.38
  415.4 63.3 all-gather.40
  480.8 39.5 all-gather.42
  522.6 136.8 all-gather.44
  662.2 136.2 all-gather.46
  802.4 311.4 reduce-scatter.60
  1117.6 312.3 reduce-scatter.56
  1433.9 312.3 reduce-scatter.54
  1750.0 312.4 reduce-scatter.52
  2066.5 68.1 reduce-scatter.48
  2138.0 67.9 reduce-scatter.44
  2209.6 128.0 reduce-scatter.40
  2341.6 128.0 reduce-scatter.36
  2472.2 24.7 reduce-scatter.62
  2499.6 25.7 reduce-scatter.58
  2528.5 25.7 reduce-scatter.74
  2557.7 61.3 reduce-scatter.70
  2623.3 60.4 reduce-scatter.66
  2687.3 60.4 reduce-scatter.68
  2751.4 60.3 reduce-scatter.64
  2815.0 24.8 reduce-scatter.72
  2842.3 19.6 reduce-scatter.50
  2864.2 19.6 reduce-scatter.46
  2886.8 21.1 reduce-scatter.42
  2910.5 21.0 reduce-scatter.38
  2933.2 17.4 all-gather.30
  2952.1 17.4 all-gather.28
  2971.1 17.4 all-gather.26
  2990.2 17.4 all-gather.24
where the time goes:
time: 3020 us
  waiting for transfers between devices  2410 us (80%)
  blocking collectives  228 us (8%)
  matrix products  158 us (5%)
  local copies, waits for them, and re-layouts  124 us (4%)
  other arithmetic  57.2 us (2%)
    reduce_scatter x2, waiting for transfers between devices, body(): lax.psum_scatter(grad_up, 'dp', scatter_dimension=1, tiled=True)  612 us
    reduce_scatter x2, waiting for transfers between devices, body(): lax.psum_scatter(grad_down, 'dp', scatter_dimension=1, tiled=True)  426 us
    unnamed x38, waiting for transfers between devices  303 us
    reduce_scatter x2, waiting for transfers between devices, body(): lax.psum_scatter(grad_qkvw, 'dp', scatter_dimension=0, tiled=True)  260 us
    all_gather x2, waiting for transfers between devices, body(): lax.all_gather(w_down[layer], 'dp', axis=1, tiled=True)  251 us
    all_gather x2, waiting for transfers between devices, body(): lax.all_gather(w_up[layer], 'dp', axis=1, tiled=True)  184 us
    reduce_scatter x2, waiting for transfers between devices, body(): lax.psum_scatter(grad_outw, 'dp', scatter_dimension=0, tiled=True)  138 us
    all_gather x2, blocking collectives, body(): lax.all_gather(norm_gain[layer], 'dp', axis=2, tiled=True)  66 us
  transfers between devices with their start and end apart: 37, of which 33 were waited for; matrix products, arithmetic and copies ran while one was open for 11% of the time, Pallas kernels for 0%

commit v1 on v0

v1 whole, which is shorter than its diff:
```python
import jax
import jax.numpy as jnp
from jax import lax
from jax.experimental import pallas as pl
from jax.experimental.pallas import tpu as pltpu
from jax.sharding import PartitionSpec as P

H = 12
HD = 64
BF = jnp.bfloat16
F32 = jnp.float32
VMEM_BYTES = 26 * 1024 * 1024
COLS = 256
PACKED = 768
KEPT = 640

far_below = -1e30
scale = HD**-0.5


def nn(a, b):
    return lax.dot_general(a, b, (((1,), (0,)), ((), ())), preferred_element_type=F32)


def nt(a, b):
    return lax.dot_general(a, b, (((1,), (1,)), ((), ())), preferred_element_type=F32)


def tn(a, b):
    return lax.dot_general(a, b, (((0,), (0,)), ((), ())), preferred_element_type=F32)


def shape(*dims, dtype=BF):
    return jax.ShapeDtypeStruct(dims, dtype)


def smem():
    return pl.BlockSpec(memory_space=pltpu.SMEM)


def whole(*dims):
    return pl.BlockSpec(dims, lambda i: (0,) * len(dims))


def call(kernel, out_shape, name, micros=0, **rest):
    return pl.pallas_call(
        kernel,
        out_shape=out_shape,
        name=name,
        compiler_params=pltpu.CompilerParams(vmem_limit_bytes=VMEM_BYTES),
        cost_estimate=pl.CostEstimate(
            flops=micros * 1_000_000_000, bytes_accessed=0, transcendentals=0
        ),
        **rest,
    )


def unit_of(values):
    centred = values - jnp.mean(values, axis=-1, keepdims=True)
    inv_std = lax.rsqrt(jnp.mean(centred * centred, axis=-1, keepdims=True) + 1e-05)
    return centred * inv_std, inv_std


def norm_rows(values, par_ref, second):
    gain = jnp.where(second, par_ref[1:2, :], par_ref[0:1, :])
    bias = jnp.where(second, par_ref[3:4, :], par_ref[2:3, :])
    return (unit_of(values)[0] * gain + bias).astype(BF)


def norm_back_rows(grad, incoming, base, par_ref, second, terms_ref):
    unit, inv_std = unit_of(base)
    scaled = incoming * jnp.where(second, par_ref[1:2, :], par_ref[0:1, :])
    fresh = grad + inv_std * (
        scaled
        - jnp.mean(scaled, axis=-1, keepdims=True)
        - unit * jnp.mean(scaled * unit, axis=-1, keepdims=True)
    )
    gain_term = incoming * unit
    zero = jnp.zeros_like(incoming)
    terms_ref[0:1, :] += jnp.sum(jnp.where(second, zero, gain_term), axis=0, keepdims=True)
    terms_ref[1:2, :] += jnp.sum(jnp.where(second, gain_term, zero), axis=0, keepdims=True)
    terms_ref[2:3, :] += jnp.sum(jnp.where(second, zero, incoming), axis=0, keepdims=True)
    terms_ref[3:4, :] += jnp.sum(jnp.where(second, incoming, zero), axis=0, keepdims=True)
    return fresh


def each_block(head, mine_ref, other_ref, act):
    core = head & 1
    pairs, rows = mine_ref.shape[0], mine_ref.shape[1]
    for pair in range(pairs):
        for ref, side in ((mine_ref, core), (other_ref, 1 - core)):
            at = pl.multiple_of((2 * pair + side) * rows, rows)
            act(pl.ds(at, rows), ref[pair].astype(F32))


def split_out(head, total_ref, keep_ref, send_ref):
    core = head & 1
    pairs, rows = keep_ref.shape[0], keep_ref.shape[1]
    for pair in range(pairs):
        at = pl.multiple_of((2 * pair + core) * rows, rows)
        keep_ref[pair] = total_ref[pl.ds(at, rows), :]
        at = pl.multiple_of((2 * pair + 1 - core) * rows, rows)
        send_ref[pair] = total_ref[pl.ds(at, rows), :].astype(BF)


def attend_math(first_ref, w_ref, segc_ref, segr_ref, qkv_ref, attn_ref, lse_ref):
    heads = attn_ref.shape[0] // HD
    qkv = nn(first_ref[...], w_ref[:, : qkv_ref.shape[1]]).astype(BF)
    qkv_ref[...] = qkv
    turned = qkv.T
    same = segc_ref[...] == segr_ref[...]
    for j in range(heads):
        at_q, at_k, at_v = (HD * (j + heads * part) for part in range(3))
        scores = nn(qkv[:, at_k : at_k + HD], turned[at_q : at_q + HD]) * scale
        scores = jnp.where(same, scores, far_below)
        top = jnp.max(scores, axis=0, keepdims=True)
        exponent = jnp.exp(scores - top)
        total = jnp.sum(exponent, axis=0, keepdims=True)
        prob = (exponent / total).astype(BF)
        attn_ref[HD * j : HD * (j + 1), :] = nn(turned[at_v : at_v + HD], prob).astype(BF)
        lse_ref[j : j + 1, :] = top + jnp.log(total)


def join_lanes(blocks_ref, layer, out_ref):
    cols = out_ref.shape[1] // blocks_ref.shape[0]
    for part in range(blocks_ref.shape[0]):
        out_ref[:, part * cols : (part + 1) * cols] = blocks_ref[
            part, :, layer * cols : (layer + 1) * cols
        ]


def attend_first_kernel(
    tok_ref, small_ref, route_ref, w_ref, segc_ref, segr_ref,
    par_ref, first_ref, qkv_ref, attn_ref, lse_ref,
):
    turned = small_ref[...].astype(F32).T
    par_ref[...] = turned[: par_ref.shape[0]]
    first_ref[...] = norm_rows(tok_ref[...].astype(F32), par_ref, route_ref[...] == 1)
    attend_math(first_ref, w_ref, segc_ref, segr_ref, qkv_ref, attn_ref, lse_ref)


def project_kernel(head_ref, attn_ref, wo_ref, keep_ref, send_ref, total_ref, wide_ref):
    join_lanes(wo_ref, 0, wide_ref)
    total_ref[...] = tn(attn_ref[...], wide_ref[...])
    split_out(head_ref[0], total_ref, keep_ref, send_ref)


def attend_kernel(
    layer, head_ref, base_ref, mine_ref, other_ref, par_ref, route_ref, w_ref, wo_ref, segc_ref, segr_ref,
    stream_ref, first_ref, qkv_ref, attn_ref, lse_ref, keep_ref, send_ref, total_ref, wide_ref,
):
    def act(rows, fresh):
        values = base_ref[rows, :].astype(F32) + fresh
        stream_ref[rows, :] = values
        first_ref[rows, :] = norm_rows(values, par_ref, route_ref[rows, :] == 1)

    each_block(head_ref[0], mine_ref, other_ref, act)
    attend_math(first_ref, w_ref, segc_ref, segr_ref, qkv_ref, attn_ref, lse_ref)
    join_lanes(wo_ref, layer, wide_ref)
    total_ref[...] = tn(attn_ref[...], wide_ref[...])
    split_out(head_ref[0], total_ref, keep_ref, send_ref)


def split_sides(dp_ref, bit, grads_ref, send_ref, keep_ref):
    side = (dp_ref[0] >> bit) & 1
    rows = send_ref.shape[-2]
    for out_ref, flip in ((send_ref, 1), (keep_ref, 0)):
        for place in range(out_ref.shape[0]):
            low = place % (1 << bit)
            block = ((place - low) << 1) + low + ((side ^ flip) << bit)
            at = pl.ds(pl.multiple_of(block * rows, 16), rows)
            if len(out_ref.shape) == 3:
                out_ref[place] = grads_ref[at, :]
            else:
                for member in range(out_ref.shape[1]):
                    out_ref[place, member] = grads_ref[member, at, :]


def attend_back_kernel(
    layer, head_ref, grad_ref, mine_ref, other_ref, base_ref, par_ref, route_ref,
    qkv_ref, lse_ref, w_ref, wo_ref, segc_ref, segr_ref,
    fresh_ref, terms_ref, m_ref, gqkv_ref, keep_ref, send_ref, total_ref, turned_ref, wide_ref,
):
    terms_ref[...] = jnp.zeros_like(terms_ref)

    def act(rows, incoming):
        fresh = norm_back_rows(
            grad_ref[rows, :].astype(F32), incoming, base_ref[rows, :].astype(F32),
            par_ref, route_ref[rows, :] == 1, terms_ref,
        )
        fresh_ref[rows, :] = fresh
        m_ref[rows, :] = fresh.astype(BF)

    each_block(head_ref[0], mine_ref, other_ref, act)
    join_lanes(wo_ref, layer, wide_ref)
    heads = wide_ref.shape[0] // HD
    grad_attn = nt(wide_ref[...], m_ref[...]).astype(BF)
    qkv = qkv_ref[...]
    turned = qkv.T
    same = segc_ref[...] == segr_ref[...]
    for j in range(heads):
        at_q, at_k, at_v = (HD * (j + heads * part) for part in range(3))
        scores = nn(qkv[:, at_k : at_k + HD], turned[at_q : at_q + HD]) * scale
        prob = jnp.exp(jnp.where(same, scores, far_below) - lse_ref[j : j + 1, :])
        g_out = grad_attn[HD * j : HD * (j + 1)]
        g_prob = nn(qkv[:, at_v : at_v + HD], g_out)
        inner = jnp.sum(prob * g_prob, axis=0, keepdims=True)
        g_scores = (prob * (g_prob - inner)).astype(BF)
        g_q = nn(turned[at_k : at_k + HD], g_scores) * scale
        g_k = nt(turned[at_q : at_q + HD], g_scores) * scale
        g_v = nt(g_out, prob.astype(BF))
        turned_ref[at_q : at_q + HD, :] = g_q.astype(BF)
        turned_ref[at_k : at_k + HD, :] = g_k.astype(BF)
        turned_ref[at_v : at_v + HD, :] = g_v.astype(BF)
    used = 3 * heads * HD
    turned_ref[used:, :] = jnp.zeros((turned_ref.shape[0] - used, turned_ref.shape[1]), BF)
    g_qkv = turned_ref[...].T
    gqkv_ref[...] = g_qkv
    total_ref[...] = nt(g_qkv, w_ref[:, : g_qkv.shape[1]])
    split_out(head_ref[0], total_ref, keep_ref, send_ref)


def attend_grads_kernel(
    head_ref, dp_ref, first_ref, gqkv_ref, attn_ref, m_ref, after_ref, *rest
):
    zero_ref, *gw_refs, grads_ref = rest
    zero_ref[0, 0] = 0.0
    into_ref = gw_refs[0] if len(gw_refs) == 1 else grads_ref
    cols = into_ref.shape[1] // 4
    grads = tn(first_ref[...], gqkv_ref[...]).astype(BF)
    into_ref[:, : 3 * cols] = grads[:, : 3 * cols]
    for j in range(4):

        @pl.when(head_ref[0] == j)
        def _():
            into_ref[:, 3 * cols :] = nn(
                attn_ref[0], m_ref[:, j * cols : (j + 1) * cols]
            ).astype(BF)

    if len(gw_refs) > 1:
        split_sides(dp_ref, 0, grads_ref, *gw_refs)


def add_up(term, total_ref):
    step = pl.program_id(0)

    @pl.when(step == 0)
    def _():
        total_ref[...] = term

    @pl.when(step > 0)
    def _():
        total_ref[...] += term


def feed_kernel(
    head_ref, base_ref, mine_ref, other_ref, par_ref, route_ref, wu0_ref, wu1_ref, wd0_ref, wd1_ref,
    middle_ref, x_ref, act_ref, slope_ref, keep_ref, send_ref, total_ref,
):
    step = pl.program_id(0)

    @pl.when(step == 0)
    def _():
        def act(rows, fresh):
            values = base_ref[rows, :].astype(F32) + fresh
            middle_ref[rows, :] = values
            x_ref[rows, :] = norm_rows(values, par_ref, route_ref[rows, :] == 1)

        each_block(head_ref[0], mine_ref, other_ref, act)

    second = route_ref[...] == 1
    x = x_ref[...]
    up = jnp.where(second, nn(x, wu1_ref[...]), nn(x, wu0_ref[...]))
    phi = 0.5 * (1.0 + lax.erf(up * 0.7071067811865476))
    active = (up * phi).astype(BF)
    act_ref[...] = active
    slope_ref[...] = (phi + up * jnp.exp(-0.5 * up * up) * 0.3989422804014327).astype(BF)
    zero = jnp.zeros_like(active)
    term = nn(jnp.where(second, zero, active), wd0_ref[...])
    term += nn(jnp.where(second, active, zero), wd1_ref[...])
    add_up(term, total_ref)

    @pl.when(step == pl.num_programs(0) - 1)
    def _():
        split_out(head_ref[0], total_ref, keep_ref, send_ref)


def feed_back_math(
    head_ref, g_ref, slope_ref, wu0_ref, wu1_ref, wd0_ref, wd1_ref, route_ref,
    gup_ref, keep_ref, send_ref, total_ref,
):
    second = route_ref[...] == 1
    g_b = g_ref[...]
    g_up = jnp.where(second, nt(g_b, wd1_ref[...]), nt(g_b, wd0_ref[...]))
    g_up = (g_up * slope_ref[...].astype(F32)).astype(BF)
    gup_ref[...] = g_up
    zero = jnp.zeros_like(g_up)
    term = nt(jnp.where(second, zero, g_up), wu0_ref[...])
    term += nt(jnp.where(second, g_up, zero), wu1_ref[...])
    add_up(term, total_ref)

    @pl.when(pl.program_id(0) == pl.num_programs(0) - 1)
    def _():
        split_out(head_ref[0], total_ref, keep_ref, send_ref)


def feed_back_first_kernel(
    head_ref, g_ref, slope_ref, wu0_ref, wu1_ref, wd0_ref, wd1_ref, route_ref,
    gup_ref, keep_ref, send_ref, total_ref,
):
    feed_back_math(
        head_ref, g_ref, slope_ref, wu0_ref, wu1_ref, wd0_ref, wd1_ref, route_ref,
        gup_ref, keep_ref, send_ref, total_ref,
    )


def feed_back_kernel(
    head_ref, grad_ref, mine_ref, other_ref, base_ref, par_ref,
    slope_ref, wu0_ref, wu1_ref, wd0_ref, wd1_ref, route_ref,
    fresh_ref, terms_ref, g_ref, gup_ref, keep_ref, send_ref, total_ref,
):
    @pl.when(pl.program_id(0) == 0)
    def _():
        terms_ref[...] = jnp.zeros_like(terms_ref)

        def act(rows, incoming):
            fresh = norm_back_rows(
                grad_ref[rows, :], incoming, base_ref[rows, :],
                par_ref, route_ref[rows, :] == 1, terms_ref,
            )
            fresh_ref[rows, :] = fresh
            g_ref[rows, :] = fresh.astype(BF)

        each_block(head_ref[0], mine_ref, other_ref, act)

    feed_back_math(
        head_ref, g_ref, slope_ref, wu0_ref, wu1_ref, wd0_ref, wd1_ref, route_ref,
        gup_ref, keep_ref, send_ref, total_ref,
    )


def feed_grads_kernel(
    carried, dp_ref, g_ref, x_ref, act_ref, gup_ref, route_ref, after_ref, attn_ref, *rest
):
    above, (zero_ref, *outs, turned_ref, grads_ref) = rest[:carried], rest[carried:]
    zero_ref[0, 0] = 0.0
    step = pl.program_id(0)
    cols = act_ref.shape[1]
    second = route_ref[...] == 1

    @pl.when(step == 0)
    def _():
        turned_ref[...] = x_ref[...].T

    into_ref = outs[0] if len(outs) == 1 else grads_ref
    active = act_ref[...]
    g_up = gup_ref[...]
    zero = jnp.zeros_like(g_up)
    here = pl.ds(pl.multiple_of(step * cols, cols), cols)
    for expert in range(2):
        mine = second if expert else jnp.logical_not(second)
        into_ref[expert, :, here] = nn(turned_ref[...], jnp.where(mine, g_up, zero)).astype(BF)
        into_ref[2 + expert, here, :] = tn(jnp.where(mine, active, zero), g_ref[...]).astype(BF)

    @pl.when(step == pl.num_programs(0) - 1)
    def _():
        if len(outs) > 1:
            split_sides(dp_ref, 0, grads_ref.at[:2], outs[0].at[:, :2], outs[1].at[:, :2])
            for from_ref, to_ref in zip(above, outs):
                to_ref[:, 2] = from_ref[...]
            split_sides(dp_ref, 1, grads_ref.at[2:], outs[2], outs[3])


def last_add_kernel(head_ref, middle_ref, own_ref, recv_ref, out_ref):
    rows = out_ref.shape[0]
    at = pl.multiple_of(head_ref[0] * rows, rows)
    out_ref[...] = middle_ref[pl.ds(at, rows), :] + own_ref[...] + recv_ref[...].astype(F32)


def last_norm_kernel(head_ref, grad_ref, own_ref, recv_ref, tok_ref, par_ref, route_ref, *refs):
    out_ref, terms_ref = refs[-2:]
    terms_ref[...] = jnp.zeros_like(terms_ref)
    rows = out_ref.shape[0]
    at = pl.multiple_of(head_ref[0] * rows, rows)
    out_ref[...] = norm_back_rows(
        grad_ref[pl.ds(at, rows), :], own_ref[...] + recv_ref[...].astype(F32),
        tok_ref[...].astype(F32), par_ref, route_ref[...] == 1, terms_ref,
    )


def add_split_kernel(count, bit, dp_ref, *refs):
    inputs, (send_ref, keep_ref) = refs[:count], refs[-2:]
    side = (dp_ref[0] >> bit) & 1
    for out_ref, flip in ((send_ref, 1), (keep_ref, 0)):
        for place in range(out_ref.shape[0]):
            at = 2 * place + (side ^ flip)
            lane = 0
            for one_ref, two_ref in zip(inputs[::2], inputs[1::2]):
                cols = one_ref.shape[-1]
                total = (one_ref[at].astype(F32) + two_ref[at].astype(F32)).astype(BF)
                out_ref[place, ..., lane : lane + cols] = total
                lane += cols


def add_last_kernel(count, *refs):
    inputs, out_ref = refs[:count], refs[-1]
    lane = 0
    for one_ref, two_ref in zip(inputs[::2], inputs[1::2]):
        cols = one_ref.shape[-1]
        total = (one_ref[0].astype(F32) + two_ref[0].astype(F32)).astype(BF)
        out_ref[..., lane : lane + cols] = total
        lane += cols


def add_each_kernel(count, *refs):
    for group in range(count):
        one_ref, two_ref = refs[2 * group : 2 * group + 2]
        total = one_ref[0].astype(F32) + two_ref[0].astype(F32)
        refs[group - count][...] = total.astype(BF)


def tie_kernel(array_ref, after_ref, out_ref):
    pass


def pack_kernel(head_ref, up_ref, down_ref, *refs):
    out_ref, tall_ref = refs[-2:]
    width = down_ref.shape[3]
    count = 4
    hidden = up_ref.shape[3] // count
    sub = down_ref.shape[2] // count
    for j in range(count):

        @pl.when(head_ref[0] == j)
        def _():
            for expert in range(2):
                to = (2 + expert) * hidden
                out_ref[:, to : to + width] = down_ref[0, expert, j * sub : (j + 1) * sub, :]
                for block in range(hidden // sub):
                    at = block * sub * count + j * sub
                    to = expert * hidden + block * sub
                    out_ref[:, to : to + sub] = up_ref[0, expert, :, at : at + sub]
            if out_ref.shape[1] > 4 * hidden:
                qkv_ref, wo_ref, small_ref = refs[:3]
                cols = width // count
                for layer in range(qkv_ref.shape[0]):
                    to = 4 * hidden + layer * PACKED
                    for part in range(3):
                        at = part * width + j * cols
                        out_ref[:, to : to + cols] = qkv_ref[layer, :, at : at + cols]
                        to += cols
                    out_ref[:, to : to + cols] = wo_ref[layer, :, j * cols : (j + 1) * cols]
                tall_ref[...] = jnp.zeros_like(tall_ref)
                tall_ref[: small_ref.shape[0], : small_ref.shape[1]] = small_ref[...].astype(F32)
                out_ref[:, 4 * hidden + qkv_ref.shape[0] * PACKED :] = tall_ref[...].T[
                    : out_ref.shape[0]
                ].astype(BF)


def gather_refs(head_ref, arrays, blocks_ref):
    for s in range(4):
        blocks_ref[head_ref[0] ^ s] = arrays[s][...]


def unpack_up(blocks_ref, gu_ref):
    sub = blocks_ref.shape[2]
    for h in range(4):
        for expert in range(2):
            for block in range(gu_ref.shape[3] // (4 * sub)):
                at = block * 4 * sub + h * sub
                gu_ref[0, expert, :, at : at + sub] = blocks_ref[
                    h, expert, :, block * sub : (block + 1) * sub
                ].astype(F32)


def unpack_down(blocks_ref, first, gd_ref):
    sub = blocks_ref.shape[2]
    for h in range(4):
        for expert in range(2):
            gd_ref[0, expert, h * sub : (h + 1) * sub, :] = blocks_ref[h, first + expert].astype(F32)


def unpack_qkv(block_of, gq_ref, go_ref):
    cols = go_ref.shape[2] // 4
    for h in range(4):
        for part in range(3):
            to = part * 4 * cols + h * cols
            gq_ref[0, :, to : to + cols] = block_of(h, part * cols, cols).astype(F32)
        go_ref[0, :, h * cols : (h + 1) * cols] = block_of(h, 3 * cols, cols).astype(F32)


def unpack_later_kernel(head_ref, ffn_ref, gu_ref, gd_ref):
    unpack_up(ffn_ref, gu_ref)
    unpack_down(ffn_ref, 2, gd_ref)


def unpack_up_kernel(head_ref, *refs):
    gu_ref, gq_ref, go_ref, blocks_ref = refs[-4:]
    gather_refs(head_ref, refs[:4], blocks_ref)
    unpack_up(blocks_ref, gu_ref)
    unpack_qkv(lambda h, at, cols: blocks_ref[h, 2, :, at : at + cols], gq_ref, go_ref)


def unpack_down_kernel(head_ref, blocks_ref, *refs):
    unpack_down(blocks_ref, 0, refs[-1])


def unpack_attn_kernel(head_ref, *refs):
    gq_ref, go_ref, gain_ref, bias_ref, blocks_ref = refs[-5:]
    gather_refs(head_ref, refs[:4], blocks_ref)
    unpack_qkv(lambda h, at, cols: blocks_ref[h, :, 128 + at : 128 + at + cols], gq_ref, go_ref)
    terms = blocks_ref[0, :, :128].astype(F32)
    for h in range(1, 4):
        terms += blocks_ref[h, :, :128].astype(F32)
    turned = terms.T
    for layer in range(2):
        for place in range(2):
            at = 8 * layer + 4 * place
            gain_ref[layer, place] = turned[at : at + 2]
            bias_ref[layer, place] = turned[at + 2 : at + 4]


def swap(array, axis, bits):
    count = lax.axis_size(axis)
    return lax.ppermute(array, axis, [(i, i ^ bits) for i in range(count)])


def half_sum(keep, send):
    return (keep + swap(send, "head", 1).astype(F32)).astype(BF)


def other_half(half, zero=None):
    recv = swap(half, "head", 2).astype(F32)
    if zero is not None:
        recv = recv + zero.reshape(())
    mine = (half.astype(F32) + recv).astype(BF)
    return mine, swap(mine, "head", 1)


def head_sum(keep, send):
    return other_half(half_sum(keep, send))


def own_sum(half, head_at):
    pair = head_at // 2
    recv = swap(lax.dynamic_index_in_dim(half, 1 - pair, 0, keepdims=False).astype(BF), "head", 2)
    return lax.dynamic_index_in_dim(half, pair, 0, keepdims=False), recv


def spread(array, axis):
    copies = jnp.broadcast_to(array[None], (lax.axis_size(axis),) + array.shape)
    return lax.all_to_all(copies, axis, 0, 0, tiled=True)


def head_pieces(shard):
    across = swap(shard, "head", 2)
    return [shard, swap(shard, "head", 1), across, swap(across, "head", 1)]


def by_pairs(grads, dp_at, dp_count):
    sides = grads.reshape(dp_count // 2, 2, -1, grads.shape[-1])
    side = dp_at % 2
    return (
        lax.dynamic_index_in_dim(sides, 1 - side, 1, keepdims=False),
        lax.dynamic_index_in_dim(sides, side, 1, keepdims=False),
    )


def add_split(dp_index, lists, bit, after):
    flat = [array for pair in lists for array in pair]
    lanes = sum(keep.shape[-1] for keep, _ in lists)
    dims = (flat[0].shape[0] // 2,) + flat[0].shape[1:-1] + (lanes,)
    vmem = pl.BlockSpec(memory_space=pltpu.VMEM)
    send, keep = call(
        lambda *refs: add_split_kernel(len(flat), bit, *refs), (shape(*dims),) * 2, "add_split",
        in_specs=[smem()] + [vmem] * len(flat) + [pl.BlockSpec(memory_space=pl.ANY)] * len(after),
    )(dp_index, *flat, *after)
    return [(keep, swap(send, "dp", 1 << bit))]


def add_last(lists, after=()):
    flat = [array for pair in lists for array in pair]
    lanes = sum(keep.shape[-1] for keep, _ in lists)
    vmem = pl.BlockSpec(memory_space=pltpu.VMEM)
    return call(
        lambda *refs: add_last_kernel(len(flat), *refs),
        shape(*flat[0].shape[1:-1], lanes), "add_last",
        in_specs=[vmem] * len(flat) + [pl.BlockSpec(memory_space=pl.ANY)] * len(after),
    )(*flat, *after)


def add_each(groups, after):
    flat = [array for pair in groups for array in pair]
    vmem = pl.BlockSpec(memory_space=pltpu.VMEM)
    return call(
        lambda *refs: add_each_kernel(len(groups), *refs),
        [shape(*keep.shape[1:]) for keep, _ in groups], "add_each",
        in_specs=[vmem] * len(flat) + [pl.BlockSpec(memory_space=pl.ANY)] * len(after),
    )(*flat, *after)


def tie(array, after):
    return call(
        tie_kernel, shape(*array.shape), "tie",
        in_specs=[pl.BlockSpec(memory_space=pl.ANY)] * 2,
        out_specs=pl.BlockSpec(memory_space=pl.ANY),
        input_output_aliases={0: 0},
    )(array, after)


def body(tokens, segments, routes, norm_gain, norm_bias, w_qkv, w_out, w_up, w_down, cotangent):
    dp_count = lax.axis_size("dp")
    head_count = lax.axis_size("head")
    head_at = lax.axis_index("head")
    dp_at = lax.axis_index("dp")
    head = head_at.reshape(1)
    dp_index = dp_at.reshape(1)
    tok_count, width = tokens.shape
    row_len = segments.shape[1]
    layers = norm_gain.shape[0]
    head_cols = H // head_count * HD
    hidden_all = w_up.shape[3]
    hidden = hidden_all // head_count
    rows = w_qkv.shape[1]
    down_rows = w_down.shape[2]
    sub = down_rows // head_count
    steps = hidden // COLS
    aligned = rows % 16 == 0 and dp_count == 8 and head_count == 4 and layers == 2

    small = jnp.stack([norm_gain, norm_bias], axis=2).reshape(layers * 8, rows)

    seg_col = segments.reshape(row_len, 1)
    seg_row = segments.reshape(1, row_len)
    route_lanes = jnp.pad(routes.astype(BF), ((0, 0), (0, 127)))
    both = spread(jnp.concatenate([tokens, cotangent, route_lanes], axis=1), "head")
    both = both.reshape(row_len, 2 * width + 128)
    row_tokens = both[:, :width]
    row_cotangent = both[:, width : 2 * width]
    row_routes = both[:, 2 * width : 2 * width + 1].astype(jnp.int32)

    packs = []
    for layer in range(layers):
        extra = (w_qkv, w_out, small) if layer == 0 else ()
        first = (row_tokens, row_cotangent, row_routes) if layer else ()
        lanes = 4 * width + (0 if layer else layers * PACKED + 128)
        if aligned:
            packs.append(
                call(
                    pack_kernel,
                    shape(rows, lanes),
                    "pack",
                    grid=(1,),
                    in_specs=[
                        smem(),
                        pl.BlockSpec(
                            (1, 2, rows, hidden_all), lambda i, layer=layer: (layer, 0, 0, 0)
                        ),
                        pl.BlockSpec(
                            (1, 2, down_rows, width), lambda i, layer=layer: (layer, 0, 0, 0)
                        ),
                    ]
                    + [whole(*array.shape) for array in extra]
                    + [pl.BlockSpec(memory_space=pl.ANY)] * len(first),
                    out_specs=whole(rows, lanes),
                    scratch_shapes=[pltpu.VMEM((128, 128), F32)],
                )(head, w_up, w_down, *extra, *first)
            )
        else:
            taken = lax.dynamic_index_in_dim(
                w_up[layer].reshape(2, rows, dp_count, head_count, sub), head_at, 3, keepdims=False
            ).reshape(2, rows, hidden)
            down = lax.dynamic_index_in_dim(
                w_down[layer].reshape(2, head_count, sub, width), head_at, 1, keepdims=False
            )
            parts = [taken[0], taken[1], down[0], down[1]]
            for at in range(layers if layer == 0 else 0):
                taken = lax.dynamic_index_in_dim(
                    w_qkv[at].reshape(rows, 3, head_count, head_cols), head_at, 2, keepdims=False
                )
                out = lax.dynamic_index_in_dim(
                    w_out[at].reshape(rows, head_count, head_cols), head_at, 1, keepdims=False
                )
                parts += [taken.reshape(rows, 3 * head_cols), out]
            if layer == 0:
                parts.append(jnp.pad(small.T, ((0, 0), (0, 128 - layers * 8))))
            packs.append(jnp.concatenate(parts, axis=1))
    gathered = [lax.all_gather(pack, "dp", axis=0, tiled=True) for pack in packs]
    taken = [
        gathered[0][:, at : at + head_cols]
        for at in (4 * width + layer * PACKED + 3 * head_cols for layer in range(layers))
    ]
    out_w = lax.all_to_all(
        jnp.concatenate(taken, axis=1).reshape(head_count, head_cols, layers * head_cols),
        "head", 0, 0, tiled=True,
    )

    pairs = head_count // 2
    flat = (row_len, width)
    halves = (pairs, tok_count, width)
    both_halves = (shape(*halves, dtype=F32), shape(*halves))
    half_specs = [whole(*halves), whole(*halves)]
    per_expert = width // COLS
    weight_specs = [
        pl.BlockSpec((width, COLS), lambda i: (0, i)),
        pl.BlockSpec((width, COLS), lambda i: (0, per_expert + i)),
        pl.BlockSpec((COLS, width), lambda i: (i, 2)),
        pl.BlockSpec((COLS, width), lambda i: (i, 3)),
    ]
    act_spec = pl.BlockSpec((row_len, COLS), lambda i: (0, i))
    total = pltpu.VMEM(flat, F32)
    vmem = pl.BlockSpec(memory_space=pltpu.VMEM)

    def attn_spec(layer):
        return pl.BlockSpec((width, PACKED), lambda i: (0, 4 * width // PACKED + layer))

    small_spec = pl.BlockSpec((width, 128), lambda i: (0, 4 * width // 128 + layers * PACKED // 128))
    out_spec = whole(head_count, head_cols, layers * head_cols)
    seg_specs = [whole(row_len, 1), whole(1, row_len)]
    wide = pltpu.VMEM((head_cols, width), BF)

    saved = []
    for layer in range(layers):
        kept = (
            shape(*flat), shape(row_len, KEPT), shape(head_cols, row_len),
            shape(8, row_len, dtype=F32),
        )
        kept_specs = [whole(*array.shape) for array in kept]
        if layer == 0:
            stream = row_tokens
            pars, first, qkv, attn, lse = call(
                attend_first_kernel, (shape(layers * 8, width, dtype=F32),) + kept, "attend_first",
                grid=(1,),
                in_specs=[whole(*flat), small_spec, whole(row_len, 1), attn_spec(0)] + seg_specs,
                out_specs=[whole(layers * 8, width)] + kept_specs,
            )(stream, gathered[0], row_routes, gathered[0], seg_col, seg_row)
            pars = pars.reshape(layers, 2, 4, width)
            keep, send = call(
                project_kernel, both_halves, "project",
                in_specs=[smem()] + [vmem] * 2,
                scratch_shapes=[total, wide],
            )(head, attn, out_w)
        else:
            stream, first, qkv, attn, lse, keep, send = call(
                lambda *refs, layer=layer: attend_kernel(layer, *refs),
                (shape(*flat, dtype=F32),) + kept + both_halves,
                "attend",
                grid=(1,),
                in_specs=[smem(), whole(*flat)] + half_specs
                + [whole(4, width), whole(row_len, 1), attn_spec(layer), out_spec] + seg_specs,
                out_specs=[whole(*flat)] + kept_specs + half_specs,
                scratch_shapes=[total, wide],
            )(
                head, middle, mine, other, pars[layer, 0], row_routes, gathered[0], out_w,
                seg_col, seg_row,
            )
        mine, other = head_sum(keep, send)
        middle, second, active, slope, keep, send = call(
            feed_kernel,
            (shape(*flat, dtype=F32), shape(*flat), shape(row_len, hidden), shape(row_len, hidden))
            + both_halves,
            "feed",
            grid=(steps,),
            in_specs=[smem(), whole(*flat)] + half_specs
            + [whole(4, width), whole(row_len, 1)] + weight_specs,
            out_specs=[whole(*flat), whole(*flat), act_spec, act_spec] + half_specs,
            scratch_shapes=[total],
        )(head, stream, mine, other, pars[layer, 1], row_routes, *[gathered[layer]] * 4)
        saved.append((stream, first, qkv, attn, lse, middle, second, active, slope))
        if layer + 1 < layers:
            mine, other = head_sum(keep, send)
    half = keep + swap(send, "head", 1).astype(F32)
    attn_all = lax.all_gather(
        jnp.stack([entry[3] for entry in saved]), "head", axis=1, tiled=True
    )
    own, recv = own_sum(half, head_at)
    output = call(
        last_add_kernel, shape(tok_count, width, dtype=F32), "last_add",
        in_specs=[smem()] + [vmem] * 3,
    )(head, middle, own, recv)

    term_list = [None] * (2 * layers)
    ffn_shards = [None] * layers
    attn_grads = [None] * layers
    markers = {}
    fresh_terms = (shape(*flat, dtype=F32), shape(8, width, dtype=F32))
    whole_grads = (4, width, hidden)
    chunk = (dp_count // 2, 2, rows, width)
    narrow = (dp_count // 2, rows, width)
    gradient = row_cotangent
    for layer in reversed(range(layers)):
        stream, first, qkv, attn, lse, middle, second, active, slope = saved[layer]
        operands = (slope,) + (gathered[layer],) * 4 + (row_routes,)
        operand_specs = [act_spec] + weight_specs + [whole(row_len, 1)]
        if layer == layers - 1:
            grad_b = gradient
            g_up, keep, send = call(
                feed_back_first_kernel, (shape(row_len, hidden),) + both_halves,
                "feed_back_first",
                grid=(steps,),
                in_specs=[smem(), whole(*flat)] + operand_specs,
                out_specs=[act_spec] + half_specs,
                scratch_shapes=[total],
            )(head, gradient, *operands)
        else:
            gradient, terms, grad_b, g_up, keep, send = call(
                feed_back_kernel,
                fresh_terms + (shape(*flat), shape(row_len, hidden)) + both_halves,
                "feed_back",
                grid=(steps,),
                in_specs=[smem(), whole(*flat)] + half_specs
                + [whole(*flat), whole(4, width)] + operand_specs,
                out_specs=[whole(*flat), whole(8, width), whole(*flat), act_spec] + half_specs,
                scratch_shapes=[total],
            )(
                head, gradient, mine, other, saved[layer + 1][0], pars[layer + 1, 0], *operands,
            )
            term_list[2 * layer + 2] = terms[:4] / head_count
        half = half_sum(keep, send)
        by_chunk = aligned and layer == 0
        more = (dp_count // 2, 3, rows, width)
        outs = [more] * 2 + [chunk] * 2 if by_chunk else [whole_grads]
        above = tuple(attn_grads[layer + 1]) if by_chunk else ()
        zero, *ffn_grads = call(
            lambda *refs, count=len(above): feed_grads_kernel(count, *refs),
            (shape(1, 1, dtype=F32),) + tuple(shape(*dims) for dims in outs), "feed_grads",
            grid=(steps,),
            in_specs=[smem(), whole(*flat), whole(*flat), act_spec, act_spec, whole(row_len, 1)]
            + [pl.BlockSpec(memory_space=pl.ANY)] * 2
            + [whole(*array.shape) for array in above],
            out_specs=[smem()] + [whole(*dims) for dims in outs],
            scratch_shapes=[
                pltpu.VMEM((width, row_len), BF),
                pltpu.VMEM(whole_grads if by_chunk else (8, 128), BF),
            ],
        )(dp_index, grad_b, second, active, g_up, row_routes, half, attn_all, *above)
        mine, other = other_half(half, zero)
        if by_chunk:
            up_send, up_keep, down_send, down_keep = ffn_grads
            up_list = [(up_keep, swap(up_send, "dp", 1))]
            down_list = [(down_keep, swap(down_send, "dp", 2))]
        else:
            ffn_shards[layer] = lax.psum_scatter(
                tie(ffn_grads[0], mine), "dp", scatter_dimension=1, tiled=True
            )
        gradient, terms, m_b, g_qkv, keep, send = call(
            lambda *refs, layer=layer: attend_back_kernel(layer, *refs),
            fresh_terms + (shape(*flat), shape(row_len, KEPT)) + both_halves,
            "attend_back",
            grid=(1,),
            in_specs=[smem(), whole(*flat)] + half_specs
            + [whole(*flat), whole(4, width), whole(row_len, 1)]
            + [whole(row_len, KEPT), whole(8, row_len), attn_spec(layer), out_spec] + seg_specs,
            out_specs=[whole(*flat), whole(8, width), whole(*flat), whole(row_len, KEPT)]
            + half_specs,
            scratch_shapes=[total, pltpu.VMEM((KEPT, row_len), BF), wide],
        )(
            head, gradient, mine, other, middle, pars[layer, 1], row_routes,
            qkv, lse, gathered[0], out_w, seg_col, seg_row,
        )
        term_list[2 * layer + 1] = terms[:4] / head_count
        markers["attend", layer] = keep
        if layer:
            half = half_sum(keep, send)
        else:
            half = keep + swap(send, "head", 1).astype(F32)
        outs = [narrow] * 2 if aligned else [(width, width)]
        zero, *qkv_grads = call(
            attend_grads_kernel,
            (shape(1, 1, dtype=F32),) + tuple(shape(*dims) for dims in outs),
            "attend_grads",
            grid=(1,),
            in_specs=[
                smem(), smem(), whole(*flat), whole(row_len, KEPT),
                pl.BlockSpec((1, width, row_len), lambda i, layer=layer: (layer, 0, 0)),
                whole(*flat), pl.BlockSpec(memory_space=pl.ANY),
            ],
            out_specs=[smem()] + [whole(*dims) for dims in outs],
            scratch_shapes=[pltpu.VMEM((width, width), BF)],
        )(head, dp_index, first, g_qkv, attn_all, m_b, half)
        if layer:
            mine, other = other_half(half, zero)
        attn_grads[layer] = qkv_grads
    first_out = ()
    if aligned:
        first_out = (attn_grads[0][0], output)
    own, recv = own_sum(half, head_at)
    grad_input, terms = call(
        last_norm_kernel,
        (shape(tok_count, width, dtype=F32), shape(8, width, dtype=F32)),
        "last_norm",
        in_specs=[smem()] + [vmem] * 6 + [pl.BlockSpec(memory_space=pl.ANY)] * len(first_out),
    )(head, gradient, own, recv, tokens, pars[0, 0], routes, *first_out)
    term_list[0] = terms[:4]
    if aligned:
        up_list = add_split(dp_index, up_list, 1, (grad_input,))
        down_list = add_split(dp_index, down_list, 0, (up_list[0][0],))

    terms = jnp.concatenate(term_list, axis=0)
    if not aligned:
        terms = terms.reshape(8 * layers, dp_count, rows)
        terms = lax.all_to_all(jnp.transpose(terms, (1, 0, 2)), "dp", 0, 0, tiled=True)
        terms = lax.psum(jnp.sum(terms, axis=0), "head").reshape(layers, 2, 2, 2, rows)
        grad_gain, grad_bias = terms[:, :, 0], terms[:, :, 1]

    if aligned:
        dims = (
            (layers, rows, 3 * width), (layers, rows, width),
            (layers, 2, rows, hidden_all), (layers, 2, down_rows, width),
        )

        def slot(dims, layer):
            return pl.BlockSpec((1,) + dims[1:], lambda i: (layer,) + (0,) * (len(dims) - 1))

        def unpack(kernel, pieces, old, outs, specs, name, scratch=()):
            return call(
                kernel, [shape(*out, dtype=F32) for out in outs], name,
                grid=(1,),
                in_specs=[smem()] + [whole(*piece.shape) for piece in pieces]
                + [pl.BlockSpec(memory_space=pl.ANY)] * len(old),
                out_specs=specs,
                scratch_shapes=[pltpu.VMEM((4,) + array, BF) for array in scratch],
                input_output_aliases={1 + len(pieces) + at: at for at in range(len(old))},
            )(head, *pieces, *old)

        ffn1 = tie(ffn_shards[1], down_list[0][0])
        up_list = add_split(dp_index, up_list, 2, (ffn1,))
        down_list = add_split(dp_index, down_list, 2, (up_list[0][0],))
        term_lanes = jnp.pad(terms.T.astype(BF), ((0, 0), (0, 128 - terms.shape[0])))
        term_send, term_keep = by_pairs(term_lanes, dp_at, dp_count)
        qkv_send, qkv_keep = attn_grads[0]
        last = [(term_keep, swap(term_send, "dp", 1)), (qkv_keep, swap(qkv_send, "dp", 1))]
        last = add_split(dp_index, last, 1, (down_list[0][0],))
        ffn1 = lax.all_gather(ffn1, "head", axis=0)
        grad_up, grad_down = unpack(
            unpack_later_kernel, [ffn1], (),
            (dims[2], dims[3]), [slot(dims[2], 1), slot(dims[3], 1)], "unpack_later",
        )
        last = add_split(dp_index, last, 2, (grad_up,))
        up0, down0 = add_each([up_list[0], down_list[0]], (last[0][0],))
        down0 = lax.all_gather(down0, "head", axis=0)
        up0 = head_pieces(up0)
        last = head_pieces(add_last(last))
        grad_up, grad_qkv, grad_out = unpack(
            unpack_up_kernel, up0, (grad_up,),
            (dims[2], dims[0], dims[1]), [slot(dims[2], 0), slot(dims[0], 1), slot(dims[1], 1)],
            "unpack_up", [up0[0].shape],
        )
        (grad_down,) = unpack(
            unpack_down_kernel, [down0], (grad_down,), (dims[3],), [slot(dims[3], 0)],
            "unpack_down",
        )
        grad_qkv, grad_out, grad_gain, grad_bias = unpack(
            unpack_attn_kernel, last, (grad_qkv, grad_out),
            (dims[0], dims[1], (layers, 2, 2, rows), (layers, 2, 2, rows)),
            [slot(dims[0], 0), slot(dims[1], 0)] + [whole(layers, 2, 2, rows)] * 2,
            "unpack_attn", [last[0].shape],
        )
        weight_grads = (grad_qkv, grad_out, grad_up, grad_down)
    else:
        grad_qkv, grad_out, grad_up, grad_down = [], [], [], []
        for layer in range(layers):
            attn_shard = lax.psum_scatter(
                attn_grads[layer][0], "dp", scatter_dimension=0, tiled=True
            )
            ffn_all = lax.all_gather(ffn_shards[layer], "head", axis=0)
            attn_all = lax.all_gather(attn_shard, "head", axis=0)
            taken = attn_all[:, :, : 3 * head_cols].reshape(head_count, rows, 3, head_cols)
            grad_qkv.append(jnp.transpose(taken, (1, 2, 0, 3)).reshape(rows, 3 * width))
            taken = jnp.transpose(attn_all[:, :, 3 * head_cols :], (1, 0, 2))
            grad_out.append(taken.reshape(rows, width))
            taken = ffn_all[:, :2].reshape(head_count, 2, rows, dp_count, sub)
            taken = jnp.transpose(taken, (1, 2, 3, 0, 4))
            grad_up.append(taken.reshape(2, rows, hidden_all))
            taken = jnp.transpose(ffn_all[:, 2:], (1, 0, 2, 3))
            grad_down.append(taken.reshape(2, down_rows, width))
        weight_grads = tuple(
            jnp.stack(part).astype(F32) for part in (grad_qkv, grad_out, grad_up, grad_down)
        )
    return (output, grad_input, grad_gain, grad_bias) + weight_grads


def solution(mesh):
    tokens = P(("dp", "head"), None)
    by_dp = (
        P(None, None, None, "dp"),
        P(None, None, None, "dp"),
        P(None, "dp", None),
        P(None, "dp", None),
        P(None, None, "dp", None),
        P(None, None, "dp", None),
    )
    return jax.shard_map(
        body,
        mesh=mesh,
        in_specs=(tokens, P("dp", None), tokens) + by_dp + (tokens,),
        out_specs=(tokens, tokens) + by_dp,
        check_vma=False,
    )
```

time: 3020 us -> 462 us (0.15)
  waiting for transfers between devices: 2410 us -> 239 us
  blocking collectives: 228 us -> 25.6 us
  matrix products: 158 us -> 0 us
  Pallas kernels: 0 us -> 81.2 us
  local copies, waits for them, and re-layouts: 124 us -> 63.3 us
  other arithmetic: 57.2 us -> 9.18 us
    reduce_scatter x14 -> x1, waiting for transfers between devices: 1540 us -> 0.01 us  [body(): lax.psum_scatter(tie(ffn_grads[0], mine), 'dp', scatter_dimension=1, tile...]
    all_gather x12 -> x5, waiting for transfers between devices: 556 us -> 84.9 us  [the longest x2 84.9 us: body(): lax.all_gather(pack, 'dp', axis=0, tiled=True)]
    unnamed x38 -> x6, waiting for transfers between devices: 303 us -> 0.1 us
    all_gather x12 -> x0, blocking collectives: 176 us -> none  [the longest x2 66 us: body(): lax.all_gather(norm_gain[layer], 'dp', axis=2, tiled=True)]
    dot_general x44 -> x0, matrix products: 158 us -> none  [the longest x2 24.4 us: body(): jnp.einsum('esf,esd->efd', active, grad_buffer, preferred_element_type=jn...]
    ppermute x0 -> x38, waiting for transfers between devices: none -> 153 us  [swap(): return lax.ppermute(array, axis, [(i, i ^ bits) for i in range(count)])]
    pallas_call x0 -> x31, Pallas kernels: none -> 81.2 us  [the longest x2 14.7 us: body(): call(feed_kernel, (shape(*flat, dtype=F32), shape(*flat), shape(row_len,...]
    slice x10 -> x3, local copies, waits for them, and re-layouts: 45.7 us -> 1.69 us  [the longest x1 1.58 us: body(): gathered[0][:, at:at + head_cols]]
  transfers between devices with their start and end apart: 37 -> 45, of which waited for: 33 -> 28; matrix products, arithmetic and copies ran while one was open for 11% -> 3% of each run, Pallas kernels for 0% -> 17%
where the time goes in v1:
time: 462 us; the launch traced here: 457 us
  waiting for transfers between devices  239 us (52%)
  Pallas kernels  81.2 us (18%)
  local copies, waits for them, and re-layouts  63.3 us (14%)
  blocking collectives  25.6 us (6%)
  starting transfers between devices  24 us (5%)
  between operations  15.4 us (3%)
  other arithmetic  9.18 us (2%)
    ppermute x38, waiting for transfers between devices, swap(): return lax.ppermute(array, axis, [(i, i ^ bits) for i in range(count)])  153 us
    all_gather x2, waiting for transfers between devices, body(): lax.all_gather(pack, 'dp', axis=0, tiled=True)  84.9 us
    unnamed x203, local copies, waits for them, and re-layouts  59.1 us
    all_to_all x1, blocking collectives, spread(): return lax.all_to_all(copies, axis, 0, 0, tiled=True)  25.6 us
    ppermute x38, starting transfers between devices, swap(): return lax.ppermute(array, axis, [(i, i ^ bits) for i in range(count)])  19.5 us
    pallas_call x2, Pallas kernels, body(): call(feed_kernel, (shape(*flat, dtype=F32), shape(*flat), shape(row_len,...  14.7 us
    pallas_call x2, Pallas kernels, body(): call(lambda *refs, layer=layer: attend_back_kernel(layer, *refs), fresh_t...  12.4 us
    pallas_call x2, Pallas kernels, body(): call(lambda *refs, count=len(above): feed_grads_kernel(count, *refs), (sh...  10 us
  transfers between devices with their start and end apart: 45, of which 28 were waited for; matrix products, arithmetic and copies ran while one was open for 3% of the time, Pallas kernels for 17%

profile of v1, /device:TPU:0, one launch (start us, length us, event | category | flops | bytes accessed | tf_op | source)
XLA Modules:
  0.0 457.5 jit_solution(4817584513482834736)
XLA Ops:
  8.0 1.7 copy-done.14
  9.6 1.7 copy-done.16
  15.1 25.6 %all_to_all.10 = bf16[4,128,1664]{2,1,0:T(8,128)(2,1)S(1)} all-to-all(bf16[4,128,1664]{2,1,0:T(8,128)(2,1)S(1)} %broadcast_in_dim.2), channel_id=1, replica_groups=mesh['dp'=8,'head'=4] {'head'}, dimensions={0} | all-to-all | bytes 3407872 | tf_op jit(solution)/shard_map/all_to_all | solution.py:552
  40.9 1.8 copy-done.15
  43.8 84.9 %all-gather.8.cloned.1.call-done.small_ref.w_ref.wu0_ref.wu1_ref.wd0_ref.wd1_ref.refs_6_.refs_9_ = bf16[768,4736]{1,0:T(8,128)(2,1)} async-done(((bf16[96,4736]{1,0:T(8,128)(2,1)}), bf16[768,4736]{1,0:T(8,128)(2,1)}) %all-gather.8.cloned.1.call-update) | async-done | bytes 7274512 | tf_op jit(solution)/shard_map/all_gather | solution.py:687
  128.7 1.6 fusion.4
  131.3 3.5 all-to-all-start.1
  135.2 3.5 copy-done
  138.7 3.0 attend_first.1
  145.2 1.7 collective-permute-done
  148.2 10.0 %collective-permute-done.1 = bf16[2,128,768]{2,1,0:T(8,128)(2,1)S(1)} collective-permute-done((bf16[2,128,768]{2,1,0:T(8,128)(2,1)S(1)}, bf16[2,128,768]{2,1,0:T(8,128)(2,1)S(1)}, u32[]{:S(2)}, u32[]{:S(2)}) %collective-permute-start.1) | collective-permute-done | bytes 393248 | tf_op jit(solution)/shard_map/ppermute | solution.py:525
  159.0 1.4 slice_bitcast_fusion
  160.4 3.1 copy-done.1
  163.5 7.0 %feed.2 = (f32[512,768]{1,0:T(8,128)S(1)}, bf16[512,768]{1,0:T(8,128)(2,1)S(1)}, bf16[512,768]{1,0:T(8,128)(2,1)S(1)}, bf16[512,768]{1,0:T(8,128)(2,1)S(1)}, f32...) custom-call(s32[1]{0:T(128)} %bitcast.head_ref.refs_0_, ...), custom_call_target="tpu_custom_call" | custom-call | tf_op jit(solution)/shard_map/feed/pallas_call | solution.py:757
  172.7 1.3 collective-permute-done.3
  174.1 1.3 collective-permute-start.4
  175.4 10.2 %collective-permute-done.4 = bf16[2,128,768]{2,1,0:T(8,128)(2,1)S(1)} collective-permute-done((bf16[2,128,768]{2,1,0:T(8,128)(2,1)S(1)}, bf16[2,128,768]{2,1,0:T(8,128)(2,1)S(1)}, u32[]{:S(2)}, u32[]{:S(2)}) %collective-permute-start.4) | collective-permute-done | bytes 393248 | tf_op jit(solution)/shard_map/ppermute | solution.py:525
  185.8 1.7 collective-permute-done.5.refs_3_
  187.5 4.5 attend.1
  198.9 1.3 collective-permute-start.7
  200.1 10.0 %collective-permute-done.7 = bf16[2,128,768]{2,1,0:T(8,128)(2,1)S(1)} collective-permute-done((bf16[2,128,768]{2,1,0:T(8,128)(2,1)S(1)}, bf16[2,128,768]{2,1,0:T(8,128)(2,1)S(1)}, u32[]{:S(2)}, u32[]{:S(2)}) %collective-permute-start.7) | collective-permute-done | bytes 393248 | tf_op jit(solution)/shard_map/ppermute | solution.py:525
  210.3 1.8 collective-permute-done.8.other_ref
  212.1 2.3 copy-done.3
  214.5 7.7 %feed.3 = (f32[512,768]{1,0:T(8,128)S(1)}, bf16[512,768]{1,0:T(8,128)(2,1)S(1)}, bf16[512,768]{1,0:T(8,128)(2,1)S(1)}, bf16[512,768]{1,0:T(8,128)(2,1)S(1)}, f32...) custom-call(s32[1]{0:T(128)} %bitcast.head_ref.refs_0_, f32[512,768]{1,0:T(8,128)S(1)} %copy-done.22, ...), custom_call_target="tpu_custom_call" | custom-call | tf_op jit(solution)/shard_map/feed/pallas_call | solution.py:757
  225.1 5.0 %feed_back_first.1 = (bf16[512,768]{1,0:T(8,128)(2,1)S(1)}, f32[2,128,768]{2,1,0:T(8,128)S(1)}, bf16[2,128,768]{2,1,0:T(8,128)(2,1)S(1)}) custom-call(s32[1]{0:T(128)} %bitcast.head_ref.refs_0_, bf16[512,768]{1,0:T(8,128)(2,1)S(1)} %get-tuple-element.178.refs_1_.g_ref, bf16[512,768]{1,0:T(8,128)(2,1)S(1)} %get-tuple-element.105.slope_ref, ...), custom_call_target="tpu_custom_call" | custom-call | tf_op jit(solution)/shard_map/feed_back_first/pallas_call | solution.py:796
  230.3 1.6 collective-permute-done.11
  233.3 1.4 copy-done.4
  235.8 3.9 feed_grads.2
  239.7 3.6 collective-permute-done.12
  243.3 1.8 add_convert_fusion.4.refs_2_.after_ref
  245.8 2.4 copy-done.10
  248.6 1.9 collective-permute-done.13.refs_3_
  250.6 3.3 copy-done.2
  257.0 1.4 copy-done.27
  261.9 5.8 %attend_back.2 = (f32[512,768]{1,0:T(8,128)S(1)}, f32[8,768]{1,0:T(8,128)S(1)}, bf16[512,768]{1,0:T(8,128)(2,1)S(1)}, bf16[512,640]{1,0:T(8,128)(2,1)S(1)}, f32[...) custom-call(s32[1]{0:T(128)} %bitcast.head_ref.refs_0_, bf16[512,768]{1,0:T(8,128)(2,1)S(1)} %copy-done.8, ...), custom_call_target="tpu_custom_call" | custom-call | tf_op jit(solution)/shard_map/attend_back/pallas_call | solution.py:845
  267.8 1.7 collective-permute-done.14
  270.8 2.2 attend_grads.2
  273.0 7.8 %collective-permute-done.15 = bf16[2,128,768]{2,1,0:T(8,128)(2,1)S(1)} collective-permute-done((bf16[2,128,768]{2,1,0:T(8,128)(2,1)S(1)}, bf16[2,128,768]{2,1,0:T(8,128)(2,1)S(1)}, u32[]{:S(2)}, u32[]{:S(2)}) %collective-permute-start.15) | collective-permute-done | bytes 393248 | tf_op jit(solution)/shard_map/ppermute | solution.py:525
  281.7 1.7 collective-permute-done.16.other_ref
  283.5 6.8 %feed_back.1 = (f32[512,768]{1,0:T(8,128)S(1)}, f32[8,768]{1,0:T(8,128)S(1)}, bf16[512,768]{1,0:T(8,128)(2,1)S(1)}, bf16[512,768]{1,0:T(8,128)(2,1)S(1)}, f32[2,...) custom-call(s32[1]{0:T(128)} %bitcast.head_ref.refs_0_, f32[512,768]{1,0:T(8,128)S(1)} %get-tuple-element.115.grad_ref, ...), custom_call_target="tpu_custom_call" | custom-call | tf_op jit(solution)/shard_map/feed_back/pallas_call | solution.py:805
  290.5 1.6 collective-permute-done.17
  293.4 6.1 %feed_grads.3 = (f32[1,1]{1,0:T(1,128)}, bf16[4,3,96,768]{3,2,1,0:T(8,128)(2,1)}, bf16[4,3,96,768]{3,2,1,0:T(8,128)(2,1)S(1)}, bf16[4,2,96,768]{3,2,1,0:T(8,128)(2,1)}, bf16[4,2,96,768]{3,2,1,0:T(8,128)(2,1)S(1)}) custom-call(s32[1]{0:T(128)} %bitcast.12.refs_0_.dp_ref, bf16[512,768]{1,0:T(8,128)(2,1)S(1)} %get-tuple-element.126.refs_1_, ...), custom_call_target="tpu_custom_call" | custom-call | tf_op jit(solution)/shard_map/feed_grads/pallas_call | solution.py:823
  299.9 3.4 collective-permute-done.18
  306.0 6.6 %attend_back.3 = (f32[512,768]{1,0:T(8,128)S(1)}, f32[8,768]{1,0:T(8,128)S(1)}, bf16[512,768]{1,0:T(8,128)(2,1)S(1)}, bf16[512,640]{1,0:T(8,128)(2,1)S(1)}, f32[...) custom-call(s32[1]{0:T(128)} %bitcast.head_ref.refs_0_, f32[512,768]{1,0:T(8,128)S(1)} %get-tuple-element.123.refs_1_, ...), custom_call_target="tpu_custom_call" | custom-call | tf_op jit(solution)/shard_map/attend_back/pallas_call | solution.py:845
  318.1 1.3 convert_add_fusion.1
  321.8 5.5 %collective-permute-done.10.recv_ref = bf16[128,768]{1,0:T(8,128)(2,1)S(1)} collective-permute-done((bf16[128,768]{1,0:T(8,128)(2,1)S(1)}, bf16[128,768]{1,0:T(8,128)(2,1)S(1)}, u32[]{:S(2)}, u32[]{:S(2)}) %collective-permute-start.10) | collective-permute-done | bytes 196640 | tf_op jit(solution)/shard_map/ppermute | solution.py:525
  328.1 1.8 attend_grads.3
  332.0 20.9 %collective-permute-done.25.refs_2_ = bf16[4,3,96,768]{3,2,1,0:T(8,128)(2,1)} collective-permute-done((bf16[4,3,96,768]{3,2,1,0:T(8,128)(2,1)}, bf16[4,3,96,768]{3,2,1,0:T(8,128)(2,1)}, u32[]{:S(2)}, u32[]{:S(2)}) %collective-permute-start.25) | collective-permute-done | bytes 1769504 | tf_op jit(solution)/shard_map/ppermute | solution.py:525
  353.9 2.0 add_split.6
  356.8 1.6 add_split.7
  361.9 1.6 collective-permute-start.26
  364.4 18.4 %collective-permute-done.27.refs_2_ = bf16[2,3,96,768]{3,2,1,0:T(8,128)(2,1)S(1)} collective-permute-done((bf16[2,3,96,768]{3,2,1,0:T(8,128)(2,1)}, bf16[2,3,96,768]{3,2,1,0:T(8,128)(2,1)S(1)}, u32[]{:S(2)}, u32[]{:S(2)}) %collective-permute-start.27) | collective-permute-done | bytes 884768 | tf_op jit(solution)/shard_map/ppermute | solution.py:525
  384.6 5.7 %collective-permute-done.26.refs_2_ = bf16[2,2,96,768]{3,2,1,0:T(8,128)(2,1)} collective-permute-done((bf16[2,2,96,768]{3,2,1,0:T(8,128)(2,1)}, bf16[2,2,96,768]{3,2,1,0:T(8,128)(2,1)}, u32[]{:S(2)}, u32[]{:S(2)}) %collective-permute-start.26) | collective-permute-done | bytes 589856 | tf_op jit(solution)/shard_map/ppermute | solution.py:525
  392.8 1.8 collective-permute-start.28
  395.5 1.7 copy-done.34
  397.2 2.8 unpack_later.1
  400.0 8.6 %collective-permute-done.28.refs_2_ = bf16[2,96,896]{2,1,0:T(8,128)(2,1)S(1)} collective-permute-done((bf16[2,96,896]{2,1,0:T(8,128)(2,1)S(1)}, bf16[2,96,896]{2,1,0:T(8,128)(2,1)S(1)}, u32[]{:S(2)}, u32[]{:S(2)}) %collective-permute-start.28) | collective-permute-done | bytes 344096 | tf_op jit(solution)/shard_map/ppermute | solution.py:525
  408.6 2.3 copy-done.9
  411.0 6.7 %collective-permute-done.34.refs_3_ = bf16[1,2,96,768]{3,2,1,0:T(8,128)(2,1)S(1)} collective-permute-done((bf16[1,2,96,768]{3,2,1,0:T(8,128)(2,1)S(1)}, bf16[1,2,96,768]{3,2,1,0:T(8,128)(2,1)S(1)}, u32[]{:S(2)}, u32[]{:S(2)}) %collective-permute-start.34) | collective-permute-done | bytes 294944 | tf_op jit(solution)/shard_map/ppermute | solution.py:525
  418.8 18.2 %collective-permute-done.36.refs_2_ = bf16[3,96,768]{2,1,0:T(8,128)(2,1)S(1)} collective-permute-done((bf16[3,96,768]{2,1,0:T(8,128)(2,1)S(1)}, bf16[3,96,768]{2,1,0:T(8,128)(2,1)S(1)}, u32[]{:S(2)}, u32[]{:S(2)}) %collective-permute-start.36) | collective-permute-done | bytes 442400 | tf_op jit(solution)/shard_map/ppermute | solution.py:525
  437.7 6.2 %collective-permute-done.31.refs_2_ = bf16[96,896]{1,0:T(8,128)(2,1)S(1)} collective-permute-done((bf16[96,896]{1,0:T(8,128)(2,1)S(1)}, bf16[96,896]{1,0:T(8,128)(2,1)S(1)}, u32[]{:S(2)}, u32[]{:S(2)}) %collective-permute-start.31) | collective-permute-done | bytes 172064 | tf_op jit(solution)/shard_map/ppermute | solution.py:525
  443.9 2.5 unpack_up.1
  447.6 1.3 copy-done.42
  448.9 1.6 unpack_down.1
  (306 shorter events, 67.5 us)
Async XLA Ops:
  7.2 121.6 %all-gather.8.cloned.1.call-start = ((), (), s32[]{:S(2)}) async-start(), calls=%async_computation.3 | async-start | bytes 8183808 | tf_op jit(solution)/shard_map/all_gather | solution.py:687
  14.7 195.6 %all-gather.10.cloned.1.call-start = ((), (), s32[]{:S(2)}) async-start(), calls=%async_computation.4 | async-start | bytes 5308416 | tf_op jit(solution)/shard_map/all_gather | solution.py:687
  15.1 25.8 %copy-start.17 = (bf16[2,2,384,768]{3,2,1,0:T(8,128)(2,1)S(1)}, bf16[2,2,384,768]{3,2,1,0:T(8,128)(2,1)}, u32[]{:S(2)}) copy-start(bf16[2,2,384,768]{3,2,1,0:T(8,128)(2,1)} %down_ref.3) | copy-start | bytes 7077892
  40.9 192.4 %copy-start.7 = (bf16[512,768]{1,0:T(8,128)(2,1)}, bf16[512,768]{1,0:T(8,128)(2,1)S(1)}, u32[]{:S(2)}) copy-start(bf16[512,768]{1,0:T(8,128)(2,1)S(1)} %get-tuple-element.178.refs_1_.g_ref) | copy-start | bytes 2359300
  43.8 91.3 %copy-start.82 = (s32[1,512]{1,0:T(1,128)S(1)}, s32[1,512]{1,0:T(1,128)}, u32[]{:S(2)}) copy-start(s32[1,512]{1,0:T(1,128)} %refs_12_.3) | copy-start | bytes 6148
  131.3 13.0 %all-to-all-start.1 = ((bf16[4,192,384]{2,1,0:T(8,128)(2,1)}), bf16[4,192,384]{2,1,0:T(8,128)(2,1)S(1)}, u32[]{:S(2)}, u32[]{:S(2)}) async-start(bf16[4,192,384]{2,1,0:T(8,128)(2,1)} %bitcast.6), calls=%async_computation.1 | async-start | bytes 1179648 | tf_op jit(solution)/shard_map/all_to_all | solution.py:692
  134.8 98.4 %all-gather.12.cloned.1.call-start = ((), (), s32[]{:S(2)}) async-start(), calls=%async_computation.5 | async-start | bytes 1966080 | tf_op jit(solution)/shard_map/all_gather | solution.py:772
  138.7 48.7 %copy-start.18 = (s32[512,1]{1,0:T(8,128)}, s32[512,1]{1,0:T(8,128)S(1)}, u32[]{:S(2)}) copy-start(s32[512,1]{1,0:T(8,128)S(1)} %copy.47.segc_ref.refs_8_.refs_11_) | copy-start | bytes 6148
  143.6 14.7 %copy-start.84 = (f32[8,512]{1,0:T(8,128)}, f32[8,512]{1,0:T(8,128)S(1)}, u32[]{:S(2)}) copy-start(f32[8,512]{1,0:T(8,128)S(1)} %get-tuple-element.134.refs_8_) | copy-start | bytes 49156
  144.3 43.1 %copy-start.11 = (bf16[4,192,384]{2,1,0:T(8,128)(2,1)}, bf16[4,192,384]{2,1,0:T(8,128)(2,1)S(1)}, u32[]{:S(2)}) copy-start(bf16[4,192,384]{2,1,0:T(8,128)(2,1)S(1)} %all-to-all-done.1.wo_ref.refs_7_.refs_10_) | copy-start | bytes 1769476
  145.1 1.8 collective-permute-start
  147.0 11.2 %collective-permute-start.1 = (bf16[2,128,768]{2,1,0:T(8,128)(2,1)S(1)}, bf16[2,128,768]{2,1,0:T(8,128)(2,1)S(1)}, u32[]{:S(2)}, u32[]{:S(2)}) collective-permute-start(bf16[2,128,768]{2,1,0:T(8,128)(2,1)S(1)} %add_convert_fusion.11), channel_id=1, source_target_pairs={{0,2},{1,3},{2,0},{3,1},{4,6},{5,7},{6,4},{7,5},{8,10},{9,11},{10,... | collective-permute-start | bytes 1179656 | tf_op jit(solution)/shard_map/ppermute | solution.py:525
  158.3 2.1 collective-permute-start.2
  160.4 27.1 %copy-start.78 = (f32[4,768]{1,0:T(4,128)}, f32[4,768]{1,0:T(4,128)S(1)}, u32[]{:S(2)}) copy-start(f32[4,768]{1,0:T(4,128)S(1)} %get-tuple-element.184.refs_4_.par_ref) | copy-start | bytes 36868
  160.4 51.8 %copy-start.80 = (f32[4,768]{1,0:T(4,128)}, f32[4,768]{1,0:T(4,128)S(1)}, u32[]{:S(2)}) copy-start(f32[4,768]{1,0:T(4,128)S(1)} %get-tuple-element.183.par_ref.refs_5_) | copy-start | bytes 36868
  172.2 15.3 %copy-start.55 = (bf16[512,768]{1,0:T(8,128)(2,1)}, bf16[512,768]{1,0:T(8,128)(2,1)S(1)}, u32[]{:S(2)}) copy-start(bf16[512,768]{1,0:T(8,128)(2,1)S(1)} %get-tuple-element.127.refs_2_) | copy-start | bytes 2359300
  172.2 19.7 %copy-start.24 = (f32[512,768]{1,0:T(8,128)}, f32[512,768]{1,0:T(8,128)S(1)}, u32[]{:S(2)}) copy-start(f32[512,768]{1,0:T(8,128)S(1)} %get-tuple-element.96.refs_1_.refs_4_) | copy-start | bytes 4718596
  172.2 1.8 collective-permute-start.3
  174.1 11.5 %collective-permute-start.4 = (bf16[2,128,768]{2,1,0:T(8,128)(2,1)S(1)}, bf16[2,128,768]{2,1,0:T(8,128)(2,1)S(1)}, u32[]{:S(2)}, u32[]{:S(2)}) collective-permute-start(bf16[2,128,768]{2,1,0:T(8,128)(2,1)S(1)} %add_convert_fusion.9), channel_id=1, source_target_pairs={{0,2},{1,3},{2,0},{3,1},{4,6},{5,7},{6,4},{7,5},{8,10},{9,11},{10,... | collective-permute-start | bytes 1179656 | tf_op jit(solution)/shard_map/ppermute | solution.py:525
  185.7 1.8 collective-permute-start.5
  195.7 14.5 %copy-start.86 = (f32[8,512]{1,0:T(8,128)}, f32[8,512]{1,0:T(8,128)S(1)}, u32[]{:S(2)}) copy-start(f32[8,512]{1,0:T(8,128)S(1)} %get-tuple-element.114.refs_8_) | copy-start | bytes 49156
  195.7 1.9 collective-permute-start.6
  196.7 15.5 %copy-start.22 = (f32[512,768]{1,0:T(8,128)S(1)}, f32[512,768]{1,0:T(8,128)}, u32[]{:S(2)}) copy-start(f32[512,768]{1,0:T(8,128)} %copy-done.21) | copy-start | bytes 4718596
  196.7 162.5 %reduce-scatter.2.cloned.1.call-start = ((), (), s32[]{:S(2)}) async-start(), calls=%async_computation.6 | async-start | bytes 5308416 | tf_op jit(solution)/shard_map/reduce_scatter | solution.py:842
  198.9 11.2 %collective-permute-start.7 = (bf16[2,128,768]{2,1,0:T(8,128)(2,1)S(1)}, bf16[2,128,768]{2,1,0:T(8,128)(2,1)S(1)}, u32[]{:S(2)}, u32[]{:S(2)}) collective-permute-start(bf16[2,128,768]{2,1,0:T(8,128)(2,1)S(1)} %add_convert_fusion.7), channel_id=1, source_target_pairs={{0,2},{1,3},{2,0},{3,1},{4,6},{5,7},{6,4},{7,5},{8,10},{9,11},{10,... | collective-permute-start | bytes 1179656 | tf_op jit(solution)/shard_map/ppermute | solution.py:525
  210.2 1.9 collective-permute-start.8
  230.1 1.8 collective-permute-start.11
  232.0 11.3 %collective-permute-start.12 = (bf16[2,128,768]{2,1,0:T(8,128)(2,1)S(1)}, bf16[2,128,768]{2,1,0:T(8,128)(2,1)}, u32[]{:S(2)}, u32[]{:S(2)}) collective-permute-start(bf16[2,128,768]{2,1,0:T(8,128)(2,1)S(1)} %add_convert_fusion.5.refs_6_), channel_id=1, source_target_pairs={{0,2},{1,3},{2,0},{3,1},{4,6},{5,7},{6,4},{7,5},{8,10},{9,11},{10,... | collective-permute-start | bytes 1179656 | tf_op jit(solution)/shard_map/ppermute | solution.py:525
  245.8 37.6 %slice-start = ((s8[7274496]{0:T(1024)(128)(4,1)}), s8[3080192]{0:T(1024)(128)(4,1)S(1)}, s32[]{:S(2)}) async-start(s8[7274496]{0:T(1024)(128)(4,1)} %bitcast.38), calls=%async_computation.9 | async-start | bytes 6160384
  248.3 147.3 %all-gather.14.cloned.1.call-start = ((), (), s32[]{:S(2)}) async-start(), calls=%async_computation.7 | async-start | bytes 2949120 | tf_op jit(solution)/shard_map/all_gather | solution.py:933
  248.6 2.0 collective-permute-start.13
  261.9 21.5 %slice-start.1 = ((s8[7274496]{0:T(1024)(128)(4,1)}), s8[4194304]{0:T(1024)(128)(4,1)S(1)}, s32[]{:S(2)}) async-start(s8[7274496]{0:T(1024)(128)(4,1)} %bitcast.38), calls=%async_computation.10 | async-start | bytes 8388608
  267.8 1.8 collective-permute-start.14
  269.6 11.2 %collective-permute-start.15 = (bf16[2,128,768]{2,1,0:T(8,128)(2,1)S(1)}, bf16[2,128,768]{2,1,0:T(8,128)(2,1)S(1)}, u32[]{:S(2)}, u32[]{:S(2)}) collective-permute-start(bf16[2,128,768]{2,1,0:T(8,128)(2,1)S(1)} %add_convert_fusion.3.after_ref), channel_id=1, source_target_pairs={{0,2},{1,3},{2,0},{3,1},{4,6},{5,7},{6,4},{7,5},{8,10},{9,11},{10,... | collective-permute-start | bytes 1179656 | tf_op jit(solution)/shard_map/ppermute | solution.py:525
  281.6 1.8 collective-permute-start.16
  290.3 1.8 collective-permute-start.17
  292.1 11.2 %collective-permute-start.18 = (bf16[2,128,768]{2,1,0:T(8,128)(2,1)S(1)}, bf16[2,128,768]{2,1,0:T(8,128)(2,1)S(1)}, u32[]{:S(2)}, u32[]{:S(2)}) collective-permute-start(bf16[2,128,768]{2,1,0:T(8,128)(2,1)S(1)} %add_convert_fusion.1.refs_6_), channel_id=1, source_target_pairs={{0,2},{1,3},{2,0},{3,1},{4,6},{5,7},{6,4},{7,5},{8,10},{9,11},{10,... | collective-permute-start | bytes 1179656 | tf_op jit(solution)/shard_map/ppermute | solution.py:525
  299.4 13.1 %copy-start.35 = (bf16[4,3,96,768]{3,2,1,0:T(8,128)(2,1)}, bf16[4,3,96,768]{3,2,1,0:T(8,128)(2,1)S(1)}, u32[]{:S(2)}) copy-start(bf16[4,3,96,768]{3,2,1,0:T(8,128)(2,1)S(1)} %get-tuple-element.150.refs_1_) | copy-start | bytes 5308420
  299.5 13.1 %copy-start.40 = (bf16[4,2,96,768]{3,2,1,0:T(8,128)(2,1)}, bf16[4,2,96,768]{3,2,1,0:T(8,128)(2,1)S(1)}, u32[]{:S(2)}) copy-start(bf16[4,2,96,768]{3,2,1,0:T(8,128)(2,1)S(1)} %get-tuple-element.148.refs_1_) | copy-start | bytes 3538948
  299.5 53.4 %collective-permute-start.25 = (bf16[4,3,96,768]{3,2,1,0:T(8,128)(2,1)}, bf16[4,3,96,768]{3,2,1,0:T(8,128)(2,1)}, u32[]{:S(2)}, u32[]{:S(2)}) collective-permute-start(bf16[4,3,96,768]{3,2,1,0:T(8,128)(2,1)} %get-tuple-element.151), channel_id=1, source_target_pairs={{0,4},{4,0},{8,12},{12,8},{16,20},{20,16},{24,28},{28,24},{1,5},{5... | collective-permute-start | bytes 5308424 | tf_op jit(solution)/shard_map/ppermute | solution.py:525
  304.1 1.8 collective-permute-start.19
  304.2 13.8 %collective-permute-start.9 = (bf16[2,128,768]{2,1,0:T(8,128)(2,1)}, bf16[2,128,768]{2,1,0:T(8,128)(2,1)}, u32[]{:S(2)}, u32[]{:S(2)}) collective-permute-start(bf16[2,128,768]{2,1,0:T(8,128)(2,1)} %get-tuple-element.104), channel_id=1, source_target_pairs={{0,1},{1,0},{2,3},{3,2},{4,5},{5,4},{6,7},{7,6},{8,9},{9,8},{10,11... | collective-permute-start | bytes 1179656 | tf_op jit(solution)/shard_map/ppermute | solution.py:525
  304.7 52.1 %collective-permute-start.24 = (bf16[4,2,96,768]{3,2,1,0:T(8,128)(2,1)}, bf16[4,2,96,768]{3,2,1,0:T(8,128)(2,1)}, u32[]{:S(2)}, u32[]{:S(2)}) collective-permute-start(bf16[4,2,96,768]{3,2,1,0:T(8,128)(2,1)} %get-tuple-element.149), channel_id=1, source_target_pairs={{0,8},{4,12},{8,0},{12,4},{16,24},{20,28},{24,16},{28,20},{1,9},{5... | collective-permute-start | bytes 3538952 | tf_op jit(solution)/shard_map/ppermute | solution.py:525
  317.0 3.6 collective-permute-start.20
  319.4 7.8 %collective-permute-start.10 = (bf16[128,768]{1,0:T(8,128)(2,1)S(1)}, bf16[128,768]{1,0:T(8,128)(2,1)S(1)}, u32[]{:S(2)}, u32[]{:S(2)}) collective-permute-start(bf16[128,768]{1,0:T(8,128)(2,1)S(1)} %fusion.2), channel_id=1, source_target_pairs={{0,2},{1,3},{2,0},{3,1},{4,6},{5,7},{6,4},{7,5},{8,10},{9,11},{10,... | collective-permute-start | bytes 589832 | tf_op jit(solution)/shard_map/ppermute | solution.py:525
  320.7 10.0 %collective-permute-start.21 = (bf16[128,768]{1,0:T(8,128)(2,1)S(1)}, bf16[128,768]{1,0:T(8,128)(2,1)S(1)}, u32[]{:S(2)}, u32[]{:S(2)}) collective-permute-start(bf16[128,768]{1,0:T(8,128)(2,1)S(1)} %fusion.3), channel_id=1, source_target_pairs={{0,2},{1,3},{2,0},{3,1},{4,6},{5,7},{6,4},{7,5},{8,10},{9,11},{10,... | collective-permute-start | bytes 589832 | tf_op jit(solution)/shard_map/ppermute | solution.py:525
  330.8 22.1 %copy-start.36 = (bf16[4,3,96,768]{3,2,1,0:T(8,128)(2,1)S(1)}, bf16[4,3,96,768]{3,2,1,0:T(8,128)(2,1)}, u32[]{:S(2)}) copy-start(bf16[4,3,96,768]{3,2,1,0:T(8,128)(2,1)} %copy-done.35) | copy-start | bytes 5308420
  361.1 21.7 %copy-start.31 = (bf16[4,96,768]{2,1,0:T(8,128)(2,1)S(1)}, bf16[4,96,768]{2,1,0:T(8,128)(2,1)}, u32[]{:S(2)}) copy-start(bf16[4,96,768]{2,1,0:T(8,128)(2,1)} %copy-done.30) | copy-start | bytes 1769476
  361.1 86.5 %all-gather.16.cloned.1.call-start = ((), (), s32[]{:S(2)}) async-start(), calls=%async_computation.8 | async-start | bytes 1474560 | tf_op jit(solution)/shard_map/all_gather | solution.py:940
  361.4 21.4 %collective-permute-start.27 = (bf16[2,3,96,768]{3,2,1,0:T(8,128)(2,1)}, bf16[2,3,96,768]{3,2,1,0:T(8,128)(2,1)S(1)}, u32[]{:S(2)}, u32[]{:S(2)}) collective-permute-start(bf16[2,3,96,768]{3,2,1,0:T(8,128)(2,1)} %copy-done.94), channel_id=1, source_target_pairs={{0,8},{4,12},{8,0},{12,4},{16,24},{20,28},{24,16},{28,20},{1,9},{5... | collective-permute-start | bytes 2654216 | tf_op jit(solution)/shard_map/ppermute | solution.py:525
  361.5 30.1 %collective-permute-start.23 = (bf16[4,96,768]{2,1,0:T(8,128)(2,1)}, bf16[4,96,768]{2,1,0:T(8,128)(2,1)}, u32[]{:S(2)}, u32[]{:S(2)}) collective-permute-start(bf16[4,96,768]{2,1,0:T(8,128)(2,1)} %copy-done.75), channel_id=1, source_target_pairs={{0,4},{4,0},{8,12},{12,8},{16,20},{20,16},{24,28},{28,24},{1,5},{5... | collective-permute-start | bytes 1769480 | tf_op jit(solution)/shard_map/ppermute | solution.py:525
  361.9 28.4 %collective-permute-start.26 = (bf16[2,2,96,768]{3,2,1,0:T(8,128)(2,1)}, bf16[2,2,96,768]{3,2,1,0:T(8,128)(2,1)}, u32[]{:S(2)}, u32[]{:S(2)}) collective-permute-start(bf16[2,2,96,768]{3,2,1,0:T(8,128)(2,1)} %copy-done.95), channel_id=1, source_target_pairs={{0,4},{4,0},{8,12},{12,8},{16,20},{20,16},{24,28},{28,24},{1,5},{5... | collective-permute-start | bytes 1769480 | tf_op jit(solution)/shard_map/ppermute | solution.py:525
  363.9 27.7 %copy-start.74 = (bf16[4,96,768]{2,1,0:T(8,128)(2,1)S(1)}, bf16[4,96,768]{2,1,0:T(8,128)(2,1)}, u32[]{:S(2)}) copy-start(bf16[4,96,768]{2,1,0:T(8,128)(2,1)} %copy-done.73) | copy-start | bytes 1769476
  363.9 27.6 %collective-permute-start.22 = (bf16[4,96,128]{2,1,0:T(8,128)(2,1)S(1)}, bf16[4,96,128]{2,1,0:T(8,128)(2,1)S(1)}, u32[]{:S(2)}, u32[]{:S(2)}) collective-permute-start(bf16[4,96,128]{2,1,0:T(8,128)(2,1)S(1)} %get-tuple-element.180), channel_id=1, source_target_pairs={{0,4},{4,0},{8,12},{12,8},{16,20},{20,16},{24,28},{28,24},{1,5},{5... | collective-permute-start | bytes 294920 | tf_op jit(solution)/shard_map/ppermute | solution.py:525
  383.6 34.1 %collective-permute-start.33 = (bf16[1,3,96,768]{3,2,1,0:T(8,128)(2,1)}, bf16[1,3,96,768]{3,2,1,0:T(8,128)(2,1)S(1)}, u32[]{:S(2)}, u32[]{:S(2)}) collective-permute-start(bf16[1,3,96,768]{3,2,1,0:T(8,128)(2,1)} %get-tuple-element.164), channel_id=1, source_target_pairs={{0,16},{4,20},{8,24},{12,28},{16,0},{20,4},{24,8},{28,12},{1,17},{... | collective-permute-start | bytes 1327112 | tf_op jit(solution)/shard_map/ppermute | solution.py:525
  392.8 15.8 %collective-permute-start.28 = (bf16[2,96,896]{2,1,0:T(8,128)(2,1)S(1)}, bf16[2,96,896]{2,1,0:T(8,128)(2,1)S(1)}, u32[]{:S(2)}, u32[]{:S(2)}) collective-permute-start(bf16[2,96,896]{2,1,0:T(8,128)(2,1)S(1)} %get-tuple-element.160), channel_id=1, source_target_pairs={{0,8},{4,12},{8,0},{12,4},{16,24},{20,28},{24,16},{28,20},{1,9},{5... | collective-permute-start | bytes 1032200 | tf_op jit(solution)/shard_map/ppermute | solution.py:525
  394.6 23.1 %collective-permute-start.34 = (bf16[1,2,96,768]{3,2,1,0:T(8,128)(2,1)S(1)}, bf16[1,2,96,768]{3,2,1,0:T(8,128)(2,1)S(1)}, u32[]{:S(2)}, u32[]{:S(2)}) collective-permute-start(bf16[1,2,96,768]{3,2,1,0:T(8,128)(2,1)S(1)} %get-tuple-element.165), channel_id=1, source_target_pairs={{0,16},{4,20},{8,24},{12,28},{16,0},{20,4},{24,8},{28,12},{1,17},{... | collective-permute-start | bytes 884744 | tf_op jit(solution)/shard_map/ppermute | solution.py:525
  418.5 18.4 %collective-permute-start.36 = (bf16[3,96,768]{2,1,0:T(8,128)(2,1)S(1)}, bf16[3,96,768]{2,1,0:T(8,128)(2,1)S(1)}, u32[]{:S(2)}, u32[]{:S(2)}) collective-permute-start(bf16[3,96,768]{2,1,0:T(8,128)(2,1)S(1)} %get-tuple-element.166.refs_0_), channel_id=1, source_target_pairs={{0,2},{1,3},{2,0},{3,1},{4,6},{5,7},{6,4},{7,5},{8,10},{9,11},{10,... | collective-permute-start | bytes 1327112 | tf_op jit(solution)/shard_map/ppermute | solution.py:525
  418.8 18.2 %collective-permute-start.29 = (bf16[1,96,896]{2,1,0:T(8,128)(2,1)S(1)}, bf16[1,96,896]{2,1,0:T(8,128)(2,1)S(1)}, u32[]{:S(2)}, u32[]{:S(2)}) collective-permute-start(bf16[1,96,896]{2,1,0:T(8,128)(2,1)S(1)} %get-tuple-element.163), channel_id=1, source_target_pairs={{0,16},{4,20},{8,24},{12,28},{16,0},{20,4},{24,8},{28,12},{1,17},{... | collective-permute-start | bytes 516104 | tf_op jit(solution)/shard_map/ppermute | solution.py:525
  418.8 25.1 %collective-permute-start.35 = (bf16[3,96,768]{2,1,0:T(8,128)(2,1)S(1)}, bf16[3,96,768]{2,1,0:T(8,128)(2,1)S(1)}, u32[]{:S(2)}, u32[]{:S(2)}) collective-permute-start(bf16[3,96,768]{2,1,0:T(8,128)(2,1)S(1)} %get-tuple-element.166.refs_0_), channel_id=1, source_target_pairs={{0,1},{1,0},{2,3},{3,2},{4,5},{5,4},{6,7},{7,6},{8,9},{9,8},{10,11... | collective-permute-start | bytes 1327112 | tf_op jit(solution)/shard_map/ppermute | solution.py:525
  437.0 6.9 %collective-permute-start.37 = (bf16[3,96,768]{2,1,0:T(8,128)(2,1)S(1)}, bf16[3,96,768]{2,1,0:T(8,128)(2,1)S(1)}, u32[]{:S(2)}, u32[]{:S(2)}) collective-permute-start(bf16[3,96,768]{2,1,0:T(8,128)(2,1)S(1)} %collective-permute-done.36.refs_2_), channel_id=1, source_target_pairs={{0,1},{1,0},{2,3},{3,2},{4,5},{5,4},{6,7},{7,6},{8,9},{9,8},{10,11... | collective-permute-start | bytes 1327112 | tf_op jit(solution)/shard_map/ppermute | solution.py:525
  437.0 6.9 %collective-permute-start.31 = (bf16[96,896]{1,0:T(8,128)(2,1)S(1)}, bf16[96,896]{1,0:T(8,128)(2,1)S(1)}, u32[]{:S(2)}, u32[]{:S(2)}) collective-permute-start(bf16[96,896]{1,0:T(8,128)(2,1)S(1)} %add_last.1.refs_0_), channel_id=1, source_target_pairs={{0,2},{1,3},{2,0},{3,1},{4,6},{5,7},{6,4},{7,5},{8,10},{9,11},{10,... | collective-permute-start | bytes 516104 | tf_op jit(solution)/shard_map/ppermute | solution.py:525
  437.4 9.0 %collective-permute-start.30 = (bf16[96,896]{1,0:T(8,128)(2,1)S(1)}, bf16[96,896]{1,0:T(8,128)(2,1)S(1)}, u32[]{:S(2)}, u32[]{:S(2)}) collective-permute-start(bf16[96,896]{1,0:T(8,128)(2,1)S(1)} %add_last.1.refs_0_), channel_id=1, source_target_pairs={{0,1},{1,0},{2,3},{3,2},{4,5},{5,4},{6,7},{7,6},{8,9},{9,8},{10,11... | collective-permute-start | bytes 516104 | tf_op jit(solution)/shard_map/ppermute | solution.py:525
  443.9 2.5 collective-permute-start.32
  (81 other events, 282.2 us)
Sparse Core Ops, SparseCore 0:
  14.8 113.8 all-gather.7
  130.9 78.0 all-gather.9
  211.1 17.7 all-gather.11
  248.4 104.6 reduce-scatter.1
  361.2 21.7 all-gather.13
  418.7 19.9 all-gather.15

commit v2 on v1

--- a/solution.py
+++ b/solution.py
@@ -9,7 +9,7 @@
 HD = 64
 BF = jnp.bfloat16
 F32 = jnp.float32
-VMEM_BYTES = 26 * 1024 * 1024
+VMEM_BYTES = 50 * 1024 * 1024
 COLS = 256
 PACKED = 768
 KEPT = 640

time: 462 us -> 453 us (0.981)
  local copies, waits for them, and re-layouts: 63.3 us -> 25.9 us
  Pallas kernels: 81.2 us -> 109 us
    unnamed x203 -> x127, local copies, waits for them, and re-layouts: 59.1 us -> 23.1 us
    pallas_call x2, Pallas kernels: 12.4 us -> 18.1 us  [body(): call(lambda *refs, layer=layer: attend_back_kernel(layer, *refs), fresh_t...]
  transfers between devices with their start and end apart: 45 -> 45, of which waited for: 28 -> 28; matrix products, arithmetic and copies ran while one was open for 3% -> 3% of each run, Pallas kernels for 17% -> 23%
where the time goes in v2:
time: 453 us; the launch traced here: 448 us
  waiting for transfers between devices  237 us (52%)
  Pallas kernels  109 us (24%)
  local copies, waits for them, and re-layouts  25.9 us (6%)
  blocking collectives  25.5 us (6%)
  starting transfers between devices  24.1 us (5%)
  between operations  15.1 us (3%)
  other arithmetic  12.4 us (3%)
    ppermute x38, waiting for transfers between devices, swap(): return lax.ppermute(array, axis, [(i, i ^ bits) for i in range(count)])  149 us
    all_gather x2, waiting for transfers between devices, body(): lax.all_gather(pack, 'dp', axis=0, tiled=True)  84.7 us
    all_to_all x1, blocking collectives, spread(): return lax.all_to_all(copies, axis, 0, 0, tiled=True)  25.5 us
    unnamed x127, local copies, waits for them, and re-layouts  23.1 us
    ppermute x38, starting transfers between devices, swap(): return lax.ppermute(array, axis, [(i, i ^ bits) for i in range(count)])  19.4 us
    pallas_call x2, Pallas kernels, body(): call(lambda *refs, layer=layer: attend_back_kernel(layer, *refs), fresh_t...  18.1 us
    pallas_call x2, Pallas kernels, body(): call(feed_kernel, (shape(*flat, dtype=F32), shape(*flat), shape(row_len,...  17.8 us
    pallas_call x2, Pallas kernels, body(): call(lambda *refs, count=len(above): feed_grads_kernel(count, *refs), (sh...  14 us
  transfers between devices with their start and end apart: 45, of which 28 were waited for; matrix products, arithmetic and copies ran while one was open for 3% of the time, Pallas kernels for 23%

profile of v2, /device:TPU:0, one launch (start us, length us, event | category | flops | bytes accessed | tf_op | source)
XLA Modules:
  0.0 448.3 jit_solution(13324468708936685461)
XLA Ops:
  10.1 2.9 pack.2
  13.4 25.5 %all_to_all.10 = bf16[4,128,1664]{2,1,0:T(8,128)(2,1)S(1)} all-to-all(bf16[4,128,1664]{2,1,0:T(8,128)(2,1)S(1)} %broadcast_in_dim.2), channel_id=1, replica_groups=mesh['dp'=8,'head'=4] {'head'}, dimensions={0} | all-to-all | bytes 3407872 | tf_op jit(solution)/shard_map/all_to_all | solution.py:552
  39.1 3.3 pack.3
  42.4 84.7 %all-gather.8.cloned.1.call-done.small_ref.w_ref.wu0_ref.wu1_ref.wd0_ref.wd1_ref.refs_6_.refs_9_ = bf16[768,4736]{1,0:T(8,128)(2,1)} async-done(((bf16[96,4736]{1,0:T(8,128)(2,1)}), bf16[768,4736]{1,0:T(8,128)(2,1)}) %all-gather.8.cloned.1.call-update) | async-done | bytes 7274512 | tf_op jit(solution)/shard_map/all_gather | solution.py:687
  127.1 1.6 fusion.4
  129.7 3.5 all-to-all-start.1
  133.6 4.4 attend_first.1
  139.8 2.9 all-to-all-done.1.wo_ref.refs_7_.refs_10_
  143.5 1.7 collective-permute-done
  145.7 10.8 %collective-permute-done.1 = bf16[2,128,768]{2,1,0:T(8,128)(2,1)S(1)} collective-permute-done((bf16[2,128,768]{2,1,0:T(8,128)(2,1)S(1)}, bf16[2,128,768]{2,1,0:T(8,128)(2,1)S(1)}, u32[]{:S(2)}, u32[]{:S(2)}) %collective-permute-start.1) | collective-permute-done | bytes 393248 | tf_op jit(solution)/shard_map/ppermute | solution.py:525
  160.2 8.7 %feed.2 = (f32[512,768]{1,0:T(8,128)}, bf16[512,768]{1,0:T(8,128)(2,1)S(1)}, bf16[512,768]{1,0:T(8,128)(2,1)S(1)}, bf16[512,768]{1,0:T(8,128)(2,1)S(1)}, f32[2,1...) custom-call(s32[1]{0:T(128)} %bitcast.head_ref.refs_0_, bf16[512,768]{1,0:T(8,128)(2,1)} %copy-done.1, ...), custom_call_target="tpu_custom_call" | custom-call | tf_op jit(solution)/shard_map/feed/pallas_call | solution.py:757
  169.0 1.6 collective-permute-done.3
  170.6 1.2 add_convert_fusion.9
  172.3 10.8 %collective-permute-done.4 = bf16[2,128,768]{2,1,0:T(8,128)(2,1)S(1)} collective-permute-done((bf16[2,128,768]{2,1,0:T(8,128)(2,1)S(1)}, bf16[2,128,768]{2,1,0:T(8,128)(2,1)S(1)}, u32[]{:S(2)}, u32[]{:S(2)}) %collective-permute-start.4) | collective-permute-done | bytes 393248 | tf_op jit(solution)/shard_map/ppermute | solution.py:525
  183.2 1.7 collective-permute-done.5.refs_3_
  185.0 6.6 %attend.1 = (f32[512,768]{1,0:T(8,128)}, bf16[512,768]{1,0:T(8,128)(2,1)S(1)}, bf16[512,640]{1,0:T(8,128)(2,1)S(1)}, bf16[192,512]{1,0:T(8,128)(2,1)S(1)}, f32[8...) custom-call(s32[1]{0:T(128)} %bitcast.head_ref.refs_0_, ...), custom_call_target="tpu_custom_call" | custom-call | tf_op jit(solution)/shard_map/attend/pallas_call | solution.py:743
  195.5 1.3 add_convert_fusion.7
  197.2 10.9 %collective-permute-done.7 = bf16[2,128,768]{2,1,0:T(8,128)(2,1)S(1)} collective-permute-done((bf16[2,128,768]{2,1,0:T(8,128)(2,1)S(1)}, bf16[2,128,768]{2,1,0:T(8,128)(2,1)S(1)}, u32[]{:S(2)}, u32[]{:S(2)}) %collective-permute-start.7) | collective-permute-done | bytes 393248 | tf_op jit(solution)/shard_map/ppermute | solution.py:525
  208.3 1.8 collective-permute-done.8.other_ref
  210.1 9.2 %feed.3 = (f32[512,768]{1,0:T(8,128)}, bf16[512,768]{1,0:T(8,128)(2,1)S(1)}, bf16[512,768]{1,0:T(8,128)(2,1)S(1)}, bf16[512,768]{1,0:T(8,128)(2,1)S(1)}, f32[2,1...) custom-call(s32[1]{0:T(128)} %bitcast.head_ref.refs_0_, f32[512,768]{1,0:T(8,128)} %get-tuple-element.99.base_ref, ...), custom_call_target="tpu_custom_call" | custom-call | tf_op jit(solution)/shard_map/feed/pallas_call | solution.py:757
  222.4 5.9 %feed_back_first.1 = (bf16[512,768]{1,0:T(8,128)(2,1)S(1)}, f32[2,128,768]{2,1,0:T(8,128)S(1)}, bf16[2,128,768]{2,1,0:T(8,128)(2,1)S(1)}) custom-call(s32[1]{0:T(128)} %bitcast.head_ref.refs_0_, bf16[512,768]{1,0:T(8,128)(2,1)S(1)} %get-tuple-element.178.refs_1_.g_ref, bf16[512,768]{1,0:T(8,128)(2,1)S(1)} %get-tuple-element.105.slope_ref, ...), custom_call_target="tpu_custom_call" | custom-call | tf_op jit(solution)/shard_map/feed_back_first/pallas_call | solution.py:796
  228.5 1.6 collective-permute-done.11
  234.0 6.1 %feed_grads.2 = (f32[1,1]{1,0:T(1,128)}, bf16[4,768,768]{2,1,0:T(8,128)(2,1)}) custom-call(s32[1]{0:T(128)} %bitcast.12.refs_0_.dp_ref, bf16[512,768]{1,0:T(8,128)(2,1)S(1)} %get-tuple-element.178.refs_1_.g_ref, bf16[512,768]{1,0:T(8,128)(2,1)S(1)} %copy-done.22, bf16[512,768]{1,0:T(8,128)(2,1)S(1)} %copy-done.24, bf16[512,768]{1,0:T(8,128)(2,1)S(1)} %copy-done.27, ...), custom_call_target="tpu_custom_call" | custom-call | tf_op jit(solution)/shard_map/feed_grads/pallas_call | solution.py:823
  240.0 1.5 collective-permute-done.12
  241.5 1.8 add_convert_fusion.4.refs_2_.after_ref
  243.9 1.7 collective-permute-done.13.refs_3_
  245.7 8.8 %attend_back.2 = (f32[512,768]{1,0:T(8,128)}, f32[8,768]{1,0:T(8,128)S(1)}, bf16[512,768]{1,0:T(8,128)(2,1)}, bf16[512,640]{1,0:T(8,128)(2,1)S(1)}, f32[2,128,76...) custom-call(s32[1]{0:T(128)} %bitcast.head_ref.refs_0_, bf16[512,768]{1,0:T(8,128)(2,1)} %copy-done, ...), custom_call_target="tpu_custom_call" | custom-call | tf_op jit(solution)/shard_map/attend_back/pallas_call | solution.py:845
  254.6 1.6 collective-permute-done.14
  257.8 2.9 attend_grads.2
  260.7 7.9 %collective-permute-done.15 = bf16[2,128,768]{2,1,0:T(8,128)(2,1)S(1)} collective-permute-done((bf16[2,128,768]{2,1,0:T(8,128)(2,1)S(1)}, bf16[2,128,768]{2,1,0:T(8,128)(2,1)S(1)}, u32[]{:S(2)}, u32[]{:S(2)}) %collective-permute-start.15) | collective-permute-done | bytes 393248 | tf_op jit(solution)/shard_map/ppermute | solution.py:525
  269.5 1.7 collective-permute-done.16.other_ref
  271.2 10.1 %feed_back.1 = (f32[512,768]{1,0:T(8,128)}, f32[8,768]{1,0:T(8,128)S(1)}, bf16[512,768]{1,0:T(8,128)(2,1)S(1)}, bf16[512,768]{1,0:T(8,128)(2,1)S(1)}, f32[2,128,...) custom-call(s32[1]{0:T(128)} %bitcast.head_ref.refs_0_, f32[512,768]{1,0:T(8,128)} %get-tuple-element.115.grad_ref, ...), custom_call_target="tpu_custom_call" | custom-call | tf_op jit(solution)/shard_map/feed_back/pallas_call | solution.py:805
  281.5 1.6 collective-permute-done.17
  283.7 7.9 %feed_grads.3 = (f32[1,1]{1,0:T(1,128)}, bf16[4,3,96,768]{3,2,1,0:T(8,128)(2,1)}, bf16[4,3,96,768]{3,2,1,0:T(8,128)(2,1)}, bf16[4,2,96,768]{3,2,1,0:T(8,128)(2,1)}, bf16[4,2,96,768]{3,2,1,0:T(8,128)(2,1)}) custom-call(s32[1]{0:T(128)} %bitcast.12.refs_0_.dp_ref, bf16[512,768]{1,0:T(8,128)(2,1)S(1)} %get-tuple-element.126.refs_1_, ...), custom_call_target="tpu_custom_call" | custom-call | tf_op jit(solution)/shard_map/feed_grads/pallas_call | solution.py:823
  292.2 2.1 collective-permute-done.18
  295.7 1.2 collective-permute-done.19.refs_3_
  296.9 9.2 %attend_back.3 = (f32[512,768]{1,0:T(8,128)}, f32[8,768]{1,0:T(8,128)S(1)}, bf16[512,768]{1,0:T(8,128)(2,1)}, bf16[512,640]{1,0:T(8,128)(2,1)S(1)}, f32[2,128,76...) custom-call(s32[1]{0:T(128)} %bitcast.head_ref.refs_0_, f32[512,768]{1,0:T(8,128)} %get-tuple-element.123.refs_1_, ...), custom_call_target="tpu_custom_call" | custom-call | tf_op jit(solution)/shard_map/attend_back/pallas_call | solution.py:845
  309.4 1.7 collective-permute-start.21
  311.0 4.5 collective-permute-done.10.recv_ref
  316.3 3.3 attend_grads.3
  320.5 1.2 last_norm.1
  321.7 23.3 %collective-permute-done.25.refs_2_ = bf16[4,3,96,768]{3,2,1,0:T(8,128)(2,1)} collective-permute-done((bf16[4,3,96,768]{3,2,1,0:T(8,128)(2,1)}, bf16[4,3,96,768]{3,2,1,0:T(8,128)(2,1)}, u32[]{:S(2)}, u32[]{:S(2)}) %collective-permute-start.25) | collective-permute-done | bytes 1769504 | tf_op jit(solution)/shard_map/ppermute | solution.py:525
  346.0 2.0 add_split.6
  348.9 1.5 add_split.7
  354.0 1.5 collective-permute-start.26
  356.4 17.7 %collective-permute-done.27.refs_2_ = bf16[2,3,96,768]{3,2,1,0:T(8,128)(2,1)S(1)} collective-permute-done((bf16[2,3,96,768]{3,2,1,0:T(8,128)(2,1)}, bf16[2,3,96,768]{3,2,1,0:T(8,128)(2,1)S(1)}, u32[]{:S(2)}, u32[]{:S(2)}) %collective-permute-start.27) | collective-permute-done | bytes 884768 | tf_op jit(solution)/shard_map/ppermute | solution.py:525
  375.0 1.5 collective-permute-start.33
  376.5 5.1 %collective-permute-done.26.refs_2_ = bf16[2,2,96,768]{3,2,1,0:T(8,128)(2,1)} collective-permute-done((bf16[2,2,96,768]{3,2,1,0:T(8,128)(2,1)}, bf16[2,2,96,768]{3,2,1,0:T(8,128)(2,1)}, u32[]{:S(2)}, u32[]{:S(2)}) %collective-permute-start.26) | collective-permute-done | bytes 589856 | tf_op jit(solution)/shard_map/ppermute | solution.py:525
  381.7 1.9 add_split.9
  383.5 1.2 add_split.10
  384.8 1.8 collective-permute-start.28
  386.6 1.5 collective-permute-start.34
  388.1 1.7 copy-done.6
  389.8 2.8 unpack_later.1
  392.6 6.9 %collective-permute-done.28.refs_2_ = bf16[2,96,896]{2,1,0:T(8,128)(2,1)S(1)} collective-permute-done((bf16[2,96,896]{2,1,0:T(8,128)(2,1)S(1)}, bf16[2,96,896]{2,1,0:T(8,128)(2,1)S(1)}, u32[]{:S(2)}, u32[]{:S(2)}) %collective-permute-start.28) | collective-permute-done | bytes 344096 | tf_op jit(solution)/shard_map/ppermute | solution.py:525
  399.5 9.0 %collective-permute-done.34.refs_3_ = bf16[1,2,96,768]{3,2,1,0:T(8,128)(2,1)S(1)} collective-permute-done((bf16[1,2,96,768]{3,2,1,0:T(8,128)(2,1)}, bf16[1,2,96,768]{3,2,1,0:T(8,128)(2,1)S(1)}, u32[]{:S(2)}, u32[]{:S(2)}) %collective-permute-start.34) | collective-permute-done | bytes 294944 | tf_op jit(solution)/shard_map/ppermute | solution.py:525
  409.4 1.7 collective-permute-start.36
  411.1 15.9 %collective-permute-done.36.refs_2_ = bf16[3,96,768]{2,1,0:T(8,128)(2,1)S(1)} collective-permute-done((bf16[3,96,768]{2,1,0:T(8,128)(2,1)S(1)}, bf16[3,96,768]{2,1,0:T(8,128)(2,1)S(1)}, u32[]{:S(2)}, u32[]{:S(2)}) %collective-permute-start.36) | collective-permute-done | bytes 442400 | tf_op jit(solution)/shard_map/ppermute | solution.py:525
  427.1 2.5 collective-permute-start.31
  429.8 4.8 %collective-permute-done.31.refs_2_ = bf16[96,896]{1,0:T(8,128)(2,1)S(1)} collective-permute-done((bf16[96,896]{1,0:T(8,128)(2,1)S(1)}, bf16[96,896]{1,0:T(8,128)(2,1)S(1)}, u32[]{:S(2)}, u32[]{:S(2)}) %collective-permute-start.31) | collective-permute-done | bytes 172064 | tf_op jit(solution)/shard_map/ppermute | solution.py:525
  434.7 2.5 unpack_up.1
  437.1 1.2 unpack_attn.1
  438.4 1.3 copy-done.11
  439.6 1.6 unpack_down.1
  (229 shorter events, 43.0 us)
Async XLA Ops:
  7.2 119.9 %all-gather.8.cloned.1.call-start = ((), (), s32[]{:S(2)}) async-start(), calls=%async_computation.3 | async-start | bytes 8183808 | tf_op jit(solution)/shard_map/all_gather | solution.py:687
  13.0 195.3 %all-gather.10.cloned.1.call-start = ((), (), s32[]{:S(2)}) async-start(), calls=%async_computation.4 | async-start | bytes 5308416 | tf_op jit(solution)/shard_map/all_gather | solution.py:687
  39.1 94.5 %copy-start.1 = (bf16[512,768]{1,0:T(8,128)(2,1)}, bf16[512,768]{1,0:T(8,128)(2,1)S(1)}, u32[]{:S(2)}) copy-start(bf16[512,768]{1,0:T(8,128)(2,1)S(1)} %get-tuple-element.179.tok_ref.base_ref.refs_0_) | copy-start | bytes 2359300
  39.1 191.5 %copy-start = (bf16[512,768]{1,0:T(8,128)(2,1)}, bf16[512,768]{1,0:T(8,128)(2,1)S(1)}, u32[]{:S(2)}) copy-start(bf16[512,768]{1,0:T(8,128)(2,1)S(1)} %get-tuple-element.178.refs_1_.g_ref) | copy-start | bytes 2359300
  42.4 91.0 %copy-start.44 = (s32[1,512]{1,0:T(1,128)S(1)}, s32[1,512]{1,0:T(1,128)}, u32[]{:S(2)}) copy-start(s32[1,512]{1,0:T(1,128)} %refs_12_.3) | copy-start | bytes 6148
  129.7 13.0 %all-to-all-start.1 = ((bf16[4,192,384]{2,1,0:T(8,128)(2,1)}), bf16[4,192,384]{2,1,0:T(8,128)(2,1)S(1)}, u32[]{:S(2)}, u32[]{:S(2)}) async-start(bf16[4,192,384]{2,1,0:T(8,128)(2,1)} %bitcast.6), calls=%async_computation.1 | async-start | bytes 1179648 | tf_op jit(solution)/shard_map/all_to_all | solution.py:692
  133.2 97.4 %all-gather.12.cloned.1.call-start = ((), (), s32[]{:S(2)}) async-start(), calls=%async_computation.5 | async-start | bytes 1966080 | tf_op jit(solution)/shard_map/all_gather | solution.py:772
  139.8 16.9 %copy-start.46 = (f32[8,512]{1,0:T(8,128)}, f32[8,512]{1,0:T(8,128)S(1)}, u32[]{:S(2)}) copy-start(f32[8,512]{1,0:T(8,128)S(1)} %get-tuple-element.134.refs_8_) | copy-start | bytes 49156
  143.4 1.8 collective-permute-start
  145.3 11.2 %collective-permute-start.1 = (bf16[2,128,768]{2,1,0:T(8,128)(2,1)S(1)}, bf16[2,128,768]{2,1,0:T(8,128)(2,1)S(1)}, u32[]{:S(2)}, u32[]{:S(2)}) collective-permute-start(bf16[2,128,768]{2,1,0:T(8,128)(2,1)S(1)} %add_convert_fusion.11), channel_id=1, source_target_pairs={{0,2},{1,3},{2,0},{3,1},{4,6},{5,7},{6,4},{7,5},{8,10},{9,11},{10,... | collective-permute-start | bytes 1179656 | tf_op jit(solution)/shard_map/ppermute | solution.py:525
  156.6 1.8 collective-permute-start.2
  168.8 16.1 %copy-start.20 = (bf16[512,768]{1,0:T(8,128)(2,1)}, bf16[512,768]{1,0:T(8,128)(2,1)S(1)}, u32[]{:S(2)}) copy-start(bf16[512,768]{1,0:T(8,128)(2,1)S(1)} %get-tuple-element.128.refs_3_) | copy-start | bytes 2359300
  168.8 16.1 %copy-start.28 = (bf16[512,768]{1,0:T(8,128)(2,1)}, bf16[512,768]{1,0:T(8,128)(2,1)S(1)}, u32[]{:S(2)}) copy-start(bf16[512,768]{1,0:T(8,128)(2,1)S(1)} %get-tuple-element.122.slope_ref) | copy-start | bytes 2359300
  168.8 22.8 %copy-start.18 = (bf16[512,768]{1,0:T(8,128)(2,1)}, bf16[512,768]{1,0:T(8,128)(2,1)S(1)}, u32[]{:S(2)}) copy-start(bf16[512,768]{1,0:T(8,128)(2,1)S(1)} %get-tuple-element.127.refs_2_) | copy-start | bytes 2359300
  168.8 1.8 collective-permute-start.3
  171.8 11.2 %collective-permute-start.4 = (bf16[2,128,768]{2,1,0:T(8,128)(2,1)S(1)}, bf16[2,128,768]{2,1,0:T(8,128)(2,1)S(1)}, u32[]{:S(2)}, u32[]{:S(2)}) collective-permute-start(bf16[2,128,768]{2,1,0:T(8,128)(2,1)S(1)} %add_convert_fusion.9), channel_id=1, source_target_pairs={{0,2},{1,3},{2,0},{3,1},{4,6},{5,7},{6,4},{7,5},{8,10},{9,11},{10,... | collective-permute-start | bytes 1179656 | tf_op jit(solution)/shard_map/ppermute | solution.py:525
  183.2 1.8 collective-permute-start.5
  193.7 1.9 collective-permute-start.6
  194.7 156.6 %reduce-scatter.2.cloned.1.call-start = ((), (), s32[]{:S(2)}) async-start(), calls=%async_computation.6 | async-start | bytes 5308416 | tf_op jit(solution)/shard_map/reduce_scatter | solution.py:842
  196.8 11.3 %collective-permute-start.7 = (bf16[2,128,768]{2,1,0:T(8,128)(2,1)S(1)}, bf16[2,128,768]{2,1,0:T(8,128)(2,1)S(1)}, u32[]{:S(2)}, u32[]{:S(2)}) collective-permute-start(bf16[2,128,768]{2,1,0:T(8,128)(2,1)S(1)} %add_convert_fusion.7), channel_id=1, source_target_pairs={{0,2},{1,3},{2,0},{3,1},{4,6},{5,7},{6,4},{7,5},{8,10},{9,11},{10,... | collective-permute-start | bytes 1179656 | tf_op jit(solution)/shard_map/ppermute | solution.py:525
  208.2 1.9 collective-permute-start.8
  228.3 1.8 collective-permute-start.11
  230.2 11.3 %collective-permute-start.12 = (bf16[2,128,768]{2,1,0:T(8,128)(2,1)S(1)}, bf16[2,128,768]{2,1,0:T(8,128)(2,1)}, u32[]{:S(2)}, u32[]{:S(2)}) collective-permute-start(bf16[2,128,768]{2,1,0:T(8,128)(2,1)S(1)} %add_convert_fusion.5.refs_6_), channel_id=1, source_target_pairs={{0,2},{1,3},{2,0},{3,1},{4,6},{5,7},{6,4},{7,5},{8,10},{9,11},{10,... | collective-permute-start | bytes 1179656 | tf_op jit(solution)/shard_map/ppermute | solution.py:525
  243.3 144.8 %all-gather.14.cloned.1.call-start = ((), (), s32[]{:S(2)}) async-start(), calls=%async_computation.7 | async-start | bytes 2949120 | tf_op jit(solution)/shard_map/all_gather | solution.py:933
  243.9 1.8 collective-permute-start.13
  254.5 1.7 collective-permute-start.14
  257.4 11.2 %collective-permute-start.15 = (bf16[2,128,768]{2,1,0:T(8,128)(2,1)S(1)}, bf16[2,128,768]{2,1,0:T(8,128)(2,1)S(1)}, u32[]{:S(2)}, u32[]{:S(2)}) collective-permute-start(bf16[2,128,768]{2,1,0:T(8,128)(2,1)S(1)} %add_convert_fusion.3.after_ref), channel_id=1, source_target_pairs={{0,2},{1,3},{2,0},{3,1},{4,6},{5,7},{6,4},{7,5},{8,10},{9,11},{10,... | collective-permute-start | bytes 1179656 | tf_op jit(solution)/shard_map/ppermute | solution.py:525
  257.8 13.4 %copy-start.41 = (f32[4,768]{1,0:T(4,128)S(1)}, f32[4,768]{1,0:T(4,128)}, u32[]{:S(2)}) copy-start(f32[4,768]{1,0:T(4,128)} %copy-done.40) | copy-start | bytes 36868
  269.4 1.8 collective-permute-start.16
  281.3 1.8 collective-permute-start.17
  283.1 11.2 %collective-permute-start.18 = (bf16[2,128,768]{2,1,0:T(8,128)(2,1)S(1)}, bf16[2,128,768]{2,1,0:T(8,128)(2,1)S(1)}, u32[]{:S(2)}, u32[]{:S(2)}) collective-permute-start(bf16[2,128,768]{2,1,0:T(8,128)(2,1)S(1)} %add_convert_fusion.1.refs_6_), channel_id=1, source_target_pairs={{0,2},{1,3},{2,0},{3,1},{4,6},{5,7},{6,4},{7,5},{8,10},{9,11},{10,... | collective-permute-start | bytes 1179656 | tf_op jit(solution)/shard_map/ppermute | solution.py:525
  283.6 11.6 %copy-start.55 = (bf16[2,128,768]{2,1,0:T(8,128)(2,1)S(1)}, bf16[2,128,768]{2,1,0:T(8,128)(2,1)}, u32[]{:S(2)}) copy-start(bf16[2,128,768]{2,1,0:T(8,128)(2,1)} %copy-done.54) | copy-start | bytes 1179652
  283.7 13.3 %copy-start.30 = (bf16[512,640]{1,0:T(8,128)(2,1)S(1)}, bf16[512,640]{1,0:T(8,128)(2,1)}, u32[]{:S(2)}) copy-start(bf16[512,640]{1,0:T(8,128)(2,1)} %copy-done.29) | copy-start | bytes 1966084
  283.7 13.3 %copy-start.47 = (f32[8,512]{1,0:T(8,128)S(1)}, f32[8,512]{1,0:T(8,128)}, u32[]{:S(2)}) copy-start(f32[8,512]{1,0:T(8,128)} %copy-done.46) | copy-start | bytes 49156
  291.6 53.4 %collective-permute-start.25 = (bf16[4,3,96,768]{3,2,1,0:T(8,128)(2,1)}, bf16[4,3,96,768]{3,2,1,0:T(8,128)(2,1)}, u32[]{:S(2)}, u32[]{:S(2)}) collective-permute-start(bf16[4,3,96,768]{3,2,1,0:T(8,128)(2,1)} %get-tuple-element.151), channel_id=1, source_target_pairs={{0,4},{4,0},{8,12},{12,8},{16,20},{20,16},{24,28},{28,24},{1,5},{5... | collective-permute-start | bytes 5308424 | tf_op jit(solution)/shard_map/ppermute | solution.py:525
  295.1 1.8 collective-permute-start.19
  295.2 11.2 %collective-permute-start.9 = (bf16[2,128,768]{2,1,0:T(8,128)(2,1)S(1)}, bf16[2,128,768]{2,1,0:T(8,128)(2,1)S(1)}, u32[]{:S(2)}, u32[]{:S(2)}) collective-permute-start(bf16[2,128,768]{2,1,0:T(8,128)(2,1)S(1)} %copy-done.55), channel_id=1, source_target_pairs={{0,1},{1,0},{2,3},{3,2},{4,5},{5,4},{6,7},{7,6},{8,9},{9,8},{10,11... | collective-permute-start | bytes 1179656 | tf_op jit(solution)/shard_map/ppermute | solution.py:525
  295.7 52.3 %collective-permute-start.24 = (bf16[4,2,96,768]{3,2,1,0:T(8,128)(2,1)}, bf16[4,2,96,768]{3,2,1,0:T(8,128)(2,1)}, u32[]{:S(2)}, u32[]{:S(2)}) collective-permute-start(bf16[4,2,96,768]{3,2,1,0:T(8,128)(2,1)} %get-tuple-element.149), channel_id=1, source_target_pairs={{0,8},{4,12},{8,0},{12,4},{16,24},{20,28},{24,16},{28,20},{1,9},{5... | collective-permute-start | bytes 3538952 | tf_op jit(solution)/shard_map/ppermute | solution.py:525
  296.9 9.4 %copy-start.61 = (s32[128,1]{0,1:T(1,128)S(1)}, s32[128,1]{0,1:T(1,128)}, u32[]{:S(2)}) copy-start(s32[128,1]{0,1:T(1,128)} %param.12) | copy-start | bytes 1540
  306.2 2.0 collective-permute-start.20
  307.7 7.9 %copy-start.2 = (f32[512,768]{1,0:T(8,128)S(1)}, f32[512,768]{1,0:T(8,128)}, u32[]{:S(2)}) copy-start(f32[512,768]{1,0:T(8,128)} %get-tuple-element.102.middle_ref.refs_4_) | copy-start | bytes 4718596
  307.7 7.8 %collective-permute-start.10 = (bf16[128,768]{1,0:T(8,128)(2,1)S(1)}, bf16[128,768]{1,0:T(8,128)(2,1)S(1)}, u32[]{:S(2)}, u32[]{:S(2)}) collective-permute-start(bf16[128,768]{1,0:T(8,128)(2,1)S(1)} %fusion.2), channel_id=1, source_target_pairs={{0,2},{1,3},{2,0},{3,1},{4,6},{5,7},{6,4},{7,5},{8,10},{9,11},{10,... | collective-permute-start | bytes 589832 | tf_op jit(solution)/shard_map/ppermute | solution.py:525
  309.3 7.0 %copy-start.56 = (f32[2,128,768]{2,1,0:T(8,128)}, f32[2,128,768]{2,1,0:T(8,128)S(1)}, u32[]{:S(2)}) copy-start(f32[2,128,768]{2,1,0:T(8,128)S(1)} %convert_add_fusion.after_ref) | copy-start | bytes 2359300
  309.3 7.0 %copy-start.14 = (bf16[512,768]{1,0:T(8,128)(2,1)S(1)}, bf16[512,768]{1,0:T(8,128)(2,1)}, u32[]{:S(2)}) copy-start(bf16[512,768]{1,0:T(8,128)(2,1)} %copy-done.13) | copy-start | bytes 2359300
  309.3 7.0 %copy-start.15 = (bf16[512,768]{1,0:T(8,128)(2,1)S(1)}, bf16[512,768]{1,0:T(8,128)(2,1)}, u32[]{:S(2)}) copy-start(bf16[512,768]{1,0:T(8,128)(2,1)} %get-tuple-element.140.m_ref) | copy-start | bytes 2359300
  309.4 11.1 %collective-permute-start.21 = (bf16[128,768]{1,0:T(8,128)(2,1)S(1)}, bf16[128,768]{1,0:T(8,128)(2,1)S(1)}, u32[]{:S(2)}, u32[]{:S(2)}) collective-permute-start(bf16[128,768]{1,0:T(8,128)(2,1)S(1)} %fusion.3), channel_id=1, source_target_pairs={{0,2},{1,3},{2,0},{3,1},{4,6},{5,7},{6,4},{7,5},{8,10},{9,11},{10,... | collective-permute-start | bytes 589832 | tf_op jit(solution)/shard_map/ppermute | solution.py:525
  320.5 24.5 %copy-start.7 = (bf16[4,3,96,768]{3,2,1,0:T(8,128)(2,1)S(1)}, bf16[4,3,96,768]{3,2,1,0:T(8,128)(2,1)}, u32[]{:S(2)}) copy-start(bf16[4,3,96,768]{3,2,1,0:T(8,128)(2,1)} %get-tuple-element.150.refs_1_) | copy-start | bytes 5308420
  353.2 20.9 %copy-start.5 = (bf16[4,96,768]{2,1,0:T(8,128)(2,1)S(1)}, bf16[4,96,768]{2,1,0:T(8,128)(2,1)}, u32[]{:S(2)}) copy-start(bf16[4,96,768]{2,1,0:T(8,128)(2,1)} %copy-done.4) | copy-start | bytes 1769476
  353.2 85.1 %all-gather.16.cloned.1.call-start = ((), (), s32[]{:S(2)}) async-start(), calls=%async_computation.8 | async-start | bytes 1474560 | tf_op jit(solution)/shard_map/all_gather | solution.py:940
  353.3 20.8 %collective-permute-start.27 = (bf16[2,3,96,768]{3,2,1,0:T(8,128)(2,1)}, bf16[2,3,96,768]{3,2,1,0:T(8,128)(2,1)S(1)}, u32[]{:S(2)}, u32[]{:S(2)}) collective-permute-start(bf16[2,3,96,768]{3,2,1,0:T(8,128)(2,1)} %copy-done.52), channel_id=1, source_target_pairs={{0,8},{4,12},{8,0},{12,4},{16,24},{20,28},{24,16},{28,20},{1,9},{5... | collective-permute-start | bytes 2654216 | tf_op jit(solution)/shard_map/ppermute | solution.py:525
  353.4 30.2 %collective-permute-start.23 = (bf16[4,96,768]{2,1,0:T(8,128)(2,1)}, bf16[4,96,768]{2,1,0:T(8,128)(2,1)}, u32[]{:S(2)}, u32[]{:S(2)}) collective-permute-start(bf16[4,96,768]{2,1,0:T(8,128)(2,1)} %copy-done.35), channel_id=1, source_target_pairs={{0,4},{4,0},{8,12},{12,8},{16,20},{20,16},{24,28},{28,24},{1,5},{5... | collective-permute-start | bytes 1769480 | tf_op jit(solution)/shard_map/ppermute | solution.py:525
  354.0 27.7 %collective-permute-start.26 = (bf16[2,2,96,768]{3,2,1,0:T(8,128)(2,1)}, bf16[2,2,96,768]{3,2,1,0:T(8,128)(2,1)}, u32[]{:S(2)}, u32[]{:S(2)}) collective-permute-start(bf16[2,2,96,768]{3,2,1,0:T(8,128)(2,1)} %copy-done.53), channel_id=1, source_target_pairs={{0,4},{4,0},{8,12},{12,8},{16,20},{20,16},{24,28},{28,24},{1,5},{5... | collective-permute-start | bytes 1769480 | tf_op jit(solution)/shard_map/ppermute | solution.py:525
  355.8 27.8 %copy-start.34 = (bf16[4,96,768]{2,1,0:T(8,128)(2,1)S(1)}, bf16[4,96,768]{2,1,0:T(8,128)(2,1)}, u32[]{:S(2)}) copy-start(bf16[4,96,768]{2,1,0:T(8,128)(2,1)} %copy-done.33) | copy-start | bytes 1769476
  355.8 27.7 %collective-permute-start.22 = (bf16[4,96,128]{2,1,0:T(8,128)(2,1)S(1)}, bf16[4,96,128]{2,1,0:T(8,128)(2,1)S(1)}, u32[]{:S(2)}, u32[]{:S(2)}) collective-permute-start(bf16[4,96,128]{2,1,0:T(8,128)(2,1)S(1)} %get-tuple-element.180), channel_id=1, source_target_pairs={{0,4},{4,0},{8,12},{12,8},{16,20},{20,16},{24,28},{28,24},{1,5},{5... | collective-permute-start | bytes 294920 | tf_op jit(solution)/shard_map/ppermute | solution.py:525
  375.0 33.5 %collective-permute-start.33 = (bf16[1,3,96,768]{3,2,1,0:T(8,128)(2,1)}, bf16[1,3,96,768]{3,2,1,0:T(8,128)(2,1)S(1)}, u32[]{:S(2)}, u32[]{:S(2)}) collective-permute-start(bf16[1,3,96,768]{3,2,1,0:T(8,128)(2,1)} %get-tuple-element.164), channel_id=1, source_target_pairs={{0,16},{4,20},{8,24},{12,28},{16,0},{20,4},{24,8},{28,12},{1,17},{... | collective-permute-start | bytes 1327112 | tf_op jit(solution)/shard_map/ppermute | solution.py:525
  384.8 14.7 %collective-permute-start.28 = (bf16[2,96,896]{2,1,0:T(8,128)(2,1)S(1)}, bf16[2,96,896]{2,1,0:T(8,128)(2,1)S(1)}, u32[]{:S(2)}, u32[]{:S(2)}) collective-permute-start(bf16[2,96,896]{2,1,0:T(8,128)(2,1)S(1)} %get-tuple-element.160), channel_id=1, source_target_pairs={{0,8},{4,12},{8,0},{12,4},{16,24},{20,28},{24,16},{28,20},{1,9},{5... | collective-permute-start | bytes 1032200 | tf_op jit(solution)/shard_map/ppermute | solution.py:525
  386.6 21.9 %collective-permute-start.34 = (bf16[1,2,96,768]{3,2,1,0:T(8,128)(2,1)}, bf16[1,2,96,768]{3,2,1,0:T(8,128)(2,1)S(1)}, u32[]{:S(2)}, u32[]{:S(2)}) collective-permute-start(bf16[1,2,96,768]{3,2,1,0:T(8,128)(2,1)} %get-tuple-element.165), channel_id=1, source_target_pairs={{0,16},{4,20},{8,24},{12,28},{16,0},{20,4},{24,8},{28,12},{1,17},{... | collective-permute-start | bytes 884744 | tf_op jit(solution)/shard_map/ppermute | solution.py:525
  409.4 17.6 %collective-permute-start.36 = (bf16[3,96,768]{2,1,0:T(8,128)(2,1)S(1)}, bf16[3,96,768]{2,1,0:T(8,128)(2,1)S(1)}, u32[]{:S(2)}, u32[]{:S(2)}) collective-permute-start(bf16[3,96,768]{2,1,0:T(8,128)(2,1)S(1)} %get-tuple-element.166.refs_0_), channel_id=1, source_target_pairs={{0,2},{1,3},{2,0},{3,1},{4,6},{5,7},{6,4},{7,5},{8,10},{9,11},{10,... | collective-permute-start | bytes 1327112 | tf_op jit(solution)/shard_map/ppermute | solution.py:525
  411.1 16.0 %collective-permute-start.29 = (bf16[1,96,896]{2,1,0:T(8,128)(2,1)S(1)}, bf16[1,96,896]{2,1,0:T(8,128)(2,1)S(1)}, u32[]{:S(2)}, u32[]{:S(2)}) collective-permute-start(bf16[1,96,896]{2,1,0:T(8,128)(2,1)S(1)} %get-tuple-element.163), channel_id=1, source_target_pairs={{0,16},{4,20},{8,24},{12,28},{16,0},{20,4},{24,8},{28,12},{1,17},{... | collective-permute-start | bytes 516104 | tf_op jit(solution)/shard_map/ppermute | solution.py:525
  411.1 23.6 %collective-permute-start.35 = (bf16[3,96,768]{2,1,0:T(8,128)(2,1)S(1)}, bf16[3,96,768]{2,1,0:T(8,128)(2,1)S(1)}, u32[]{:S(2)}, u32[]{:S(2)}) collective-permute-start(bf16[3,96,768]{2,1,0:T(8,128)(2,1)S(1)} %get-tuple-element.166.refs_0_), channel_id=1, source_target_pairs={{0,1},{1,0},{2,3},{3,2},{4,5},{5,4},{6,7},{7,6},{8,9},{9,8},{10,11... | collective-permute-start | bytes 1327112 | tf_op jit(solution)/shard_map/ppermute | solution.py:525
  427.0 7.6 %collective-permute-start.37 = (bf16[3,96,768]{2,1,0:T(8,128)(2,1)S(1)}, bf16[3,96,768]{2,1,0:T(8,128)(2,1)S(1)}, u32[]{:S(2)}, u32[]{:S(2)}) collective-permute-start(bf16[3,96,768]{2,1,0:T(8,128)(2,1)S(1)} %collective-permute-done.36.refs_2_), channel_id=1, source_target_pairs={{0,1},{1,0},{2,3},{3,2},{4,5},{5,4},{6,7},{7,6},{8,9},{9,8},{10,11... | collective-permute-start | bytes 1327112 | tf_op jit(solution)/shard_map/ppermute | solution.py:525
  427.1 7.6 %collective-permute-start.31 = (bf16[96,896]{1,0:T(8,128)(2,1)S(1)}, bf16[96,896]{1,0:T(8,128)(2,1)S(1)}, u32[]{:S(2)}, u32[]{:S(2)}) collective-permute-start(bf16[96,896]{1,0:T(8,128)(2,1)S(1)} %add_last.1.refs_0_), channel_id=1, source_target_pairs={{0,2},{1,3},{2,0},{3,1},{4,6},{5,7},{6,4},{7,5},{8,10},{9,11},{10,... | collective-permute-start | bytes 516104 | tf_op jit(solution)/shard_map/ppermute | solution.py:525
  429.6 7.5 %collective-permute-start.30 = (bf16[96,896]{1,0:T(8,128)(2,1)S(1)}, bf16[96,896]{1,0:T(8,128)(2,1)S(1)}, u32[]{:S(2)}, u32[]{:S(2)}) collective-permute-start(bf16[96,896]{1,0:T(8,128)(2,1)S(1)} %add_last.1.refs_0_), channel_id=1, source_target_pairs={{0,1},{1,0},{2,3},{3,2},{4,5},{5,4},{6,7},{7,6},{8,9},{9,8},{10,11... | collective-permute-start | bytes 516104 | tf_op jit(solution)/shard_map/ppermute | solution.py:525
  434.6 2.5 collective-permute-start.32
  (43 other events, 82.5 us)
Sparse Core Ops, SparseCore 0:
  13.2 113.8 all-gather.7
  129.8 78.0 all-gather.9
  210.1 17.7 all-gather.11
  243.5 104.1 reduce-scatter.1
  353.3 22.4 all-gather.13
  409.5 19.7 all-gather.15

commit v3 on v2

--- a/solution.py
+++ b/solution.py
@@ -552,8 +552,10 @@
     return lax.all_to_all(copies, axis, 0, 0, tiled=True)
 
 
-def head_pieces(shard):
+def head_pieces(shard, after=None):
     across = swap(shard, "head", 2)
+    if after is not None:
+        across = tie(across, after)
     return [shard, swap(shard, "head", 1), across, swap(across, "head", 1)]
 
 
@@ -938,8 +940,8 @@
         last = add_split(dp_index, last, 2, (grad_up,))
         up0, down0 = add_each([up_list[0], down_list[0]], (last[0][0],))
         down0 = lax.all_gather(down0, "head", axis=0)
-        up0 = head_pieces(up0)
         last = head_pieces(add_last(last))
+        up0 = head_pieces(up0, last[2])
         grad_up, grad_qkv, grad_out = unpack(
             unpack_up_kernel, up0, (grad_up,),
             (dims[2], dims[0], dims[1]), [slot(dims[2], 0), slot(dims[0], 1), slot(dims[1], 1)],

time: 453 us -> 451 us (level)
  transfers between devices with their start and end apart: 45 -> 45, of which waited for: 28 -> 29; matrix products, arithmetic and copies ran while one was open for 3% -> 3% of each run, Pallas kernels for 23% -> 23%
where the time goes in v3:
time: 451 us; the launch traced here: 447 us
  waiting for transfers between devices  237 us (53%)
  Pallas kernels  109 us (24%)
  local copies, waits for them, and re-layouts  25.9 us (6%)
  blocking collectives  25.5 us (6%)
  starting transfers between devices  22.4 us (5%)
  between operations  15.1 us (3%)
  other arithmetic  12.4 us (3%)
    ppermute x38, waiting for transfers between devices, swap(): return lax.ppermute(array, axis, [(i, i ^ bits) for i in range(count)])  149 us
    all_gather x2, waiting for transfers between devices, body(): lax.all_gather(pack, 'dp', axis=0, tiled=True)  84.7 us
    all_to_all x1, blocking collectives, spread(): return lax.all_to_all(copies, axis, 0, 0, tiled=True)  25.5 us
    unnamed x127, local copies, waits for them, and re-layouts  23.1 us
    pallas_call x2, Pallas kernels, body(): call(lambda *refs, layer=layer: attend_back_kernel(layer, *refs), fresh_t...  18.1 us
    pallas_call x2, Pallas kernels, body(): call(feed_kernel, (shape(*flat, dtype=F32), shape(*flat), shape(row_len,...  17.8 us
    ppermute x38, starting transfers between devices, swap(): return lax.ppermute(array, axis, [(i, i ^ bits) for i in range(count)])  17.7 us
    pallas_call x2, Pallas kernels, body(): call(lambda *refs, count=len(above): feed_grads_kernel(count, *refs), (sh...  14 us
  transfers between devices with their start and end apart: 45, of which 29 were waited for; matrix products, arithmetic and copies ran while one was open for 3% of the time, Pallas kernels for 23%

profile of v3, /device:TPU:0, one launch (start us, length us, event | category | flops | bytes accessed | tf_op | source)
XLA Modules:
  0.0 446.9 jit_solution(3730083155014888074)
XLA Ops:
  10.1 2.9 pack.2
  13.4 25.5 %all_to_all.10 = bf16[4,128,1664]{2,1,0:T(8,128)(2,1)S(1)} all-to-all(bf16[4,128,1664]{2,1,0:T(8,128)(2,1)S(1)} %broadcast_in_dim.2), channel_id=1, replica_groups=mesh['dp'=8,'head'=4] {'head'}, dimensions={0} | all-to-all | bytes 3407872 | tf_op jit(solution)/shard_map/all_to_all | solution.py:552
  39.1 3.3 pack.3
  42.4 84.7 %all-gather.8.cloned.1.call-done.small_ref.w_ref.wu0_ref.wu1_ref.wd0_ref.wd1_ref.refs_6_.refs_9_ = bf16[768,4736]{1,0:T(8,128)(2,1)} async-done(((bf16[96,4736]{1,0:T(8,128)(2,1)}), bf16[768,4736]{1,0:T(8,128)(2,1)}) %all-gather.8.cloned.1.call-update) | async-done | bytes 7274512 | tf_op jit(solution)/shard_map/all_gather | solution.py:689
  127.1 1.6 fusion.4
  129.7 3.5 all-to-all-start.1
  133.6 4.4 attend_first.1
  139.8 2.9 all-to-all-done.1.wo_ref.refs_7_.refs_10_
  143.5 1.7 collective-permute-done
  145.7 10.8 %collective-permute-done.1 = bf16[2,128,768]{2,1,0:T(8,128)(2,1)S(1)} collective-permute-done((bf16[2,128,768]{2,1,0:T(8,128)(2,1)S(1)}, bf16[2,128,768]{2,1,0:T(8,128)(2,1)S(1)}, u32[]{:S(2)}, u32[]{:S(2)}) %collective-permute-start.1) | collective-permute-done | bytes 393248 | tf_op jit(solution)/shard_map/ppermute | solution.py:525
  160.2 8.7 %feed.2 = (f32[512,768]{1,0:T(8,128)}, bf16[512,768]{1,0:T(8,128)(2,1)S(1)}, bf16[512,768]{1,0:T(8,128)(2,1)S(1)}, bf16[512,768]{1,0:T(8,128)(2,1)S(1)}, f32[2,1...) custom-call(s32[1]{0:T(128)} %bitcast.head_ref.refs_0_, bf16[512,768]{1,0:T(8,128)(2,1)} %copy-done.1, ...), custom_call_target="tpu_custom_call" | custom-call | tf_op jit(solution)/shard_map/feed/pallas_call | solution.py:759
  169.0 1.6 collective-permute-done.3
  170.6 1.2 add_convert_fusion.9
  172.3 10.8 %collective-permute-done.4 = bf16[2,128,768]{2,1,0:T(8,128)(2,1)S(1)} collective-permute-done((bf16[2,128,768]{2,1,0:T(8,128)(2,1)S(1)}, bf16[2,128,768]{2,1,0:T(8,128)(2,1)S(1)}, u32[]{:S(2)}, u32[]{:S(2)}) %collective-permute-start.4) | collective-permute-done | bytes 393248 | tf_op jit(solution)/shard_map/ppermute | solution.py:525
  183.2 1.7 collective-permute-done.5.refs_3_
  185.0 6.6 %attend.1 = (f32[512,768]{1,0:T(8,128)}, bf16[512,768]{1,0:T(8,128)(2,1)S(1)}, bf16[512,640]{1,0:T(8,128)(2,1)S(1)}, bf16[192,512]{1,0:T(8,128)(2,1)S(1)}, f32[8...) custom-call(s32[1]{0:T(128)} %bitcast.head_ref.refs_0_, ...), custom_call_target="tpu_custom_call" | custom-call | tf_op jit(solution)/shard_map/attend/pallas_call | solution.py:745
  195.5 1.3 add_convert_fusion.7
  197.2 10.9 %collective-permute-done.7 = bf16[2,128,768]{2,1,0:T(8,128)(2,1)S(1)} collective-permute-done((bf16[2,128,768]{2,1,0:T(8,128)(2,1)S(1)}, bf16[2,128,768]{2,1,0:T(8,128)(2,1)S(1)}, u32[]{:S(2)}, u32[]{:S(2)}) %collective-permute-start.7) | collective-permute-done | bytes 393248 | tf_op jit(solution)/shard_map/ppermute | solution.py:525
  208.3 1.8 collective-permute-done.8.other_ref
  210.1 9.2 %feed.3 = (f32[512,768]{1,0:T(8,128)}, bf16[512,768]{1,0:T(8,128)(2,1)S(1)}, bf16[512,768]{1,0:T(8,128)(2,1)S(1)}, bf16[512,768]{1,0:T(8,128)(2,1)S(1)}, f32[2,1...) custom-call(s32[1]{0:T(128)} %bitcast.head_ref.refs_0_, f32[512,768]{1,0:T(8,128)} %get-tuple-element.99.base_ref, ...), custom_call_target="tpu_custom_call" | custom-call | tf_op jit(solution)/shard_map/feed/pallas_call | solution.py:759
  222.4 5.9 %feed_back_first.1 = (bf16[512,768]{1,0:T(8,128)(2,1)S(1)}, f32[2,128,768]{2,1,0:T(8,128)S(1)}, bf16[2,128,768]{2,1,0:T(8,128)(2,1)S(1)}) custom-call(s32[1]{0:T(128)} %bitcast.head_ref.refs_0_, bf16[512,768]{1,0:T(8,128)(2,1)S(1)} %get-tuple-element.178.refs_1_.g_ref, bf16[512,768]{1,0:T(8,128)(2,1)S(1)} %get-tuple-element.105.slope_ref, ...), custom_call_target="tpu_custom_call" | custom-call | tf_op jit(solution)/shard_map/feed_back_first/pallas_call | solution.py:798
  228.5 1.6 collective-permute-done.11
  234.0 6.1 %feed_grads.2 = (f32[1,1]{1,0:T(1,128)}, bf16[4,768,768]{2,1,0:T(8,128)(2,1)}) custom-call(s32[1]{0:T(128)} %bitcast.12.refs_0_.dp_ref, bf16[512,768]{1,0:T(8,128)(2,1)S(1)} %get-tuple-element.178.refs_1_.g_ref, bf16[512,768]{1,0:T(8,128)(2,1)S(1)} %copy-done.22, bf16[512,768]{1,0:T(8,128)(2,1)S(1)} %copy-done.24, bf16[512,768]{1,0:T(8,128)(2,1)S(1)} %copy-done.27, ...), custom_call_target="tpu_custom_call" | custom-call | tf_op jit(solution)/shard_map/feed_grads/pallas_call | solution.py:825
  240.0 1.5 collective-permute-done.12
  241.5 1.8 add_convert_fusion.4.refs_2_.after_ref
  243.9 1.7 collective-permute-done.13.refs_3_
  245.7 8.8 %attend_back.2 = (f32[512,768]{1,0:T(8,128)}, f32[8,768]{1,0:T(8,128)S(1)}, bf16[512,768]{1,0:T(8,128)(2,1)}, bf16[512,640]{1,0:T(8,128)(2,1)S(1)}, f32[2,128,76...) custom-call(s32[1]{0:T(128)} %bitcast.head_ref.refs_0_, bf16[512,768]{1,0:T(8,128)(2,1)} %copy-done, ...), custom_call_target="tpu_custom_call" | custom-call | tf_op jit(solution)/shard_map/attend_back/pallas_call | solution.py:847
  254.6 1.6 collective-permute-done.14
  257.8 2.9 attend_grads.2
  260.7 7.9 %collective-permute-done.15 = bf16[2,128,768]{2,1,0:T(8,128)(2,1)S(1)} collective-permute-done((bf16[2,128,768]{2,1,0:T(8,128)(2,1)S(1)}, bf16[2,128,768]{2,1,0:T(8,128)(2,1)S(1)}, u32[]{:S(2)}, u32[]{:S(2)}) %collective-permute-start.15) | collective-permute-done | bytes 393248 | tf_op jit(solution)/shard_map/ppermute | solution.py:525
  269.5 1.7 collective-permute-done.16.other_ref
  271.2 10.1 %feed_back.1 = (f32[512,768]{1,0:T(8,128)}, f32[8,768]{1,0:T(8,128)S(1)}, bf16[512,768]{1,0:T(8,128)(2,1)S(1)}, bf16[512,768]{1,0:T(8,128)(2,1)S(1)}, f32[2,128,...) custom-call(s32[1]{0:T(128)} %bitcast.head_ref.refs_0_, f32[512,768]{1,0:T(8,128)} %get-tuple-element.115.grad_ref, ...), custom_call_target="tpu_custom_call" | custom-call | tf_op jit(solution)/shard_map/feed_back/pallas_call | solution.py:807
  281.5 1.6 collective-permute-done.17
  283.7 7.9 %feed_grads.3 = (f32[1,1]{1,0:T(1,128)}, bf16[4,3,96,768]{3,2,1,0:T(8,128)(2,1)}, bf16[4,3,96,768]{3,2,1,0:T(8,128)(2,1)}, bf16[4,2,96,768]{3,2,1,0:T(8,128)(2,1)}, bf16[4,2,96,768]{3,2,1,0:T(8,128)(2,1)}) custom-call(s32[1]{0:T(128)} %bitcast.12.refs_0_.dp_ref, bf16[512,768]{1,0:T(8,128)(2,1)S(1)} %get-tuple-element.126.refs_1_, ...), custom_call_target="tpu_custom_call" | custom-call | tf_op jit(solution)/shard_map/feed_grads/pallas_call | solution.py:825
  292.2 2.1 collective-permute-done.18
  295.7 1.2 collective-permute-done.19.refs_3_
  296.9 9.2 %attend_back.3 = (f32[512,768]{1,0:T(8,128)}, f32[8,768]{1,0:T(8,128)S(1)}, bf16[512,768]{1,0:T(8,128)(2,1)}, bf16[512,640]{1,0:T(8,128)(2,1)S(1)}, f32[2,128,76...) custom-call(s32[1]{0:T(128)} %bitcast.head_ref.refs_0_, f32[512,768]{1,0:T(8,128)} %get-tuple-element.123.refs_1_, ...), custom_call_target="tpu_custom_call" | custom-call | tf_op jit(solution)/shard_map/attend_back/pallas_call | solution.py:847
  309.4 1.7 collective-permute-start.21
  311.0 4.5 collective-permute-done.10.recv_ref
  316.3 3.3 attend_grads.3
  320.5 1.2 last_norm.1
  321.7 23.3 %collective-permute-done.25.refs_2_ = bf16[4,3,96,768]{3,2,1,0:T(8,128)(2,1)} collective-permute-done((bf16[4,3,96,768]{3,2,1,0:T(8,128)(2,1)}, bf16[4,3,96,768]{3,2,1,0:T(8,128)(2,1)}, u32[]{:S(2)}, u32[]{:S(2)}) %collective-permute-start.25) | collective-permute-done | bytes 1769504 | tf_op jit(solution)/shard_map/ppermute | solution.py:525
  346.0 2.0 add_split.6
  348.9 1.5 add_split.7
  354.0 1.5 collective-permute-start.26
  356.4 17.7 %collective-permute-done.27.refs_2_ = bf16[2,3,96,768]{3,2,1,0:T(8,128)(2,1)S(1)} collective-permute-done((bf16[2,3,96,768]{3,2,1,0:T(8,128)(2,1)}, bf16[2,3,96,768]{3,2,1,0:T(8,128)(2,1)S(1)}, u32[]{:S(2)}, u32[]{:S(2)}) %collective-permute-start.27) | collective-permute-done | bytes 884768 | tf_op jit(solution)/shard_map/ppermute | solution.py:525
  375.0 1.5 collective-permute-start.33
  376.5 5.1 %collective-permute-done.26.refs_2_ = bf16[2,2,96,768]{3,2,1,0:T(8,128)(2,1)} collective-permute-done((bf16[2,2,96,768]{3,2,1,0:T(8,128)(2,1)}, bf16[2,2,96,768]{3,2,1,0:T(8,128)(2,1)}, u32[]{:S(2)}, u32[]{:S(2)}) %collective-permute-start.26) | collective-permute-done | bytes 589856 | tf_op jit(solution)/shard_map/ppermute | solution.py:525
  381.7 1.9 add_split.9
  383.5 1.2 add_split.10
  384.8 1.8 collective-permute-start.28
  386.6 1.5 collective-permute-start.34
  388.1 1.7 copy-done.6
  389.8 2.8 unpack_later.1
  392.6 6.9 %collective-permute-done.28.refs_2_ = bf16[2,96,896]{2,1,0:T(8,128)(2,1)S(1)} collective-permute-done((bf16[2,96,896]{2,1,0:T(8,128)(2,1)S(1)}, bf16[2,96,896]{2,1,0:T(8,128)(2,1)S(1)}, u32[]{:S(2)}, u32[]{:S(2)}) %collective-permute-start.28) | collective-permute-done | bytes 344096 | tf_op jit(solution)/shard_map/ppermute | solution.py:525
  399.5 9.0 %collective-permute-done.34.refs_3_ = bf16[1,2,96,768]{3,2,1,0:T(8,128)(2,1)S(1)} collective-permute-done((bf16[1,2,96,768]{3,2,1,0:T(8,128)(2,1)}, bf16[1,2,96,768]{3,2,1,0:T(8,128)(2,1)S(1)}, u32[]{:S(2)}, u32[]{:S(2)}) %collective-permute-start.34) | collective-permute-done | bytes 294944 | tf_op jit(solution)/shard_map/ppermute | solution.py:525
  409.4 1.7 collective-permute-start.36
  411.1 8.4 %collective-permute-done.29.refs_1_ = bf16[1,96,896]{2,1,0:T(8,128)(2,1)S(1)} collective-permute-done((bf16[1,96,896]{2,1,0:T(8,128)(2,1)S(1)}, bf16[1,96,896]{2,1,0:T(8,128)(2,1)S(1)}, u32[]{:S(2)}, u32[]{:S(2)}) %collective-permute-start.29) | collective-permute-done | bytes 172064 | tf_op jit(solution)/shard_map/ppermute | solution.py:525
  420.0 11.5 %collective-permute-done.31.after_ref.refs_2_ = bf16[96,896]{1,0:T(8,128)(2,1)S(1)} collective-permute-done((bf16[96,896]{1,0:T(8,128)(2,1)S(1)}, bf16[96,896]{1,0:T(8,128)(2,1)S(1)}, u32[]{:S(2)}, u32[]{:S(2)}) %collective-permute-start.31) | collective-permute-done | bytes 172064 | tf_op jit(solution)/shard_map/ppermute | solution.py:525
  432.1 1.2 collective-permute-done.37.refs_3_
  433.3 2.5 unpack_up.1
  435.8 1.2 unpack_attn.1
  437.0 1.3 copy-done.11
  438.3 1.6 unpack_down.1
  (230 shorter events, 43.9 us)
Async XLA Ops:
  7.2 119.9 %all-gather.8.cloned.1.call-start = ((), (), s32[]{:S(2)}) async-start(), calls=%async_computation.3 | async-start | bytes 8183808 | tf_op jit(solution)/shard_map/all_gather | solution.py:689
  13.0 195.3 %all-gather.10.cloned.1.call-start = ((), (), s32[]{:S(2)}) async-start(), calls=%async_computation.4 | async-start | bytes 5308416 | tf_op jit(solution)/shard_map/all_gather | solution.py:689
  39.1 94.5 %copy-start.1 = (bf16[512,768]{1,0:T(8,128)(2,1)}, bf16[512,768]{1,0:T(8,128)(2,1)S(1)}, u32[]{:S(2)}) copy-start(bf16[512,768]{1,0:T(8,128)(2,1)S(1)} %get-tuple-element.179.tok_ref.base_ref.refs_0_) | copy-start | bytes 2359300
  39.1 191.5 %copy-start = (bf16[512,768]{1,0:T(8,128)(2,1)}, bf16[512,768]{1,0:T(8,128)(2,1)S(1)}, u32[]{:S(2)}) copy-start(bf16[512,768]{1,0:T(8,128)(2,1)S(1)} %get-tuple-element.178.refs_1_.g_ref) | copy-start | bytes 2359300
  42.4 91.0 %copy-start.44 = (s32[1,512]{1,0:T(1,128)S(1)}, s32[1,512]{1,0:T(1,128)}, u32[]{:S(2)}) copy-start(s32[1,512]{1,0:T(1,128)} %refs_12_.3) | copy-start | bytes 6148
  129.7 13.0 %all-to-all-start.1 = ((bf16[4,192,384]{2,1,0:T(8,128)(2,1)}), bf16[4,192,384]{2,1,0:T(8,128)(2,1)S(1)}, u32[]{:S(2)}, u32[]{:S(2)}) async-start(bf16[4,192,384]{2,1,0:T(8,128)(2,1)} %bitcast.6), calls=%async_computation.1 | async-start | bytes 1179648 | tf_op jit(solution)/shard_map/all_to_all | solution.py:694
  133.2 97.4 %all-gather.12.cloned.1.call-start = ((), (), s32[]{:S(2)}) async-start(), calls=%async_computation.5 | async-start | bytes 1966080 | tf_op jit(solution)/shard_map/all_gather | solution.py:774
  139.8 16.9 %copy-start.46 = (f32[8,512]{1,0:T(8,128)}, f32[8,512]{1,0:T(8,128)S(1)}, u32[]{:S(2)}) copy-start(f32[8,512]{1,0:T(8,128)S(1)} %get-tuple-element.134.refs_8_) | copy-start | bytes 49156
  143.4 1.8 collective-permute-start
  145.3 11.2 %collective-permute-start.1 = (bf16[2,128,768]{2,1,0:T(8,128)(2,1)S(1)}, bf16[2,128,768]{2,1,0:T(8,128)(2,1)S(1)}, u32[]{:S(2)}, u32[]{:S(2)}) collective-permute-start(bf16[2,128,768]{2,1,0:T(8,128)(2,1)S(1)} %add_convert_fusion.11), channel_id=1, source_target_pairs={{0,2},{1,3},{2,0},{3,1},{4,6},{5,7},{6,4},{7,5},{8,10},{9,11},{10,... | collective-permute-start | bytes 1179656 | tf_op jit(solution)/shard_map/ppermute | solution.py:525
  156.6 1.8 collective-permute-start.2
  168.8 16.1 %copy-start.20 = (bf16[512,768]{1,0:T(8,128)(2,1)}, bf16[512,768]{1,0:T(8,128)(2,1)S(1)}, u32[]{:S(2)}) copy-start(bf16[512,768]{1,0:T(8,128)(2,1)S(1)} %get-tuple-element.128.refs_3_) | copy-start | bytes 2359300
  168.8 16.1 %copy-start.28 = (bf16[512,768]{1,0:T(8,128)(2,1)}, bf16[512,768]{1,0:T(8,128)(2,1)S(1)}, u32[]{:S(2)}) copy-start(bf16[512,768]{1,0:T(8,128)(2,1)S(1)} %get-tuple-element.122.slope_ref) | copy-start | bytes 2359300
  168.8 22.8 %copy-start.18 = (bf16[512,768]{1,0:T(8,128)(2,1)}, bf16[512,768]{1,0:T(8,128)(2,1)S(1)}, u32[]{:S(2)}) copy-start(bf16[512,768]{1,0:T(8,128)(2,1)S(1)} %get-tuple-element.127.refs_2_) | copy-start | bytes 2359300
  168.8 1.8 collective-permute-start.3
  171.8 11.2 %collective-permute-start.4 = (bf16[2,128,768]{2,1,0:T(8,128)(2,1)S(1)}, bf16[2,128,768]{2,1,0:T(8,128)(2,1)S(1)}, u32[]{:S(2)}, u32[]{:S(2)}) collective-permute-start(bf16[2,128,768]{2,1,0:T(8,128)(2,1)S(1)} %add_convert_fusion.9), channel_id=1, source_target_pairs={{0,2},{1,3},{2,0},{3,1},{4,6},{5,7},{6,4},{7,5},{8,10},{9,11},{10,... | collective-permute-start | bytes 1179656 | tf_op jit(solution)/shard_map/ppermute | solution.py:525
  183.2 1.8 collective-permute-start.5
  193.7 1.9 collective-permute-start.6
  194.7 156.6 %reduce-scatter.2.cloned.1.call-start = ((), (), s32[]{:S(2)}) async-start(), calls=%async_computation.6 | async-start | bytes 5308416 | tf_op jit(solution)/shard_map/reduce_scatter | solution.py:844
  196.8 11.3 %collective-permute-start.7 = (bf16[2,128,768]{2,1,0:T(8,128)(2,1)S(1)}, bf16[2,128,768]{2,1,0:T(8,128)(2,1)S(1)}, u32[]{:S(2)}, u32[]{:S(2)}) collective-permute-start(bf16[2,128,768]{2,1,0:T(8,128)(2,1)S(1)} %add_convert_fusion.7), channel_id=1, source_target_pairs={{0,2},{1,3},{2,0},{3,1},{4,6},{5,7},{6,4},{7,5},{8,10},{9,11},{10,... | collective-permute-start | bytes 1179656 | tf_op jit(solution)/shard_map/ppermute | solution.py:525
  208.2 1.9 collective-permute-start.8
  228.3 1.8 collective-permute-start.11
  230.2 11.3 %collective-permute-start.12 = (bf16[2,128,768]{2,1,0:T(8,128)(2,1)S(1)}, bf16[2,128,768]{2,1,0:T(8,128)(2,1)}, u32[]{:S(2)}, u32[]{:S(2)}) collective-permute-start(bf16[2,128,768]{2,1,0:T(8,128)(2,1)S(1)} %add_convert_fusion.5.refs_6_), channel_id=1, source_target_pairs={{0,2},{1,3},{2,0},{3,1},{4,6},{5,7},{6,4},{7,5},{8,10},{9,11},{10,... | collective-permute-start | bytes 1179656 | tf_op jit(solution)/shard_map/ppermute | solution.py:525
  243.3 144.8 %all-gather.14.cloned.1.call-start = ((), (), s32[]{:S(2)}) async-start(), calls=%async_computation.7 | async-start | bytes 2949120 | tf_op jit(solution)/shard_map/all_gather | solution.py:935
  243.9 1.8 collective-permute-start.13
  254.5 1.7 collective-permute-start.14
  257.4 11.2 %collective-permute-start.15 = (bf16[2,128,768]{2,1,0:T(8,128)(2,1)S(1)}, bf16[2,128,768]{2,1,0:T(8,128)(2,1)S(1)}, u32[]{:S(2)}, u32[]{:S(2)}) collective-permute-start(bf16[2,128,768]{2,1,0:T(8,128)(2,1)S(1)} %add_convert_fusion.3.after_ref), channel_id=1, source_target_pairs={{0,2},{1,3},{2,0},{3,1},{4,6},{5,7},{6,4},{7,5},{8,10},{9,11},{10,... | collective-permute-start | bytes 1179656 | tf_op jit(solution)/shard_map/ppermute | solution.py:525
  257.8 13.4 %copy-start.41 = (f32[4,768]{1,0:T(4,128)S(1)}, f32[4,768]{1,0:T(4,128)}, u32[]{:S(2)}) copy-start(f32[4,768]{1,0:T(4,128)} %copy-done.40) | copy-start | bytes 36868
  269.4 1.8 collective-permute-start.16
  281.3 1.8 collective-permute-start.17
  283.1 11.2 %collective-permute-start.18 = (bf16[2,128,768]{2,1,0:T(8,128)(2,1)S(1)}, bf16[2,128,768]{2,1,0:T(8,128)(2,1)S(1)}, u32[]{:S(2)}, u32[]{:S(2)}) collective-permute-start(bf16[2,128,768]{2,1,0:T(8,128)(2,1)S(1)} %add_convert_fusion.1.refs_6_), channel_id=1, source_target_pairs={{0,2},{1,3},{2,0},{3,1},{4,6},{5,7},{6,4},{7,5},{8,10},{9,11},{10,... | collective-permute-start | bytes 1179656 | tf_op jit(solution)/shard_map/ppermute | solution.py:525
  283.6 11.6 %copy-start.55 = (bf16[2,128,768]{2,1,0:T(8,128)(2,1)S(1)}, bf16[2,128,768]{2,1,0:T(8,128)(2,1)}, u32[]{:S(2)}) copy-start(bf16[2,128,768]{2,1,0:T(8,128)(2,1)} %copy-done.54) | copy-start | bytes 1179652
  283.7 13.3 %copy-start.30 = (bf16[512,640]{1,0:T(8,128)(2,1)S(1)}, bf16[512,640]{1,0:T(8,128)(2,1)}, u32[]{:S(2)}) copy-start(bf16[512,640]{1,0:T(8,128)(2,1)} %copy-done.29) | copy-start | bytes 1966084
  283.7 13.3 %copy-start.47 = (f32[8,512]{1,0:T(8,128)S(1)}, f32[8,512]{1,0:T(8,128)}, u32[]{:S(2)}) copy-start(f32[8,512]{1,0:T(8,128)} %copy-done.46) | copy-start | bytes 49156
  291.6 53.4 %collective-permute-start.25 = (bf16[4,3,96,768]{3,2,1,0:T(8,128)(2,1)}, bf16[4,3,96,768]{3,2,1,0:T(8,128)(2,1)}, u32[]{:S(2)}, u32[]{:S(2)}) collective-permute-start(bf16[4,3,96,768]{3,2,1,0:T(8,128)(2,1)} %get-tuple-element.151), channel_id=1, source_target_pairs={{0,4},{4,0},{8,12},{12,8},{16,20},{20,16},{24,28},{28,24},{1,5},{5... | collective-permute-start | bytes 5308424 | tf_op jit(solution)/shard_map/ppermute | solution.py:525
  295.1 1.8 collective-permute-start.19
  295.2 11.2 %collective-permute-start.9 = (bf16[2,128,768]{2,1,0:T(8,128)(2,1)S(1)}, bf16[2,128,768]{2,1,0:T(8,128)(2,1)S(1)}, u32[]{:S(2)}, u32[]{:S(2)}) collective-permute-start(bf16[2,128,768]{2,1,0:T(8,128)(2,1)S(1)} %copy-done.55), channel_id=1, source_target_pairs={{0,1},{1,0},{2,3},{3,2},{4,5},{5,4},{6,7},{7,6},{8,9},{9,8},{10,11... | collective-permute-start | bytes 1179656 | tf_op jit(solution)/shard_map/ppermute | solution.py:525
  295.7 52.3 %collective-permute-start.24 = (bf16[4,2,96,768]{3,2,1,0:T(8,128)(2,1)}, bf16[4,2,96,768]{3,2,1,0:T(8,128)(2,1)}, u32[]{:S(2)}, u32[]{:S(2)}) collective-permute-start(bf16[4,2,96,768]{3,2,1,0:T(8,128)(2,1)} %get-tuple-element.149), channel_id=1, source_target_pairs={{0,8},{4,12},{8,0},{12,4},{16,24},{20,28},{24,16},{28,20},{1,9},{5... | collective-permute-start | bytes 3538952 | tf_op jit(solution)/shard_map/ppermute | solution.py:525
  296.9 9.4 %copy-start.61 = (s32[128,1]{0,1:T(1,128)S(1)}, s32[128,1]{0,1:T(1,128)}, u32[]{:S(2)}) copy-start(s32[128,1]{0,1:T(1,128)} %param.12) | copy-start | bytes 1540
  306.2 2.0 collective-permute-start.20
  307.7 7.9 %copy-start.2 = (f32[512,768]{1,0:T(8,128)S(1)}, f32[512,768]{1,0:T(8,128)}, u32[]{:S(2)}) copy-start(f32[512,768]{1,0:T(8,128)} %get-tuple-element.102.middle_ref.refs_4_) | copy-start | bytes 4718596
  307.7 7.8 %collective-permute-start.10 = (bf16[128,768]{1,0:T(8,128)(2,1)S(1)}, bf16[128,768]{1,0:T(8,128)(2,1)S(1)}, u32[]{:S(2)}, u32[]{:S(2)}) collective-permute-start(bf16[128,768]{1,0:T(8,128)(2,1)S(1)} %fusion.2), channel_id=1, source_target_pairs={{0,2},{1,3},{2,0},{3,1},{4,6},{5,7},{6,4},{7,5},{8,10},{9,11},{10,... | collective-permute-start | bytes 589832 | tf_op jit(solution)/shard_map/ppermute | solution.py:525
  309.3 7.0 %copy-start.56 = (f32[2,128,768]{2,1,0:T(8,128)}, f32[2,128,768]{2,1,0:T(8,128)S(1)}, u32[]{:S(2)}) copy-start(f32[2,128,768]{2,1,0:T(8,128)S(1)} %convert_add_fusion.after_ref) | copy-start | bytes 2359300
  309.3 7.0 %copy-start.14 = (bf16[512,768]{1,0:T(8,128)(2,1)S(1)}, bf16[512,768]{1,0:T(8,128)(2,1)}, u32[]{:S(2)}) copy-start(bf16[512,768]{1,0:T(8,128)(2,1)} %copy-done.13) | copy-start | bytes 2359300
  309.3 7.0 %copy-start.15 = (bf16[512,768]{1,0:T(8,128)(2,1)S(1)}, bf16[512,768]{1,0:T(8,128)(2,1)}, u32[]{:S(2)}) copy-start(bf16[512,768]{1,0:T(8,128)(2,1)} %get-tuple-element.140.m_ref) | copy-start | bytes 2359300
  309.4 11.1 %collective-permute-start.21 = (bf16[128,768]{1,0:T(8,128)(2,1)S(1)}, bf16[128,768]{1,0:T(8,128)(2,1)S(1)}, u32[]{:S(2)}, u32[]{:S(2)}) collective-permute-start(bf16[128,768]{1,0:T(8,128)(2,1)S(1)} %fusion.3), channel_id=1, source_target_pairs={{0,2},{1,3},{2,0},{3,1},{4,6},{5,7},{6,4},{7,5},{8,10},{9,11},{10,... | collective-permute-start | bytes 589832 | tf_op jit(solution)/shard_map/ppermute | solution.py:525
  320.5 24.5 %copy-start.7 = (bf16[4,3,96,768]{3,2,1,0:T(8,128)(2,1)S(1)}, bf16[4,3,96,768]{3,2,1,0:T(8,128)(2,1)}, u32[]{:S(2)}) copy-start(bf16[4,3,96,768]{3,2,1,0:T(8,128)(2,1)} %get-tuple-element.150.refs_1_) | copy-start | bytes 5308420
  353.2 20.9 %copy-start.5 = (bf16[4,96,768]{2,1,0:T(8,128)(2,1)S(1)}, bf16[4,96,768]{2,1,0:T(8,128)(2,1)}, u32[]{:S(2)}) copy-start(bf16[4,96,768]{2,1,0:T(8,128)(2,1)} %copy-done.4) | copy-start | bytes 1769476
  353.2 83.8 %all-gather.16.cloned.1.call-start = ((), (), s32[]{:S(2)}) async-start(), calls=%async_computation.8 | async-start | bytes 1474560 | tf_op jit(solution)/shard_map/all_gather | solution.py:942
  353.3 20.8 %collective-permute-start.27 = (bf16[2,3,96,768]{3,2,1,0:T(8,128)(2,1)}, bf16[2,3,96,768]{3,2,1,0:T(8,128)(2,1)S(1)}, u32[]{:S(2)}, u32[]{:S(2)}) collective-permute-start(bf16[2,3,96,768]{3,2,1,0:T(8,128)(2,1)} %copy-done.52), channel_id=1, source_target_pairs={{0,8},{4,12},{8,0},{12,4},{16,24},{20,28},{24,16},{28,20},{1,9},{5... | collective-permute-start | bytes 2654216 | tf_op jit(solution)/shard_map/ppermute | solution.py:525
  353.4 30.2 %collective-permute-start.23 = (bf16[4,96,768]{2,1,0:T(8,128)(2,1)}, bf16[4,96,768]{2,1,0:T(8,128)(2,1)}, u32[]{:S(2)}, u32[]{:S(2)}) collective-permute-start(bf16[4,96,768]{2,1,0:T(8,128)(2,1)} %copy-done.35), channel_id=1, source_target_pairs={{0,4},{4,0},{8,12},{12,8},{16,20},{20,16},{24,28},{28,24},{1,5},{5... | collective-permute-start | bytes 1769480 | tf_op jit(solution)/shard_map/ppermute | solution.py:525
  354.0 27.7 %collective-permute-start.26 = (bf16[2,2,96,768]{3,2,1,0:T(8,128)(2,1)}, bf16[2,2,96,768]{3,2,1,0:T(8,128)(2,1)}, u32[]{:S(2)}, u32[]{:S(2)}) collective-permute-start(bf16[2,2,96,768]{3,2,1,0:T(8,128)(2,1)} %copy-done.53), channel_id=1, source_target_pairs={{0,4},{4,0},{8,12},{12,8},{16,20},{20,16},{24,28},{28,24},{1,5},{5... | collective-permute-start | bytes 1769480 | tf_op jit(solution)/shard_map/ppermute | solution.py:525
  355.8 27.8 %copy-start.34 = (bf16[4,96,768]{2,1,0:T(8,128)(2,1)S(1)}, bf16[4,96,768]{2,1,0:T(8,128)(2,1)}, u32[]{:S(2)}) copy-start(bf16[4,96,768]{2,1,0:T(8,128)(2,1)} %copy-done.33) | copy-start | bytes 1769476
  355.8 27.7 %collective-permute-start.22 = (bf16[4,96,128]{2,1,0:T(8,128)(2,1)S(1)}, bf16[4,96,128]{2,1,0:T(8,128)(2,1)S(1)}, u32[]{:S(2)}, u32[]{:S(2)}) collective-permute-start(bf16[4,96,128]{2,1,0:T(8,128)(2,1)S(1)} %get-tuple-element.180), channel_id=1, source_target_pairs={{0,4},{4,0},{8,12},{12,8},{16,20},{20,16},{24,28},{28,24},{1,5},{5... | collective-permute-start | bytes 294920 | tf_op jit(solution)/shard_map/ppermute | solution.py:525
  375.0 33.5 %collective-permute-start.33 = (bf16[1,3,96,768]{3,2,1,0:T(8,128)(2,1)}, bf16[1,3,96,768]{3,2,1,0:T(8,128)(2,1)S(1)}, u32[]{:S(2)}, u32[]{:S(2)}) collective-permute-start(bf16[1,3,96,768]{3,2,1,0:T(8,128)(2,1)} %get-tuple-element.164), channel_id=1, source_target_pairs={{0,16},{4,20},{8,24},{12,28},{16,0},{20,4},{24,8},{28,12},{1,17},{... | collective-permute-start | bytes 1327112 | tf_op jit(solution)/shard_map/ppermute | solution.py:525
  384.8 14.7 %collective-permute-start.28 = (bf16[2,96,896]{2,1,0:T(8,128)(2,1)S(1)}, bf16[2,96,896]{2,1,0:T(8,128)(2,1)S(1)}, u32[]{:S(2)}, u32[]{:S(2)}) collective-permute-start(bf16[2,96,896]{2,1,0:T(8,128)(2,1)S(1)} %get-tuple-element.160), channel_id=1, source_target_pairs={{0,8},{4,12},{8,0},{12,4},{16,24},{20,28},{24,16},{28,20},{1,9},{5... | collective-permute-start | bytes 1032200 | tf_op jit(solution)/shard_map/ppermute | solution.py:525
  386.6 21.9 %collective-permute-start.34 = (bf16[1,2,96,768]{3,2,1,0:T(8,128)(2,1)}, bf16[1,2,96,768]{3,2,1,0:T(8,128)(2,1)S(1)}, u32[]{:S(2)}, u32[]{:S(2)}) collective-permute-start(bf16[1,2,96,768]{3,2,1,0:T(8,128)(2,1)} %get-tuple-element.165), channel_id=1, source_target_pairs={{0,16},{4,20},{8,24},{12,28},{16,0},{20,4},{24,8},{28,12},{1,17},{... | collective-permute-start | bytes 884744 | tf_op jit(solution)/shard_map/ppermute | solution.py:525
  409.4 22.2 %collective-permute-start.36 = (bf16[3,96,768]{2,1,0:T(8,128)(2,1)S(1)}, bf16[3,96,768]{2,1,0:T(8,128)(2,1)S(1)}, u32[]{:S(2)}, u32[]{:S(2)}) collective-permute-start(bf16[3,96,768]{2,1,0:T(8,128)(2,1)S(1)} %get-tuple-element.166.refs_0_), channel_id=1, source_target_pairs={{0,2},{1,3},{2,0},{3,1},{4,6},{5,7},{6,4},{7,5},{8,10},{9,11},{10,... | collective-permute-start | bytes 1327112 | tf_op jit(solution)/shard_map/ppermute | solution.py:525
  411.1 8.4 %collective-permute-start.29 = (bf16[1,96,896]{2,1,0:T(8,128)(2,1)S(1)}, bf16[1,96,896]{2,1,0:T(8,128)(2,1)S(1)}, u32[]{:S(2)}, u32[]{:S(2)}) collective-permute-start(bf16[1,96,896]{2,1,0:T(8,128)(2,1)S(1)} %get-tuple-element.163), channel_id=1, source_target_pairs={{0,16},{4,20},{8,24},{12,28},{16,0},{20,4},{24,8},{28,12},{1,17},{... | collective-permute-start | bytes 516104 | tf_op jit(solution)/shard_map/ppermute | solution.py:525
  419.5 12.0 %collective-permute-start.31 = (bf16[96,896]{1,0:T(8,128)(2,1)S(1)}, bf16[96,896]{1,0:T(8,128)(2,1)S(1)}, u32[]{:S(2)}, u32[]{:S(2)}) collective-permute-start(bf16[96,896]{1,0:T(8,128)(2,1)S(1)} %add_last.1.refs_0_), channel_id=1, source_target_pairs={{0,2},{1,3},{2,0},{3,1},{4,6},{5,7},{6,4},{7,5},{8,10},{9,11},{10,... | collective-permute-start | bytes 516104 | tf_op jit(solution)/shard_map/ppermute | solution.py:525
  420.0 12.1 %collective-permute-start.35 = (bf16[3,96,768]{2,1,0:T(8,128)(2,1)S(1)}, bf16[3,96,768]{2,1,0:T(8,128)(2,1)S(1)}, u32[]{:S(2)}, u32[]{:S(2)}) collective-permute-start(bf16[3,96,768]{2,1,0:T(8,128)(2,1)S(1)} %get-tuple-element.166.refs_0_), channel_id=1, source_target_pairs={{0,1},{1,0},{2,3},{3,2},{4,5},{5,4},{6,7},{7,6},{8,9},{9,8},{10,11... | collective-permute-start | bytes 1327112 | tf_op jit(solution)/shard_map/ppermute | solution.py:525
  431.5 1.8 collective-permute-start.37
  431.5 4.3 collective-permute-start.30
  432.0 3.8 collective-permute-start.32
  (43 other events, 82.5 us)
Sparse Core Ops, SparseCore 0:
  13.2 113.8 all-gather.7
  129.8 78.0 all-gather.9
  210.1 17.7 all-gather.11
  243.5 104.1 reduce-scatter.1
  353.3 22.4 all-gather.13
  409.5 22.0 all-gather.15
